TPU v7x, 256 devices: a whole 4x4x8 slice. The times are simulated.
256 devices in a mesh: vec: 16 (over x, z_lo, core), pair: 16 (over z_hi, y).
Axes of the slice: x: 4, y: 4, z: 8 (z_hi: 4, z_lo: 2; z = z_hi * 2 + z_lo), core: 2. Of those that a mesh axis runs over, the one named last changes fastest.
Arguments:
- cholesky: bfloat16 [256, 1600, 1600], P('vec', 'pair'), may hold values from -0.0390625 to 0.0390625
- walkers: bfloat16 [16, 1600, 200], P('vec', 'pair'), may hold values from -1.1953125 to 1.1953125
- inv_correlation: float32 [16, 200, 200], P('vec'), may hold values from -1.25 to 1.25
- trial_orbitals: bfloat16 [1600, 200], replicated, may hold values from -0.15625 to 0.15625
- aux_fields: float32 [16, 256], P(None, 'vec'), may hold values from -4 to 4
Outputs:
- new_walkers: bfloat16 [16, 1600, 200], P('vec', 'pair')
- fields: float32 [16, 256], P(None, 'vec')
All inputs are finite; a program needn't handle non-finite values.
Results may differ from a plain program's by a relative error of at most 0.035.
Values may be sent and summed in bfloat16 or wider, within the bound.
No kernel may reach another device: no remote copies, remote signals or barrier semaphores. Data moves between devices by JAX's collectives and lax.ppermute only.
A program may use at most 64 MiB of HBM per device.

v0:
```python
import jax
import jax.numpy as jnp
from jax import lax
from jax.experimental import pallas as pl
from jax.experimental.pallas import tpu as pltpu
from jax.sharding import PartitionSpec as P

TAYLOR = 6
NX, NL, NC = 4, 2, 2
NH, NY = 4, 4
PITCH = 56
GROUP = 16

root_step = 0.5
shift_cap = 1.0

VMEM = pl.BlockSpec(memory_space=pltpu.VMEM)
FAR = pl.BlockSpec(memory_space=pl.ANY)
NT = (((1,), (1,)), ((), ()))


def vec_of(x, low, core):
    return ((x % NX) * NL + low) * NC + core


def places():
    return [(x, low, core) for x in range(NX) for low in range(NL) for core in range(NC)]


def send_x(array, step):
    return lax.ppermute(array, "vec", [(vec_of(*p), vec_of(p[0] + step, p[1], p[2])) for p in places()])


def swap_low(array):
    return lax.ppermute(array, "vec", [(vec_of(*p), vec_of(p[0], 1 - p[1], p[2])) for p in places()])


def swap_core(array):
    return lax.ppermute(array, "vec", [(vec_of(*p), vec_of(p[0], p[1], 1 - p[2])) for p in places()])


def send_y(array, step):
    return lax.ppermute(array, "pair", [(h * NY + y, h * NY + (y + step) % NY) for h in range(NH) for y in range(NY)])


def flip_y(array, bit):
    return lax.ppermute(array, "pair", [(h * NY + y, h * NY + (y ^ bit)) for h in range(NH) for y in range(NY)])


def send_h(array, step):
    return lax.ppermute(array, "pair", [(h * NY + y, ((h + step) % NH) * NY + y) for h in range(NH) for y in range(NY)])


def everywhere(array, target):
    pairs = []
    for x, low, core in places():
        for high in range(NH):
            for y in range(NY):
                to = target(x, low, core, high, y)
                if to is not None:
                    pairs.append(
                        (vec_of(x, low, core) * NH * NY + high * NY + y, vec_of(*to[:3]) * NH * NY + to[3] * NY + to[4])
                    )
    return lax.ppermute(array, ("vec", "pair"), pairs)


def exchange(array):
    return everywhere(array, lambda x, low, core, high, y: (x, high // NC, high % NC, low * NC + core, y))


def first_target(x, low, core, high, y):
    turn = (high - core) % NH
    return (x, low, core if turn % 2 == 0 else 1 - core, core + 2 if turn in (0, 3) else core, y)


def second_target(x, low, core, high, y):
    turn = (high - core) % NH
    return None if turn % 2 == 0 else (x, low, 1 - core, core + 2 if turn == 1 else core, y)


def position():
    me, pair = lax.axis_index("vec"), lax.axis_index("pair")
    return (me // NC) % NL, me // (NL * NC), me % NC, pair // NY, pair % NY


def diagonal_mask(rows, columns):
    row = lax.broadcasted_iota(jnp.int32, (rows, columns), 0)
    column = lax.broadcasted_iota(jnp.int32, (rows, columns), 1)
    return (row % GROUP) == (column // GROUP)


def groups_of(rows):
    return [(start, min(GROUP, rows - start)) for start in range(0, rows, GROUP)]


def rotate_kernel(walkers, inverse, out_ref, walkers_out):
    rows = walkers.shape[1]
    mine = walkers[...].astype(jnp.float32).T
    walkers_out[...] = mine.astype(jnp.bfloat16)
    out_ref[...] = jnp.zeros_like(out_ref)
    out_ref[:rows, :] = jnp.dot(
        mine, inverse[...], precision=lax.Precision.HIGHEST, preferred_element_type=jnp.float32
    ).astype(jnp.bfloat16)


def order_kernel(rotated, partner, trial, out_ref, trial_out):
    at = position()
    trial_out[...] = trial[...]
    out_ref[at[0]] = rotated[...]
    out_ref[1 - at[0]] = partner[...]


def sum_kernel(b0, b1, b2, b3, out_ref):
    out_ref[...] = (b0[...] + b2[...]) + (b1[...] + b3[...])


def write_fields(at, shifted, swapped, out_ref):
    vectors = out_ref.shape[1]
    for step in range(NX):
        for low in range(NL):
            chip = ((at[1] + step) % NX) * NL + low
            row = step * NL + low
            out_ref[pl.ds(chip * NC + at[2], 1), :] = shifted[row : row + 1, :vectors]
            out_ref[pl.ds(chip * NC + 1 - at[2], 1), :] = swapped[row : row + 1, :]


def factor_kernel(trial, block, a1, a2, a3, a4, out_ref):
    count, vectors, depth = block.shape
    product = lax.dot_general(
        block[...].reshape(count * vectors, depth), trial[...], NT, preferred_element_type=jnp.float32
    ).astype(jnp.bfloat16)
    out_ref[...] = product.reshape(count, vectors, trial.shape[0])


def bias_kernel(r0, r1, r2, r3, own, other, aux, walkers, passed, out_ref, aux_out, walkers_out, passed_out):
    aux_out[...] = aux[...]
    walkers_out[...] = walkers[...]
    rows, vectors, depth = own.shape
    parts = []
    for factor in (own, other):
        total = jnp.zeros((8 * GROUP, GROUP * vectors), jnp.float32)
        tail = None
        for start, count in groups_of(rows):
            left = jnp.concatenate(
                [r[low, start : start + GROUP, :] for r in (r0, r1, r2, r3) for low in range(NL)], axis=0
            )
            right = factor[start : start + count].reshape(count * vectors, depth)
            product = lax.dot_general(left, right, NT, preferred_element_type=jnp.float32)
            if count == GROUP:
                total = total + product
            else:
                tail = product
        pieces = [total] if tail is None else [total, tail]
        summed = jnp.zeros((8, vectors), jnp.float32)
        for piece in pieces:
            width = piece.shape[1]
            kept = jnp.where(diagonal_mask(8 * GROUP, width), piece, 0.0)
            kept = jnp.sum(kept.reshape(8, GROUP, width), axis=1)
            pick = lax.broadcasted_iota(jnp.int32, (width, vectors), 0) % vectors == lax.broadcasted_iota(
                jnp.int32, (width, vectors), 1
            )
            summed = summed + jnp.dot(
                kept, pick.astype(jnp.float32), precision=lax.Precision.HIGHEST, preferred_element_type=jnp.float32
            )
        parts.append(summed)
    out_ref[...] = jnp.concatenate(parts, axis=1)


def fields_of(bias_refs, at, aux, aux_other, gathered):
    b0, b1, b2, b3 = bias_refs
    bias = (b0[...] + b2[...]) + (b1[...] + b3[...])
    vectors = aux.shape[1]
    for step in range(NX):
        for low in range(NL):
            walker = (((at[1] + step) % NX) * NL + low) * NC + at[2]
            row = step * NL + low
            gathered[row : row + 1, :vectors] = aux[pl.ds(walker, 1), :]
            gathered[row : row + 1, vectors:] = aux_other[pl.ds(walker, 1), :]
    return gathered[...] - jnp.clip(-root_step * bias, -shift_cap, shift_cap)


def block_diagonals(coefficients, vectors):
    tall, wide = 8 * GROUP, GROUP * vectors
    spread = (
        lax.broadcasted_iota(jnp.int32, (tall, 8), 0) // GROUP == lax.broadcasted_iota(jnp.int32, (tall, 8), 1)
    ).astype(jnp.bfloat16)
    repeat = (
        lax.broadcasted_iota(jnp.int32, (vectors, wide), 1) % vectors
        == lax.broadcasted_iota(jnp.int32, (vectors, wide), 0)
    ).astype(jnp.bfloat16)
    mask = diagonal_mask(tall, wide)
    blocks = []
    for at in range(2):
        piece = coefficients[:, at * vectors : (at + 1) * vectors]
        piece = jnp.dot(spread, piece, preferred_element_type=jnp.float32).astype(jnp.bfloat16)
        piece = jnp.dot(piece, repeat, preferred_element_type=jnp.float32)
        blocks.append(jnp.where(mask, piece, 0.0).astype(jnp.bfloat16))
    return blocks


def walker_sums(blocks, own, other, base, half, store):
    vectors, columns = own.shape[1:]
    for start, count in groups_of(half):
        depth = count * vectors
        for left in range(0, columns, 512):
            right = min(columns, left + 512)
            total = jnp.dot(
                blocks[0][:, :depth],
                own[pl.ds(base + start, count), :, left:right].reshape(depth, right - left),
                preferred_element_type=jnp.float32,
            ) + jnp.dot(
                blocks[1][:, :depth],
                other[pl.ds(base + start, count), :, left:right].reshape(depth, right - left),
                preferred_element_type=jnp.float32,
            )
            total = total.astype(jnp.bfloat16)
            for walker in ALL:
                store(walker, start, count, left, right, total[walker * GROUP : walker * GROUP + count, :])


ALL = list(range(NX * NL))


def operator_kernel(
    b0, b1, b2, b3, aux, aux_other, walkers, neighbours, own, other,
    fields_ref, swap_ref, e0, e1, e2, e3, away_ref, o0, o1, o2, o3, two_rows, gathered,
):
    at = position()
    stack(two_rows, walkers, neighbours)
    half = o0.shape[0]
    fields = fields_of((b0, b1, b2, b3), at, aux, aux_other, gathered)
    fields_ref[...] = fields
    swap_ref[...] = fields[:, own.shape[1] :]
    blocks = block_diagonals((root_step * fields).astype(jnp.bfloat16), own.shape[1])
    evens, odds = (e0, e1, e2, e3), (o0, o1, o2, o3)

    def store_away(walker, start, count, left, right, value):
        if walker % NL:
            row = walker // NL * PITCH + start
            away_ref[row : row + count, left:right] = value
        else:
            evens[walker // NL][half + start : half + start + count, left:right] = value

    def store_keep(walker, start, count, left, right, value):
        out = odds if walker % NL else evens
        out[walker // NL][start : start + count, left:right] = value

    walker_sums(blocks, own, other, (1 - at[0]) * half, half, store_away)
    walker_sums(blocks, own, other, at[0] * half, half, store_keep)


def wide(value):
    return value.astype(jnp.float32)


def pair_sum_kernel(k0, k1, k2, k3, arrived, shifted, swapped, walkers, partners, o0, o1, o2, o3, fields_ref, stacked):
    stack(stacked, walkers, partners)
    write_fields(position(), shifted, swapped, fields_ref)
    half = o0.shape[0]
    for step, (keep, out) in enumerate(((k0, o0), (k1, o1), (k2, o2), (k3, o3))):
        out[...] = (wide(keep[...]) + wide(arrived[step * PITCH : step * PITCH + half, :])).astype(out.dtype)


def stack(out, low, high):
    rows = low.shape[0]
    out[:rows, :] = low[...]
    out[rows:, :] = high[...]


def x_sum_kernel(p0, p1, p2, p3, out):
    half = out.shape[0]
    out[...] = (
        (wide(p0[half:, :]) + wide(p1[half:, :])) + (wide(p2[half:, :]) + wide(p3[half:, :]))
    ).astype(out.dtype)


def last_sum_kernel(p0, p1, p2, p3, arrived, q0, q1, q2, q3, walkers, partners, first, second, stacked):
    stack(stacked, walkers, partners)
    half = first.shape[0]
    even = (
        (wide(p0[:half, :]) + wide(p1[:half, :])) + (wide(p2[:half, :]) + wide(p3[:half, :]))
    ) + wide(arrived[...])
    odd = (wide(q0[...]) + wide(q1[...])) + (wide(q2[...]) + wide(q3[...]))
    at = position()
    turn = (at[3] - at[2] + NH) % NH
    pick = jnp.logical_or(turn == 1, turn == 2)
    first[...] = jnp.where(pick, even, odd).astype(first.dtype)
    second[...] = jnp.where(pick, odd, even).astype(second.dtype)


def choose_kernel(second, got, more, block0, block1):
    at = position()
    active = (at[2] + at[3]) % 2 == 0

    @pl.when(active)
    def _():
        block0[...] = second[...]
        block1[...] = got[...]

    @pl.when(jnp.logical_not(active))
    def _():
        block0[...] = got[...]
        block1[...] = more[...]


def stack_kernel(low, high, out):
    stack(out, low, high)


def stack_y_kernel(b0, b1, b2, b3, pair, after, quad, both):
    half = b0.shape[0]
    both[: 2 * half, :] = pair[...]
    for step, ref in enumerate((b0, b1, b2, b3)):
        quad[step * half : (step + 1) * half, :] = ref[...]
        both[(step + 2) * half : (step + 3) * half, :] = ref[...]


def pass_kernel(*refs):
    pass


def place_rows(pieces, base, held, out):
    low, _, _, _, y = position()
    half = held.shape[1]

    def take(source, index):
        ref, skip = pieces[source]
        return ref[(skip + index) * half : (skip + index + 1) * half, :]

    for step in range(NY):
        row = (((base % NH) // 2) * NY + (y - step + NY) % NY) * NL
        held[row + low] = take(step, 0)
        held[row + 1 - low] = take(step, 1)
        row = ((((base + 2) % NH) // 2) * NY + (y - step + NY) % NY) * NL
        held[row + low] = take(4, step)
        held[row + 1 - low] = take(5, step)
    for block in range(held.shape[0]):
        out[block * half : (block + 1) * half, :] = held[block]


def assemble_kernel(p0, p1, p2, p3, p4, p5, near, far, own_rows, last_rows, start, held, total):
    low, _, core, high, y = position()
    place_rows([(ref, 0) for ref in (p0, p1, p2, p3, p4, p5)], high + ((high + core) & 1), held, own_rows)
    half = held.shape[1]
    rows = 2 * half
    for part in range(NL):
        last_rows[part * half : (part + 1) * half, :] = held[(low * NY + y) * NL + part]
    for step, ref in enumerate((near, far)):
        for index in range(2 * NL * NC):
            total[step, index // (NL * NC), index % (NL * NC)] = ref[index * rows : (index + 1) * rows, :]
    for block in range(NH * NY):
        turn = y ^ (block % NY)
        index = ((block // NY // NC) ^ low) * NC + ((block // NY % NC) ^ core)
        start[block * rows : (block + 1) * rows, :] = total[turn // 2, turn % 2, index]


def taylor_kernel(own_rows, last_rows, start, mine, y1, y2, y3, quad, walkers, out_ref, held, other_rows, terms, total):
    low, _, core, high, y = position()
    base = high + ((high + core + 1) & 1)
    place_rows([(mine, 0), (y1, 0), (y2, 0), (y3, 0), (mine, 2), (quad, 0)], base, held, other_rows)
    rows = last_rows.shape[0]
    stretch = NY * rows
    block_here = (low * NC + core) * NY + y
    terms[0] = start[...]
    total[...] = wide(walkers[:rows, :])

    @pl.loop(1, TAYLOR)
    def _(degree):
        source = (degree - 1) % 2
        for side, ref in enumerate((own_rows, other_rows)):
            product = jnp.dot(ref[...], terms[source], preferred_element_type=jnp.float32)
            term = (product / degree.astype(jnp.float32)).astype(jnp.bfloat16)
            for pair in range(NH // 2):
                to = pl.multiple_of((2 * pair + (core ^ side)) * stretch, 16)
                terms[1 - source, pl.ds(to, stretch), :] = term[pair * stretch : (pair + 1) * stretch, :]
        for block in range(NH * NY):

            @pl.when(block_here == block)
            def _():
                total[...] += wide(terms[1 - source, block * rows : (block + 1) * rows, :])

    product = jnp.dot(last_rows[...], terms[(TAYLOR - 1) % 2], preferred_element_type=jnp.float32)
    out_ref[...] = (total[...] + wide((product / TAYLOR).astype(jnp.bfloat16))).astype(out_ref.dtype)


def call(kernel, outs, args, name, scratch=(), idle=0, limit=16):
    specs = [VMEM] * (len(args) - idle) + [FAR] * idle
    return pl.pallas_call(
        kernel,
        out_shape=outs,
        in_specs=specs,
        out_specs=[VMEM] * len(outs) if isinstance(outs, (list, tuple)) else VMEM,
        scratch_shapes=list(scratch),
        compiler_params=pltpu.CompilerParams(vmem_limit_bytes=limit * 2**20),
        name=name,
    )(*args)


def on_device(cholesky, walkers, inv_correlation, trial_orbitals, aux_fields):
    vectors, rows, orbitals = cholesky.shape
    occupied = walkers.shape[2]
    half = rows // NL
    bf16, f32 = jnp.bfloat16, jnp.float32
    shaped = jax.ShapeDtypeStruct
    own = jnp.transpose(cholesky, (1, 0, 2))
    other = swap_core(own)
    rotated, walker = call(
        rotate_kernel,
        [shaped((rows + -rows % GROUP, occupied), bf16), shaped((rows, occupied), bf16)],
        (walkers[0].T, inv_correlation[0]),
        "rotate",
    )
    partner = swap_low(rotated)
    both, trial = call(
        order_kernel,
        [shaped((NL,) + rotated.shape, bf16), shaped((occupied, orbitals), bf16)],
        (rotated, partner, trial_orbitals.T),
        "order",
    )
    rows_here = exchange(walker)
    met = [both] + [send_x(both, -step) for step in range(1, NX)]
    factor = call(
        factor_kernel,
        shaped((rows, vectors, occupied), bf16),
        (trial, other, *met[1:], rows_here),
        "vector_factor",
        idle=4,
    )
    bias, aux_here, rows_here, other = pl.pallas_call(
        bias_kernel,
        out_shape=[
            shaped((8, 2 * vectors), f32),
            shaped(aux_fields.shape, f32),
            shaped((rows, occupied), bf16),
            shaped(other.shape, bf16),
        ],
        in_specs=[VMEM] * 8 + [FAR],
        out_specs=[VMEM] * 3 + [FAR],
        input_output_aliases={8: 3},
        compiler_params=pltpu.CompilerParams(vmem_limit_bytes=16 * 2**20),
        name="force_bias",
    )(*met, swap_core(factor), factor, aux_fields, rows_here, other)
    near = swap_core(other)
    aux_other = swap_core(aux_here)
    from_y = [bias] + [send_y(bias, step) for step in range(1, NY)]
    bias = call(sum_kernel, shaped(bias.shape, f32), tuple(from_y), "sum_y")
    from_h = [bias] + [send_h(bias, step) for step in range(1, NH)]

    piece, two, quad = [shaped((n * half, orbitals), bf16) for n in (1, 2, 4)]
    shifted, shifted_other, *parts, two_rows = call(
        operator_kernel,
        [shaped((8, 2 * vectors), f32), shaped((8, vectors), f32)]
        + [two] * NX
        + [shaped((NX * PITCH, orbitals), bf16)]
        + [piece] * NX
        + [shaped((NC * rows, occupied), bf16)],
        (*from_h, aux_fields, aux_other, rows_here, swap_core(rows_here), near, other),
        "field_operator",
        scratch=[pltpu.VMEM((8, 2 * vectors), f32)],
    )
    even, away, odd = parts[:NX], parts[NX], parts[NX + 1 :]
    shifted_other = swap_core(shifted_other)
    away = swap_low(away)
    even = [even[0]] + [send_x(even[step], step) for step in range(1, NX)]
    low_rows = swap_low(two_rows)
    arrived = swap_low(call(x_sum_kernel, piece, tuple(even), "x_sum"))
    *odd, fields, four_rows = call(
        pair_sum_kernel,
        [piece] * NX + [shaped(aux_fields.shape, f32), shaped((NL * NC * rows, occupied), bf16)],
        (*odd, away, shifted, shifted_other, two_rows, low_rows),
        "pair_sum",
    )
    odd = [odd[0]] + [send_x(odd[step], step) for step in range(1, NX)]
    first, second, eight_rows = call(
        last_sum_kernel,
        [piece] * 2 + [shaped((2 * NL * NC * rows, occupied), bf16)],
        (*even, arrived, *odd, four_rows, flip_y(four_rows, 1)),
        "last_sum",
    )
    far_rows = flip_y(eight_rows, 2)

    got = everywhere(first, first_target)
    more = everywhere(second, second_target)
    block0, block1 = call(choose_kernel, [piece] * 2, (second, got, more), "choose")
    pair0 = call(stack_kernel, two, (block0, swap_low(block0)), "stack_low")
    block1s = [block1] + [send_y(block1, step) for step in range(1, NY)]
    quad1, mine = call(
        stack_y_kernel, [quad, shaped((6 * half, orbitals), bf16)], (*block1s, pair0, far_rows), "stack_y", idle=1
    )
    mine = swap_core(mine)
    arrived = [send_y(pair0, step) for step in range(1, NY)] + [swap_low(quad1)]
    arrived = pl.pallas_call(
        pass_kernel,
        out_shape=[two] * 3 + [quad],
        in_specs=[FAR] * 5,
        out_specs=[FAR] * 4,
        input_output_aliases={at: at for at in range(4)},
        compiler_params=pltpu.CompilerParams(vmem_limit_bytes=4 * 2**20),
        name="gathered",
    )(*arrived, mine)
    held = pltpu.VMEM((NH * NY, half, orbitals), bf16)
    own_rows, last_rows, start = call(
        assemble_kernel,
        [shaped((orbitals // 2, orbitals), bf16), two, shaped((orbitals, occupied), bf16)],
        (pair0, *arrived[:3], quad1, arrived[3], eight_rows, far_rows),
        "assemble",
        scratch=[held, pltpu.VMEM((2, 2, NL * NC, rows, occupied), bf16)],
    )
    updated = call(
        taylor_kernel,
        shaped((rows, occupied), bf16),
        (own_rows, last_rows, start, mine, *[swap_core(a) for a in arrived], eight_rows),
        "taylor",
        scratch=[
            held,
            pltpu.VMEM((orbitals // 2, orbitals), bf16),
            pltpu.VMEM((2, orbitals, occupied), bf16),
            pltpu.VMEM((rows, occupied), f32),
        ],
        limit=24,
    )
    return (exchange(updated)[None], fields)


def solution(mesh):
    placed = (
        P("vec", "pair", None),
        P("vec", "pair", None),
        P("vec", None, None),
        P(),
        P(None, "vec"),
    )
    return jax.shard_map(
        on_device,
        mesh=mesh,
        in_specs=placed,
        out_specs=(P("vec", "pair", None), P(None, "vec")),
        check_vma=False,
    )
```

profile of v0, /device:TPU:33, one launch (start us, length us, event | category | flops | bytes accessed | tf_op | source)
XLA Modules:
  0.0 165.0 jit_solution(12171867753669953132)
XLA Ops:
  0.6 0.8 collective-permute-start.4
  1.4 0.9 copy-done.1
  2.3 0.8 copy-done.2
  3.4 1.6 collective-permute-start
  5.1 2.2 %collective-permute-done.partner = bf16[112,200]{1,0:T(8,128)(2,1)S(1)} collective-permute-done((bf16[112,200]{1,0:T(8,128)(2,1)S(1)}, bf16[112,200]{1,0:T(8,128)(2,1)S(1)}, u32[]{:S(2)}, u32[]{:S(2)}) %collective-permute-start) | collective-permute-done | bytes 44832 | tf_op jit(solution)/shard_map/ppermute | solution.py:35
  7.3 1.1 copy-done
  8.4 1.1 collective-permute-start.3
  9.5 2.4 %collective-permute-start.2 = (bf16[2,112,200]{2,1,0:T(8,128)(2,1)S(1)}, bf16[2,112,200]{2,1,0:T(8,128)(2,1)S(1)}, u32[]{:S(2)}, u32[]{:S(2)}) collective-permute-start(bf16[2,112,200]{2,1,0:T(8,128)(2,1)S(1)} %get-tuple-element.43.r0), channel_id=1, source_target_pairs={{0,128},{16,144},{32,160},{48,176},{64,192},{80,208},{96,224},{112... | collective-permute-start | bytes 268808 | tf_op jit(solution)/shard_map/ppermute | solution.py:31
  11.9 1.2 collective-permute-start.1
  13.1 9.0 %collective-permute-start.5 = (bf16[100,200]{1,0:T(8,128)(2,1)S(1)}, bf16[100,200]{1,0:T(8,128)(2,1)S(1)}, u32[]{:S(2)}, u32[]{:S(2)}) collective-permute-start(bf16[100,200]{1,0:T(8,128)(2,1)S(1)} %get-tuple-element.45), channel_id=1, source_target_pairs={{0,0},{1,1},{2,2},{3,3},{4,16},{5,17},{6,18},{7,19},{8,32},{9,33},... | collective-permute-start | bytes 120008 | tf_op jit(solution)/shard_map/ppermute | solution.py:64
  22.1 2.1 %collective-permute-done.5.a4.walkers = bf16[100,200]{1,0:T(8,128)(2,1)S(1)} collective-permute-done((bf16[100,200]{1,0:T(8,128)(2,1)S(1)}, bf16[100,200]{1,0:T(8,128)(2,1)S(1)}, u32[]{:S(2)}, u32[]{:S(2)}) %collective-permute-start.5) | collective-permute-done | bytes 40032 | tf_op jit(solution)/shard_map/ppermute | solution.py:64
  24.2 1.7 %vector_factor.1.other = bf16[100,16,200]{2,1,0:T(8,128)(2,1)S(1)} custom-call(bf16[200,1600]{1,0:T(8,128)(2,1)S(1)} %get-tuple-element.44.trial, bf16[100,16,1600]{2,1,0:T(8,128)(2,1)S(1)} %collective-permute-done.4.block.passed, bf16[2,112,200]{2,1,0:T(8,128)(2,1)S(1)} %collective-permute-done.1.a1.r1, ...), custom_call_target="tpu_custom_call" | custom-call | tf_op jit(solution)/shard_map/vector_factor/pallas_call | solution.py:388
  25.9 1.1 collective-permute-start.6
  27.1 2.0 %collective-permute-done.6.own = bf16[100,16,200]{2,1,0:T(8,128)(2,1)S(1)} collective-permute-done((bf16[100,16,200]{2,1,0:T(8,128)(2,1)S(1)}, bf16[100,16,200]{2,1,0:T(8,128)(2,1)S(1)}, u32[]{:S(2)}, u32[]{:S(2)}) %collective-permute-start.6) | collective-permute-done | bytes 640032 | tf_op jit(solution)/shard_map/ppermute | solution.py:39
  29.0 1.5 force_bias.1
  31.1 2.7 %collective-permute-start.9 = (f32[8,32]{1,0:T(8,128)S(1)}, f32[8,32]{1,0:T(8,128)S(1)}, u32[]{:S(2)}, u32[]{:S(2)}) collective-permute-start(f32[8,32]{1,0:T(8,128)S(1)} %get-tuple-element.46.b0), channel_id=1, source_target_pairs={{0,3},{1,0},{2,1},{3,2},{4,7},{5,4},{6,5},{7,6},{8,11},{9,8},{10,9... | collective-permute-start | bytes 3080 | tf_op jit(solution)/shard_map/ppermute | solution.py:43
  34.1 0.7 collective-permute-start.7
  34.9 1.2 collective-permute-start.13
  36.1 1.7 %collective-permute-done.8.b2 = f32[8,32]{1,0:T(8,128)S(1)} collective-permute-done((f32[8,32]{1,0:T(8,128)S(1)}, f32[8,32]{1,0:T(8,128)S(1)}, u32[]{:S(2)}, u32[]{:S(2)}) %collective-permute-start.8) | collective-permute-done | bytes 1056 | tf_op jit(solution)/shard_map/ppermute | solution.py:43
  37.8 1.0 collective-permute-start.12
  38.8 2.3 %collective-permute-start.11 = (f32[8,32]{1,0:T(8,128)S(1)}, f32[8,32]{1,0:T(8,128)S(1)}, u32[]{:S(2)}, u32[]{:S(2)}) collective-permute-start(f32[8,32]{1,0:T(8,128)S(1)} %sum_y.1.b0), channel_id=1, source_target_pairs={{0,8},{1,9},{2,10},{3,11},{4,12},{5,13},{6,14},{7,15},{8,0},{9,1},... | collective-permute-start | bytes 3080 | tf_op jit(solution)/shard_map/ppermute | solution.py:51
  41.2 4.0 %collective-permute-done.11.b2 = f32[8,32]{1,0:T(8,128)S(1)} collective-permute-done((f32[8,32]{1,0:T(8,128)S(1)}, f32[8,32]{1,0:T(8,128)S(1)}, u32[]{:S(2)}, u32[]{:S(2)}) %collective-permute-start.11) | collective-permute-done | bytes 1056 | tf_op jit(solution)/shard_map/ppermute | solution.py:51
  45.2 0.5 collective-permute-done.10.b1
  45.7 2.5 %field_operator.1 = (f32[8,32]{1,0:T(8,128)S(1)}, f32[8,16]{1,0:T(8,128)S(1)}, bf16[100,1600]{1,0:T(8,128)(2,1)S(1)}, bf16[100,1600]{1,0:T(8,128)(2,1)S(1)}, bf1...) custom-call(f32[8,32]{1,0:T(8,128)S(1)} %sum_y.1.b0, ...), custom_call_target="tpu_custom_call" | custom-call | tf_op jit(solution)/shard_map/field_operator/pallas_call | solution.py:388
  48.2 2.4 %collective-permute-start.20 = (bf16[224,1600]{1,0:T(8,128)(2,1)S(1)}, bf16[224,1600]{1,0:T(8,128)(2,1)S(1)}, u32[]{:S(2)}, u32[]{:S(2)}) collective-permute-start(bf16[224,1600]{1,0:T(8,128)(2,1)S(1)} %get-tuple-element.58), channel_id=1, source_target_pairs={{0,32},{16,48},{32,0},{48,16},{64,96},{80,112},{96,64},{112,80},{1... | collective-permute-start | bytes 2150408 | tf_op jit(solution)/shard_map/ppermute | solution.py:35
  50.9 0.6 collective-permute-start.17
  51.5 1.8 %collective-permute-start.18 = (bf16[100,1600]{1,0:T(8,128)(2,1)S(1)}, bf16[100,1600]{1,0:T(8,128)(2,1)S(1)}, u32[]{:S(2)}, u32[]{:S(2)}) collective-permute-start(bf16[100,1600]{1,0:T(8,128)(2,1)S(1)} %get-tuple-element.53), channel_id=1, source_target_pairs={{0,192},{16,208},{32,224},{48,240},{64,0},{80,16},{96,32},{112,48}... | collective-permute-start | bytes 960008 | tf_op jit(solution)/shard_map/ppermute | solution.py:31
  53.5 8.8 %collective-permute-done.16.p1 = bf16[100,1600]{1,0:T(8,128)(2,1)S(1)} collective-permute-done((bf16[100,1600]{1,0:T(8,128)(2,1)S(1)}, bf16[100,1600]{1,0:T(8,128)(2,1)S(1)}, u32[]{:S(2)}, u32[]{:S(2)}) %collective-permute-start.16) | collective-permute-done | bytes 320032 | tf_op jit(solution)/shard_map/ppermute | solution.py:31
  62.3 7.5 %collective-permute-start.21 = (f32[8,16]{1,0:T(8,128)S(1)}, f32[8,16]{1,0:T(8,128)S(1)}, u32[]{:S(2)}, u32[]{:S(2)}) collective-permute-start(f32[8,16]{1,0:T(8,128)S(1)} %get-tuple-element.60), channel_id=1, source_target_pairs={{0,16},{16,0},{32,48},{48,32},{64,80},{80,64},{96,112},{112,96},{1... | collective-permute-start | bytes 1544 | tf_op jit(solution)/shard_map/ppermute | solution.py:39
  70.1 0.5 collective-permute-done.21.swapped
  70.6 0.7 pair_sum.1
  71.3 2.5 %collective-permute-start.24 = (bf16[50,1600]{1,0:T(8,128)(2,1)S(1)}, bf16[50,1600]{1,0:T(8,128)(2,1)S(1)}, u32[]{:S(2)}, u32[]{:S(2)}) collective-permute-start(bf16[50,1600]{1,0:T(8,128)(2,1)S(1)} %get-tuple-element.64), channel_id=1, source_target_pairs={{0,128},{16,144},{32,160},{48,176},{64,192},{80,208},{96,224},{112... | collective-permute-start | bytes 480008 | tf_op jit(solution)/shard_map/ppermute | solution.py:31
  74.0 1.6 collective-permute-done.19.arrived
  75.6 3.9 %collective-permute-done.23.q1 = bf16[50,1600]{1,0:T(8,128)(2,1)S(1)} collective-permute-done((bf16[50,1600]{1,0:T(8,128)(2,1)S(1)}, bf16[50,1600]{1,0:T(8,128)(2,1)S(1)}, u32[]{:S(2)}, u32[]{:S(2)}) %collective-permute-start.23) | collective-permute-done | bytes 160032 | tf_op jit(solution)/shard_map/ppermute | solution.py:31
  79.5 1.7 %collective-permute-done.24.q2 = bf16[50,1600]{1,0:T(8,128)(2,1)S(1)} collective-permute-done((bf16[50,1600]{1,0:T(8,128)(2,1)S(1)}, bf16[50,1600]{1,0:T(8,128)(2,1)S(1)}, u32[]{:S(2)}, u32[]{:S(2)}) %collective-permute-start.24) | collective-permute-done | bytes 160032 | tf_op jit(solution)/shard_map/ppermute | solution.py:31
  81.2 1.5 collective-permute-done.25.q3
  83.0 3.2 %collective-permute-start.27 = (bf16[50,1600]{1,0:T(8,128)(2,1)S(1)}, bf16[50,1600]{1,0:T(8,128)(2,1)S(1)}, u32[]{:S(2)}, u32[]{:S(2)}) collective-permute-start(bf16[50,1600]{1,0:T(8,128)(2,1)S(1)} %get-tuple-element.68), channel_id=1, source_target_pairs={{0,8},{1,9},{2,10},{3,11},{4,16},{5,17},{6,18},{7,19},{8,0},{9,1},... | collective-permute-start | bytes 480008 | tf_op jit(solution)/shard_map/ppermute | solution.py:64
  86.2 1.9 %collective-permute-start.28 = (bf16[50,1600]{1,0:T(8,128)(2,1)S(1)}, bf16[50,1600]{1,0:T(8,128)(2,1)S(1)}, u32[]{:S(2)}, u32[]{:S(2)}) collective-permute-start(bf16[50,1600]{1,0:T(8,128)(2,1)S(1)} %get-tuple-element.67.second), channel_id=1, source_target_pairs={{4,24},{5,25},{6,26},{7,27},{12,16},{13,17},{14,18},{15,19},{16,4}... | collective-permute-start | bytes 480008 | tf_op jit(solution)/shard_map/ppermute | solution.py:64
  88.1 1.8 %collective-permute-start.36 = (bf16[800,200]{1,0:T(8,128)(2,1)S(1)}, bf16[800,200]{1,0:T(8,128)(2,1)S(1)}, u32[]{:S(2)}, u32[]{:S(2)}) collective-permute-start(bf16[800,200]{1,0:T(8,128)(2,1)S(1)} %get-tuple-element.71.near.walkers), channel_id=1, source_target_pairs={{0,2},{1,3},{2,0},{3,1},{4,6},{5,7},{6,4},{7,5},{8,10},{9,11},{10,... | collective-permute-start | bytes 960008 | tf_op jit(solution)/shard_map/ppermute | solution.py:47
  89.9 2.9 %collective-permute-done.27.got = bf16[50,1600]{1,0:T(8,128)(2,1)S(1)} collective-permute-done((bf16[50,1600]{1,0:T(8,128)(2,1)S(1)}, bf16[50,1600]{1,0:T(8,128)(2,1)S(1)}, u32[]{:S(2)}, u32[]{:S(2)}) %collective-permute-start.27) | collective-permute-done | bytes 160032 | tf_op jit(solution)/shard_map/ppermute | solution.py:64
  92.8 6.1 %collective-permute-done.28.more = bf16[50,1600]{1,0:T(8,128)(2,1)S(1)} collective-permute-done((bf16[50,1600]{1,0:T(8,128)(2,1)S(1)}, bf16[50,1600]{1,0:T(8,128)(2,1)S(1)}, u32[]{:S(2)}, u32[]{:S(2)}) %collective-permute-start.28) | collective-permute-done | bytes 160032 | tf_op jit(solution)/shard_map/ppermute | solution.py:64
  98.9 1.4 collective-permute-start.29
  100.3 1.7 %collective-permute-start.35 = (bf16[50,1600]{1,0:T(8,128)(2,1)S(1)}, bf16[50,1600]{1,0:T(8,128)(2,1)S(1)}, u32[]{:S(2)}, u32[]{:S(2)}) collective-permute-start(bf16[50,1600]{1,0:T(8,128)(2,1)S(1)} %get-tuple-element.70.b0), channel_id=1, source_target_pairs={{0,3},{1,0},{2,1},{3,2},{4,7},{5,4},{6,5},{7,6},{8,11},{9,8},{10,9... | collective-permute-start | bytes 480008 | tf_op jit(solution)/shard_map/ppermute | solution.py:43
  102.2 0.8 collective-permute-start.33
  102.9 2.8 %collective-permute-done.29.high = bf16[50,1600]{1,0:T(8,128)(2,1)S(1)} collective-permute-done((bf16[50,1600]{1,0:T(8,128)(2,1)S(1)}, bf16[50,1600]{1,0:T(8,128)(2,1)S(1)}, u32[]{:S(2)}, u32[]{:S(2)}) %collective-permute-start.29) | collective-permute-done | bytes 160032 | tf_op jit(solution)/shard_map/ppermute | solution.py:35
  105.8 3.7 %collective-permute-done.35.b3 = bf16[50,1600]{1,0:T(8,128)(2,1)S(1)} collective-permute-done((bf16[50,1600]{1,0:T(8,128)(2,1)S(1)}, bf16[50,1600]{1,0:T(8,128)(2,1)S(1)}, u32[]{:S(2)}, u32[]{:S(2)}) %collective-permute-start.35) | collective-permute-done | bytes 160032 | tf_op jit(solution)/shard_map/ppermute | solution.py:43
  109.5 0.5 collective-permute-done.34.b2
  110.0 3.5 %collective-permute-done.33.b1 = bf16[50,1600]{1,0:T(8,128)(2,1)S(1)} collective-permute-done((bf16[50,1600]{1,0:T(8,128)(2,1)S(1)}, bf16[50,1600]{1,0:T(8,128)(2,1)S(1)}, u32[]{:S(2)}, u32[]{:S(2)}) %collective-permute-start.33) | collective-permute-done | bytes 160032 | tf_op jit(solution)/shard_map/ppermute | solution.py:43
  113.6 0.5 collective-permute-start.38
  114.1 0.8 collective-permute-start.37
  115.0 0.7 collective-permute-start.31
  115.7 0.7 collective-permute-start.30
  116.4 7.9 %collective-permute-done.32.refs_2_ = bf16[100,1600]{1,0:T(8,128)(2,1)S(1)} collective-permute-done((bf16[100,1600]{1,0:T(8,128)(2,1)S(1)}, bf16[100,1600]{1,0:T(8,128)(2,1)S(1)}, u32[]{:S(2)}, u32[]{:S(2)}) %collective-permute-start.32) | collective-permute-done | bytes 320032 | tf_op jit(solution)/shard_map/ppermute | solution.py:43
  124.3 1.2 collective-permute-done.31.refs_1_
  125.5 8.5 %collective-permute-done.30.refs_0_ = bf16[100,1600]{1,0:T(8,128)(2,1)S(1)} collective-permute-done((bf16[100,1600]{1,0:T(8,128)(2,1)S(1)}, bf16[100,1600]{1,0:T(8,128)(2,1)S(1)}, u32[]{:S(2)}, u32[]{:S(2)}) %collective-permute-start.30) | collective-permute-done | bytes 320032 | tf_op jit(solution)/shard_map/ppermute | solution.py:43
  133.9 0.6 collective-permute-start.42
  135.1 0.9 assemble.1
  136.0 0.7 collective-permute-done.39.y1
  136.7 0.5 collective-permute-done.40.y2
  137.2 0.5 collective-permute-done.41.y3
  137.7 17.8 %taylor.1 = bf16[100,200]{1,0:T(8,128)(2,1)S(1)} custom-call(bf16[800,1600]{1,0:T(8,128)(2,1)S(1)} %get-tuple-element.78.own_rows, bf16[100,1600]{1,0:T(8,128)(2,1)S(1)} %get-tuple-element.79.last_rows, bf16[1600,200]{1,0:T(8,128)(2,1)S(1)} %get-tuple-element.80.start, bf16[300,1600]{1,0:T(8,128)(2,1)S(1)} %collective-permute-done.38.refs_4_.mine, ...), custom_call_target="tpu_custom_call" | custom-call | tf_op jit(solution)/shard_map/taylor/pallas_call | solution.py:388
  155.5 1.9 %collective-permute-start.43 = (bf16[100,200]{1,0:T(8,128)(2,1)S(1)}, bf16[100,200]{1,0:T(8,128)(2,1)S(1)}, u32[]{:S(2)}, u32[]{:S(2)}) collective-permute-start(bf16[100,200]{1,0:T(8,128)(2,1)S(1)} %taylor.1), channel_id=1, source_target_pairs={{0,0},{1,1},{2,2},{3,3},{4,16},{5,17},{6,18},{7,19},{8,32},{9,33},... | collective-permute-start | bytes 120008 | tf_op jit(solution)/shard_map/ppermute | solution.py:64
  157.4 6.8 %collective-permute-done.43 = bf16[100,200]{1,0:T(8,128)(2,1)S(1)} collective-permute-done((bf16[100,200]{1,0:T(8,128)(2,1)S(1)}, bf16[100,200]{1,0:T(8,128)(2,1)S(1)}, u32[]{:S(2)}, u32[]{:S(2)}) %collective-permute-start.43) | collective-permute-done | bytes 40032 | tf_op jit(solution)/shard_map/ppermute | solution.py:64
  164.3 0.7 copy.12
  (48 shorter events, 3.7 us)
Async XLA Ops:
  0.6 23.6 %collective-permute-start.4 = (bf16[100,16,1600]{2,1,0:T(8,128)(2,1)}, bf16[100,16,1600]{2,1,0:T(8,128)(2,1)S(1)}, u32[]{:S(2)}, u32[]{:S(2)}) collective-permute-start(bf16[100,16,1600]{2,1,0:T(8,128)(2,1)} %bitcast.11), channel_id=1, source_target_pairs={{0,16},{16,0},{32,48},{48,32},{64,80},{80,64},{96,112},{112,96},{1... | collective-permute-start | bytes 15360008 | tf_op jit(solution)/shard_map/ppermute | solution.py:39
  1.4 0.9 copy-start.1
  2.3 0.8 copy-start.2
  3.1 25.9 %copy-start.3 = (f32[16,16]{1,0:T(8,128)S(1)}, f32[16,16]{1,0:T(8,128)}, u32[]{:S(2)}) copy-start(f32[16,16]{1,0:T(8,128)} %aux.3) | copy-start | bytes 3076
  3.4 3.9 %collective-permute-start = (bf16[112,200]{1,0:T(8,128)(2,1)S(1)}, bf16[112,200]{1,0:T(8,128)(2,1)S(1)}, u32[]{:S(2)}, u32[]{:S(2)}) collective-permute-start(bf16[112,200]{1,0:T(8,128)(2,1)S(1)} %get-tuple-element.42.rotated), channel_id=1, source_target_pairs={{0,32},{16,48},{32,0},{48,16},{64,96},{80,112},{96,64},{112,80},{1... | collective-permute-start | bytes 134408 | tf_op jit(solution)/shard_map/ppermute | solution.py:35
  7.3 1.1 copy-start
  8.4 15.8 %collective-permute-start.3 = (bf16[2,112,200]{2,1,0:T(8,128)(2,1)S(1)}, bf16[2,112,200]{2,1,0:T(8,128)(2,1)S(1)}, u32[]{:S(2)}, u32[]{:S(2)}) collective-permute-start(bf16[2,112,200]{2,1,0:T(8,128)(2,1)S(1)} %get-tuple-element.43.r0), channel_id=1, source_target_pairs={{0,64},{16,80},{32,96},{48,112},{64,128},{80,144},{96,160},{112,17... | collective-permute-start | bytes 268808 | tf_op jit(solution)/shard_map/ppermute | solution.py:31
  9.5 14.7 %collective-permute-start.2 = (bf16[2,112,200]{2,1,0:T(8,128)(2,1)S(1)}, bf16[2,112,200]{2,1,0:T(8,128)(2,1)S(1)}, u32[]{:S(2)}, u32[]{:S(2)}) collective-permute-start(bf16[2,112,200]{2,1,0:T(8,128)(2,1)S(1)} %get-tuple-element.43.r0), channel_id=1, source_target_pairs={{0,128},{16,144},{32,160},{48,176},{64,192},{80,208},{96,224},{112... | collective-permute-start | bytes 268808 | tf_op jit(solution)/shard_map/ppermute | solution.py:31
  11.9 12.3 %collective-permute-start.1 = (bf16[2,112,200]{2,1,0:T(8,128)(2,1)S(1)}, bf16[2,112,200]{2,1,0:T(8,128)(2,1)S(1)}, u32[]{:S(2)}, u32[]{:S(2)}) collective-permute-start(bf16[2,112,200]{2,1,0:T(8,128)(2,1)S(1)} %get-tuple-element.43.r0), channel_id=1, source_target_pairs={{0,192},{16,208},{32,224},{48,240},{64,0},{80,16},{96,32},{112,48}... | collective-permute-start | bytes 268808 | tf_op jit(solution)/shard_map/ppermute | solution.py:31
  13.1 11.1 %collective-permute-start.5 = (bf16[100,200]{1,0:T(8,128)(2,1)S(1)}, bf16[100,200]{1,0:T(8,128)(2,1)S(1)}, u32[]{:S(2)}, u32[]{:S(2)}) collective-permute-start(bf16[100,200]{1,0:T(8,128)(2,1)S(1)} %get-tuple-element.45), channel_id=1, source_target_pairs={{0,0},{1,1},{2,2},{3,3},{4,16},{5,17},{6,18},{7,19},{8,32},{9,33},... | collective-permute-start | bytes 120008 | tf_op jit(solution)/shard_map/ppermute | solution.py:64
  25.9 3.1 %collective-permute-start.6 = (bf16[100,16,200]{2,1,0:T(8,128)(2,1)S(1)}, bf16[100,16,200]{2,1,0:T(8,128)(2,1)S(1)}, u32[]{:S(2)}, u32[]{:S(2)}) collective-permute-start(bf16[100,16,200]{2,1,0:T(8,128)(2,1)S(1)} %vector_factor.1.other), channel_id=1, source_target_pairs={{0,16},{16,0},{32,48},{48,32},{64,80},{80,64},{96,112},{112,96},{1... | collective-permute-start | bytes 1920008 | tf_op jit(solution)/shard_map/ppermute | solution.py:39
  30.5 15.2 %collective-permute-start.15 = (bf16[100,16,1600]{2,1,0:T(8,128)(2,1)S(1)}, bf16[100,16,1600]{2,1,0:T(8,128)(2,1)S(1)}, u32[]{:S(2)}, u32[]{:S(2)}) collective-permute-start(bf16[100,16,1600]{2,1,0:T(8,128)(2,1)S(1)} %get-tuple-element.49.other), channel_id=1, source_target_pairs={{0,16},{16,0},{32,48},{48,32},{64,80},{80,64},{96,112},{112,96},{1... | collective-permute-start | bytes 15360008 | tf_op jit(solution)/shard_map/ppermute | solution.py:39
  30.9 14.8 %collective-permute-start.14 = (bf16[100,200]{1,0:T(8,128)(2,1)S(1)}, bf16[100,200]{1,0:T(8,128)(2,1)S(1)}, u32[]{:S(2)}, u32[]{:S(2)}) collective-permute-start(bf16[100,200]{1,0:T(8,128)(2,1)S(1)} %get-tuple-element.48.walkers), channel_id=1, source_target_pairs={{0,16},{16,0},{32,48},{48,32},{64,80},{80,64},{96,112},{112,96},{1... | collective-permute-start | bytes 120008 | tf_op jit(solution)/shard_map/ppermute | solution.py:39
  31.1 3.8 %collective-permute-start.9 = (f32[8,32]{1,0:T(8,128)S(1)}, f32[8,32]{1,0:T(8,128)S(1)}, u32[]{:S(2)}, u32[]{:S(2)}) collective-permute-start(f32[8,32]{1,0:T(8,128)S(1)} %get-tuple-element.46.b0), channel_id=1, source_target_pairs={{0,3},{1,0},{2,1},{3,2},{4,7},{5,4},{6,5},{7,6},{8,11},{9,8},{10,9... | collective-permute-start | bytes 3080 | tf_op jit(solution)/shard_map/ppermute | solution.py:43
  33.8 4.0 %collective-permute-start.8 = (f32[8,32]{1,0:T(8,128)S(1)}, f32[8,32]{1,0:T(8,128)S(1)}, u32[]{:S(2)}, u32[]{:S(2)}) collective-permute-start(f32[8,32]{1,0:T(8,128)S(1)} %get-tuple-element.46.b0), channel_id=1, source_target_pairs={{0,2},{1,3},{2,0},{3,1},{4,6},{5,7},{6,4},{7,5},{8,10},{9,11},{10,... | collective-permute-start | bytes 3080 | tf_op jit(solution)/shard_map/ppermute | solution.py:43
  34.1 3.7 %collective-permute-start.7 = (f32[8,32]{1,0:T(8,128)S(1)}, f32[8,32]{1,0:T(8,128)S(1)}, u32[]{:S(2)}, u32[]{:S(2)}) collective-permute-start(f32[8,32]{1,0:T(8,128)S(1)} %get-tuple-element.46.b0), channel_id=1, source_target_pairs={{0,1},{1,2},{2,3},{3,0},{4,5},{5,6},{6,7},{7,4},{8,9},{9,10},{10,1... | collective-permute-start | bytes 3080 | tf_op jit(solution)/shard_map/ppermute | solution.py:43
  34.9 6.3 %collective-permute-start.13 = (f32[16,16]{1,0:T(8,128)S(1)}, f32[16,16]{1,0:T(8,128)S(1)}, u32[]{:S(2)}, u32[]{:S(2)}) collective-permute-start(f32[16,16]{1,0:T(8,128)S(1)} %get-tuple-element.47), channel_id=1, source_target_pairs={{0,16},{16,0},{32,48},{48,32},{64,80},{80,64},{96,112},{112,96},{1... | collective-permute-start | bytes 3080 | tf_op jit(solution)/shard_map/ppermute | solution.py:39
  37.8 3.4 %collective-permute-start.12 = (f32[8,32]{1,0:T(8,128)S(1)}, f32[8,32]{1,0:T(8,128)S(1)}, u32[]{:S(2)}, u32[]{:S(2)}) collective-permute-start(f32[8,32]{1,0:T(8,128)S(1)} %sum_y.1.b0), channel_id=1, source_target_pairs={{0,12},{1,13},{2,14},{3,15},{4,0},{5,1},{6,2},{7,3},{8,4},{9,5},{1... | collective-permute-start | bytes 3080 | tf_op jit(solution)/shard_map/ppermute | solution.py:51
  38.8 6.4 %collective-permute-start.11 = (f32[8,32]{1,0:T(8,128)S(1)}, f32[8,32]{1,0:T(8,128)S(1)}, u32[]{:S(2)}, u32[]{:S(2)}) collective-permute-start(f32[8,32]{1,0:T(8,128)S(1)} %sum_y.1.b0), channel_id=1, source_target_pairs={{0,8},{1,9},{2,10},{3,11},{4,12},{5,13},{6,14},{7,15},{8,0},{9,1},... | collective-permute-start | bytes 3080 | tf_op jit(solution)/shard_map/ppermute | solution.py:51
  41.1 4.6 %collective-permute-start.10 = (f32[8,32]{1,0:T(8,128)S(1)}, f32[8,32]{1,0:T(8,128)S(1)}, u32[]{:S(2)}, u32[]{:S(2)}) collective-permute-start(f32[8,32]{1,0:T(8,128)S(1)} %sum_y.1.b0), channel_id=1, source_target_pairs={{0,4},{1,5},{2,6},{3,7},{4,8},{5,9},{6,10},{7,11},{8,12},{9,13},{1... | collective-permute-start | bytes 3080 | tf_op jit(solution)/shard_map/ppermute | solution.py:51
  48.2 22.4 %collective-permute-start.20 = (bf16[224,1600]{1,0:T(8,128)(2,1)S(1)}, bf16[224,1600]{1,0:T(8,128)(2,1)S(1)}, u32[]{:S(2)}, u32[]{:S(2)}) collective-permute-start(bf16[224,1600]{1,0:T(8,128)(2,1)S(1)} %get-tuple-element.58), channel_id=1, source_target_pairs={{0,32},{16,48},{32,0},{48,16},{64,96},{80,112},{96,64},{112,80},{1... | collective-permute-start | bytes 2150408 | tf_op jit(solution)/shard_map/ppermute | solution.py:35
  50.6 11.7 %collective-permute-start.16 = (bf16[100,1600]{1,0:T(8,128)(2,1)S(1)}, bf16[100,1600]{1,0:T(8,128)(2,1)S(1)}, u32[]{:S(2)}, u32[]{:S(2)}) collective-permute-start(bf16[100,1600]{1,0:T(8,128)(2,1)S(1)} %get-tuple-element.51), channel_id=1, source_target_pairs={{0,64},{16,80},{32,96},{48,112},{64,128},{80,144},{96,160},{112,17... | collective-permute-start | bytes 960008 | tf_op jit(solution)/shard_map/ppermute | solution.py:31
  50.9 18.8 %collective-permute-start.17 = (bf16[100,1600]{1,0:T(8,128)(2,1)S(1)}, bf16[100,1600]{1,0:T(8,128)(2,1)S(1)}, u32[]{:S(2)}, u32[]{:S(2)}) collective-permute-start(bf16[100,1600]{1,0:T(8,128)(2,1)S(1)} %get-tuple-element.52), channel_id=1, source_target_pairs={{0,128},{16,144},{32,160},{48,176},{64,192},{80,208},{96,224},{112... | collective-permute-start | bytes 960008 | tf_op jit(solution)/shard_map/ppermute | solution.py:31
  51.5 18.3 %collective-permute-start.18 = (bf16[100,1600]{1,0:T(8,128)(2,1)S(1)}, bf16[100,1600]{1,0:T(8,128)(2,1)S(1)}, u32[]{:S(2)}, u32[]{:S(2)}) collective-permute-start(bf16[100,1600]{1,0:T(8,128)(2,1)S(1)} %get-tuple-element.53), channel_id=1, source_target_pairs={{0,192},{16,208},{32,224},{48,240},{64,0},{80,16},{96,32},{112,48}... | collective-permute-start | bytes 960008 | tf_op jit(solution)/shard_map/ppermute | solution.py:31
  53.3 17.3 %collective-permute-start.22 = (bf16[200,200]{1,0:T(8,128)(2,1)S(1)}, bf16[200,200]{1,0:T(8,128)(2,1)S(1)}, u32[]{:S(2)}, u32[]{:S(2)}) collective-permute-start(bf16[200,200]{1,0:T(8,128)(2,1)S(1)} %get-tuple-element.61.walkers), channel_id=1, source_target_pairs={{0,32},{16,48},{32,0},{48,16},{64,96},{80,112},{96,64},{112,80},{1... | collective-permute-start | bytes 240008 | tf_op jit(solution)/shard_map/ppermute | solution.py:35
  62.3 8.3 %collective-permute-start.21 = (f32[8,16]{1,0:T(8,128)S(1)}, f32[8,16]{1,0:T(8,128)S(1)}, u32[]{:S(2)}, u32[]{:S(2)}) collective-permute-start(f32[8,16]{1,0:T(8,128)S(1)} %get-tuple-element.60), channel_id=1, source_target_pairs={{0,16},{16,0},{32,48},{48,32},{64,80},{80,64},{96,112},{112,96},{1... | collective-permute-start | bytes 1544 | tf_op jit(solution)/shard_map/ppermute | solution.py:39
  69.9 5.7 %collective-permute-start.19 = (bf16[50,1600]{1,0:T(8,128)(2,1)S(1)}, bf16[50,1600]{1,0:T(8,128)(2,1)S(1)}, u32[]{:S(2)}, u32[]{:S(2)}) collective-permute-start(bf16[50,1600]{1,0:T(8,128)(2,1)S(1)} %x_sum.1), channel_id=1, source_target_pairs={{0,32},{16,48},{32,0},{48,16},{64,96},{80,112},{96,64},{112,80},{1... | collective-permute-start | bytes 480008 | tf_op jit(solution)/shard_map/ppermute | solution.py:35
  71.3 8.2 %collective-permute-start.23 = (bf16[50,1600]{1,0:T(8,128)(2,1)S(1)}, bf16[50,1600]{1,0:T(8,128)(2,1)S(1)}, u32[]{:S(2)}, u32[]{:S(2)}) collective-permute-start(bf16[50,1600]{1,0:T(8,128)(2,1)S(1)} %get-tuple-element.63), channel_id=1, source_target_pairs={{0,64},{16,80},{32,96},{48,112},{64,128},{80,144},{96,160},{112,17... | collective-permute-start | bytes 480008 | tf_op jit(solution)/shard_map/ppermute | solution.py:31
  71.3 9.9 %collective-permute-start.24 = (bf16[50,1600]{1,0:T(8,128)(2,1)S(1)}, bf16[50,1600]{1,0:T(8,128)(2,1)S(1)}, u32[]{:S(2)}, u32[]{:S(2)}) collective-permute-start(bf16[50,1600]{1,0:T(8,128)(2,1)S(1)} %get-tuple-element.64), channel_id=1, source_target_pairs={{0,128},{16,144},{32,160},{48,176},{64,192},{80,208},{96,224},{112... | collective-permute-start | bytes 480008 | tf_op jit(solution)/shard_map/ppermute | solution.py:31
  73.8 8.9 %collective-permute-start.25 = (bf16[50,1600]{1,0:T(8,128)(2,1)S(1)}, bf16[50,1600]{1,0:T(8,128)(2,1)S(1)}, u32[]{:S(2)}, u32[]{:S(2)}) collective-permute-start(bf16[50,1600]{1,0:T(8,128)(2,1)S(1)} %get-tuple-element.65), channel_id=1, source_target_pairs={{0,192},{16,208},{32,224},{48,240},{64,0},{80,16},{96,32},{112,48}... | collective-permute-start | bytes 480008 | tf_op jit(solution)/shard_map/ppermute | solution.py:31
  73.9 8.7 %collective-permute-start.26 = (bf16[400,200]{1,0:T(8,128)(2,1)S(1)}, bf16[400,200]{1,0:T(8,128)(2,1)S(1)}, u32[]{:S(2)}, u32[]{:S(2)}) collective-permute-start(bf16[400,200]{1,0:T(8,128)(2,1)S(1)} %get-tuple-element.66.walkers), channel_id=1, source_target_pairs={{0,1},{1,0},{2,3},{3,2},{4,5},{5,4},{6,7},{7,6},{8,9},{9,8},{10,11... | collective-permute-start | bytes 480008 | tf_op jit(solution)/shard_map/ppermute | solution.py:47
  83.0 9.8 %collective-permute-start.27 = (bf16[50,1600]{1,0:T(8,128)(2,1)S(1)}, bf16[50,1600]{1,0:T(8,128)(2,1)S(1)}, u32[]{:S(2)}, u32[]{:S(2)}) collective-permute-start(bf16[50,1600]{1,0:T(8,128)(2,1)S(1)} %get-tuple-element.68), channel_id=1, source_target_pairs={{0,8},{1,9},{2,10},{3,11},{4,16},{5,17},{6,18},{7,19},{8,0},{9,1},... | collective-permute-start | bytes 480008 | tf_op jit(solution)/shard_map/ppermute | solution.py:64
  86.2 12.7 %collective-permute-start.28 = (bf16[50,1600]{1,0:T(8,128)(2,1)S(1)}, bf16[50,1600]{1,0:T(8,128)(2,1)S(1)}, u32[]{:S(2)}, u32[]{:S(2)}) collective-permute-start(bf16[50,1600]{1,0:T(8,128)(2,1)S(1)} %get-tuple-element.67.second), channel_id=1, source_target_pairs={{4,24},{5,25},{6,26},{7,27},{12,16},{13,17},{14,18},{15,19},{16,4}... | collective-permute-start | bytes 480008 | tf_op jit(solution)/shard_map/ppermute | solution.py:64
  88.1 17.7 %collective-permute-start.36 = (bf16[800,200]{1,0:T(8,128)(2,1)S(1)}, bf16[800,200]{1,0:T(8,128)(2,1)S(1)}, u32[]{:S(2)}, u32[]{:S(2)}) collective-permute-start(bf16[800,200]{1,0:T(8,128)(2,1)S(1)} %get-tuple-element.71.near.walkers), channel_id=1, source_target_pairs={{0,2},{1,3},{2,0},{3,1},{4,6},{5,7},{6,4},{7,5},{8,10},{9,11},{10,... | collective-permute-start | bytes 960008 | tf_op jit(solution)/shard_map/ppermute | solution.py:47
  98.9 6.8 %collective-permute-start.29 = (bf16[50,1600]{1,0:T(8,128)(2,1)S(1)}, bf16[50,1600]{1,0:T(8,128)(2,1)S(1)}, u32[]{:S(2)}, u32[]{:S(2)}) collective-permute-start(bf16[50,1600]{1,0:T(8,128)(2,1)S(1)} %get-tuple-element.69.low), channel_id=1, source_target_pairs={{0,32},{16,48},{32,0},{48,16},{64,96},{80,112},{96,64},{112,80},{1... | collective-permute-start | bytes 480008 | tf_op jit(solution)/shard_map/ppermute | solution.py:35
  100.3 9.2 %collective-permute-start.35 = (bf16[50,1600]{1,0:T(8,128)(2,1)S(1)}, bf16[50,1600]{1,0:T(8,128)(2,1)S(1)}, u32[]{:S(2)}, u32[]{:S(2)}) collective-permute-start(bf16[50,1600]{1,0:T(8,128)(2,1)S(1)} %get-tuple-element.70.b0), channel_id=1, source_target_pairs={{0,3},{1,0},{2,1},{3,2},{4,7},{5,4},{6,5},{7,6},{8,11},{9,8},{10,9... | collective-permute-start | bytes 480008 | tf_op jit(solution)/shard_map/ppermute | solution.py:43
  102.0 7.9 %collective-permute-start.34 = (bf16[50,1600]{1,0:T(8,128)(2,1)S(1)}, bf16[50,1600]{1,0:T(8,128)(2,1)S(1)}, u32[]{:S(2)}, u32[]{:S(2)}) collective-permute-start(bf16[50,1600]{1,0:T(8,128)(2,1)S(1)} %get-tuple-element.70.b0), channel_id=1, source_target_pairs={{0,2},{1,3},{2,0},{3,1},{4,6},{5,7},{6,4},{7,5},{8,10},{9,11},{10,... | collective-permute-start | bytes 480008 | tf_op jit(solution)/shard_map/ppermute | solution.py:43
  102.2 11.3 %collective-permute-start.33 = (bf16[50,1600]{1,0:T(8,128)(2,1)S(1)}, bf16[50,1600]{1,0:T(8,128)(2,1)S(1)}, u32[]{:S(2)}, u32[]{:S(2)}) collective-permute-start(bf16[50,1600]{1,0:T(8,128)(2,1)S(1)} %get-tuple-element.70.b0), channel_id=1, source_target_pairs={{0,1},{1,2},{2,3},{3,0},{4,5},{5,6},{6,7},{7,4},{8,9},{9,10},{10,1... | collective-permute-start | bytes 480008 | tf_op jit(solution)/shard_map/ppermute | solution.py:43
  113.6 20.3 %collective-permute-start.38 = (bf16[300,1600]{1,0:T(8,128)(2,1)S(1)}, bf16[300,1600]{1,0:T(8,128)(2,1)S(1)}, u32[]{:S(2)}, u32[]{:S(2)}) collective-permute-start(bf16[300,1600]{1,0:T(8,128)(2,1)S(1)} %get-tuple-element.73), channel_id=1, source_target_pairs={{0,16},{16,0},{32,48},{48,32},{64,80},{80,64},{96,112},{112,96},{1... | collective-permute-start | bytes 2880008 | tf_op jit(solution)/shard_map/ppermute | solution.py:39
  114.1 19.8 %collective-permute-start.37 = (bf16[200,1600]{1,0:T(8,128)(2,1)S(1)}, bf16[200,1600]{1,0:T(8,128)(2,1)S(1)}, u32[]{:S(2)}, u32[]{:S(2)}) collective-permute-start(bf16[200,1600]{1,0:T(8,128)(2,1)S(1)} %get-tuple-element.72.p4), channel_id=1, source_target_pairs={{0,32},{16,48},{32,0},{48,16},{64,96},{80,112},{96,64},{112,80},{1... | collective-permute-start | bytes 1920008 | tf_op jit(solution)/shard_map/ppermute | solution.py:35
  115.0 9.3 %collective-permute-start.32 = (bf16[100,1600]{1,0:T(8,128)(2,1)S(1)}, bf16[100,1600]{1,0:T(8,128)(2,1)S(1)}, u32[]{:S(2)}, u32[]{:S(2)}) collective-permute-start(bf16[100,1600]{1,0:T(8,128)(2,1)S(1)} %stack_low.1.pair.p0), channel_id=1, source_target_pairs={{0,3},{1,0},{2,1},{3,2},{4,7},{5,4},{6,5},{7,6},{8,11},{9,8},{10,9... | collective-permute-start | bytes 960008 | tf_op jit(solution)/shard_map/ppermute | solution.py:43
  115.0 10.5 %collective-permute-start.31 = (bf16[100,1600]{1,0:T(8,128)(2,1)S(1)}, bf16[100,1600]{1,0:T(8,128)(2,1)S(1)}, u32[]{:S(2)}, u32[]{:S(2)}) collective-permute-start(bf16[100,1600]{1,0:T(8,128)(2,1)S(1)} %stack_low.1.pair.p0), channel_id=1, source_target_pairs={{0,2},{1,3},{2,0},{3,1},{4,6},{5,7},{6,4},{7,5},{8,10},{9,11},{10,... | collective-permute-start | bytes 960008 | tf_op jit(solution)/shard_map/ppermute | solution.py:43
  115.7 18.2 %collective-permute-start.30 = (bf16[100,1600]{1,0:T(8,128)(2,1)S(1)}, bf16[100,1600]{1,0:T(8,128)(2,1)S(1)}, u32[]{:S(2)}, u32[]{:S(2)}) collective-permute-start(bf16[100,1600]{1,0:T(8,128)(2,1)S(1)} %stack_low.1.pair.p0), channel_id=1, source_target_pairs={{0,1},{1,2},{2,3},{3,0},{4,5},{5,6},{6,7},{7,4},{8,9},{9,10},{10,1... | collective-permute-start | bytes 960008 | tf_op jit(solution)/shard_map/ppermute | solution.py:43
  133.9 3.8 %collective-permute-start.42 = (bf16[200,1600]{1,0:T(8,128)(2,1)S(1)}, bf16[200,1600]{1,0:T(8,128)(2,1)S(1)}, u32[]{:S(2)}, u32[]{:S(2)}) collective-permute-start(bf16[200,1600]{1,0:T(8,128)(2,1)S(1)} %get-tuple-element.77.p5), channel_id=1, source_target_pairs={{0,16},{16,0},{32,48},{48,32},{64,80},{80,64},{96,112},{112,96},{1... | collective-permute-start | bytes 1920008 | tf_op jit(solution)/shard_map/ppermute | solution.py:39
  134.5 2.2 %collective-permute-start.39 = (bf16[100,1600]{1,0:T(8,128)(2,1)S(1)}, bf16[100,1600]{1,0:T(8,128)(2,1)S(1)}, u32[]{:S(2)}, u32[]{:S(2)}) collective-permute-start(bf16[100,1600]{1,0:T(8,128)(2,1)S(1)} %get-tuple-element.74.p1), channel_id=1, source_target_pairs={{0,16},{16,0},{32,48},{48,32},{64,80},{80,64},{96,112},{112,96},{1... | collective-permute-start | bytes 960008 | tf_op jit(solution)/shard_map/ppermute | solution.py:39
  134.6 2.6 %collective-permute-start.40 = (bf16[100,1600]{1,0:T(8,128)(2,1)S(1)}, bf16[100,1600]{1,0:T(8,128)(2,1)S(1)}, u32[]{:S(2)}, u32[]{:S(2)}) collective-permute-start(bf16[100,1600]{1,0:T(8,128)(2,1)S(1)} %get-tuple-element.75.p2), channel_id=1, source_target_pairs={{0,16},{16,0},{32,48},{48,32},{64,80},{80,64},{96,112},{112,96},{1... | collective-permute-start | bytes 960008 | tf_op jit(solution)/shard_map/ppermute | solution.py:39
  135.0 2.7 %collective-permute-start.41 = (bf16[100,1600]{1,0:T(8,128)(2,1)S(1)}, bf16[100,1600]{1,0:T(8,128)(2,1)S(1)}, u32[]{:S(2)}, u32[]{:S(2)}) collective-permute-start(bf16[100,1600]{1,0:T(8,128)(2,1)S(1)} %get-tuple-element.76.p3), channel_id=1, source_target_pairs={{0,16},{16,0},{32,48},{48,32},{64,80},{80,64},{96,112},{112,96},{1... | collective-permute-start | bytes 960008 | tf_op jit(solution)/shard_map/ppermute | solution.py:39
  155.5 8.8 %collective-permute-start.43 = (bf16[100,200]{1,0:T(8,128)(2,1)S(1)}, bf16[100,200]{1,0:T(8,128)(2,1)S(1)}, u32[]{:S(2)}, u32[]{:S(2)}) collective-permute-start(bf16[100,200]{1,0:T(8,128)(2,1)S(1)} %taylor.1), channel_id=1, source_target_pairs={{0,0},{1,1},{2,2},{3,3},{4,16},{5,17},{6,18},{7,19},{8,32},{9,33},... | collective-permute-start | bytes 120008 | tf_op jit(solution)/shard_map/ppermute | solution.py:64
where the time goes:
time: 165 us
  waiting for transfers between devices  76.1 us (46%)
  starting transfers between devices  58.5 us (35%)
  Pallas kernels  26 us (16%)
  local copies, waits for them, and re-layouts  3.55 us (2%)
    ppermute x9, waiting for transfers between devices, send_y(): lax.ppermute(array, 'pair', [(h * NY + y, h * NY + (y + step) % NY) for h...  26.9 us
    pallas_call x13, Pallas kernels, call(): pl.pallas_call(kernel, out_shape=outs, in_specs=specs, out_specs=[VMEM] *...  24.5 us
    ppermute x4, waiting for transfers between devices, everywhere(): return lax.ppermute(array, ('vec', 'pair'), pairs)  18 us
    ppermute x4, starting transfers between devices, everywhere(): return lax.ppermute(array, ('vec', 'pair'), pairs)  16 us
    ppermute x9, waiting for transfers between devices, send_x(): lax.ppermute(array, 'vec', [(vec_of(*p), vec_of(p[0] + step, p[1], p[2]))...  15.9 us
    ppermute x11, starting transfers between devices, swap_core(): lax.ppermute(array, 'vec', [(vec_of(*p), vec_of(p[0], p[1], 1 - p[2])) fo...  12.8 us
    ppermute x9, starting transfers between devices, send_x(): lax.ppermute(array, 'vec', [(vec_of(*p), vec_of(p[0] + step, p[1], p[2]))...  10.1 us
    ppermute x9, starting transfers between devices, send_y(): lax.ppermute(array, 'pair', [(h * NY + y, h * NY + (y + step) % NY) for h...  7.89 us
  transfers between devices with their start and end apart: 44, of which 26 were waited for; matrix products, arithmetic and copies ran while one was open for 0% of the time, Pallas kernels for 1%

commit v1 on v0

--- a/solution.py
+++ b/solution.py
@@ -93,17 +93,16 @@
     return [(start, min(GROUP, rows - start)) for start in range(0, rows, GROUP)]
 
 
-def rotate_kernel(walkers, inverse, out_ref, walkers_out):
+def rotate_kernel(walkers, inverse, out_ref):
     rows = walkers.shape[1]
     mine = walkers[...].astype(jnp.float32).T
-    walkers_out[...] = mine.astype(jnp.bfloat16)
     out_ref[...] = jnp.zeros_like(out_ref)
     out_ref[:rows, :] = jnp.dot(
         mine, inverse[...], precision=lax.Precision.HIGHEST, preferred_element_type=jnp.float32
     ).astype(jnp.bfloat16)
 
 
-def order_kernel(rotated, partner, trial, out_ref, trial_out):
+def order_kernel(rotated, partner, trial, after, out_ref, trial_out):
     at = position()
     trial_out[...] = trial[...]
     out_ref[at[0]] = rotated[...]
@@ -124,7 +123,7 @@
             out_ref[pl.ds(chip * NC + 1 - at[2], 1), :] = swapped[row : row + 1, :]
 
 
-def factor_kernel(trial, block, a1, a2, a3, a4, out_ref):
+def factor_kernel(trial, block, a1, a2, a3, out_ref):
     count, vectors, depth = block.shape
     product = lax.dot_general(
         block[...].reshape(count * vectors, depth), trial[...], NT, preferred_element_type=jnp.float32
@@ -134,7 +133,7 @@
 
 def bias_kernel(r0, r1, r2, r3, own, other, aux, walkers, passed, out_ref, aux_out, walkers_out, passed_out):
     aux_out[...] = aux[...]
-    walkers_out[...] = walkers[...]
+    walkers_out[...] = walkers[...].astype(jnp.float32).T.astype(walkers_out.dtype)
     rows, vectors, depth = own.shape
     parts = []
     for factor in (own, other):
@@ -307,44 +306,35 @@
     stack(out, low, high)
 
 
-def stack_y_kernel(b0, b1, b2, b3, pair, after, quad, both):
+def stack_y_kernel(b0, b1, b2, b3, after, quad):
     half = b0.shape[0]
-    both[: 2 * half, :] = pair[...]
     for step, ref in enumerate((b0, b1, b2, b3)):
         quad[step * half : (step + 1) * half, :] = ref[...]
-        both[(step + 2) * half : (step + 3) * half, :] = ref[...]
-
-
-def pass_kernel(*refs):
-    pass
-
-
-def place_rows(pieces, base, held, out):
-    low, _, _, _, y = position()
+
+
+def own_base():
+    _, _, core, high, _ = position()
+    return (high + ((high + core) & 1)) % NH
+
+
+def compact(held, out, last):
     half = held.shape[1]
-
-    def take(source, index):
-        ref, skip = pieces[source]
-        return ref[(skip + index) * half : (skip + index + 1) * half, :]
-
-    for step in range(NY):
-        row = (((base % NH) // 2) * NY + (y - step + NY) % NY) * NL
-        held[row + low] = take(step, 0)
-        held[row + 1 - low] = take(step, 1)
-        row = ((((base + 2) % NH) // 2) * NY + (y - step + NY) % NY) * NL
-        held[row + low] = take(4, step)
-        held[row + 1 - low] = take(5, step)
+    y = position()[4]
     for block in range(held.shape[0]):
         out[block * half : (block + 1) * half, :] = held[block]
-
-
-def assemble_kernel(p0, p1, p2, p3, p4, p5, near, far, own_rows, last_rows, start, held, total):
-    low, _, core, high, y = position()
-    place_rows([(ref, 0) for ref in (p0, p1, p2, p3, p4, p5)], high + ((high + core) & 1), held, own_rows)
+    for part in range(NL):
+        last[part * half : (part + 1) * half, :] = held[y * NL + part]
+
+
+def first_rows_kernel(p0, p1, p2, p3, near, far, out, last, start, held, total):
+    low, _, core, _, y = position()
     half = held.shape[1]
+    for step, ref in enumerate((p0, p1, p2, p3)):
+        row = ((y - step + NY) % NY) * NL
+        held[row + low] = ref[:half, :]
+        held[row + 1 - low] = ref[half:, :]
+    compact(held, out, last)
     rows = 2 * half
-    for part in range(NL):
-        last_rows[part * half : (part + 1) * half, :] = held[(low * NY + y) * NL + part]
     for step, ref in enumerate((near, far)):
         for index in range(2 * NL * NC):
             total[step, index // (NL * NC), index % (NL * NC)] = ref[index * rows : (index + 1) * rows, :]
@@ -354,12 +344,23 @@
         start[block * rows : (block + 1) * rows, :] = total[turn // 2, turn % 2, index]
 
 
-def taylor_kernel(own_rows, last_rows, start, mine, y1, y2, y3, quad, walkers, out_ref, held, other_rows, terms, total):
+def second_rows_kernel(mine, partner, after, out, last, held):
+    low, _, _, _, y = position()
+    half = held.shape[1]
+    for step in range(NY):
+        row = ((y - step + NY) % NY) * NL
+        held[row + low] = mine[step * half : (step + 1) * half, :]
+        held[row + 1 - low] = partner[step * half : (step + 1) * half, :]
+    compact(held, out, last)
+
+
+def taylor_kernel(rows0, rows1, other0, other1, last0, last1, start, walkers, out_ref, operator, terms, total):
     low, _, core, high, y = position()
-    base = high + ((high + core + 1) & 1)
-    place_rows([(mine, 0), (y1, 0), (y2, 0), (y3, 0), (mine, 2), (quad, 0)], base, held, other_rows)
-    rows = last_rows.shape[0]
-    stretch = NY * rows
+    base = own_base()
+    other = (high + ((high + core + 1) & 1)) % NH
+    stretch, rows = rows0.shape[0], last0.shape[0]
+    for place, ref in ((base, rows0), ((base + 2) % NH, rows1), (other, other0), ((other + 2) % NH, other1)):
+        operator[pl.ds(pl.multiple_of(place * stretch, 16), stretch), :] = ref[...]
     block_here = (low * NC + core) * NY + y
     terms[0] = start[...]
     total[...] = wide(walkers[:rows, :])
@@ -367,23 +368,20 @@
     @pl.loop(1, TAYLOR)
     def _(degree):
         source = (degree - 1) % 2
-        for side, ref in enumerate((own_rows, other_rows)):
-            product = jnp.dot(ref[...], terms[source], preferred_element_type=jnp.float32)
-            term = (product / degree.astype(jnp.float32)).astype(jnp.bfloat16)
-            for pair in range(NH // 2):
-                to = pl.multiple_of((2 * pair + (core ^ side)) * stretch, 16)
-                terms[1 - source, pl.ds(to, stretch), :] = term[pair * stretch : (pair + 1) * stretch, :]
+        product = jnp.dot(operator[...], terms[source], preferred_element_type=jnp.float32)
+        terms[1 - source] = (product / degree.astype(jnp.float32)).astype(jnp.bfloat16)
         for block in range(NH * NY):
 
             @pl.when(block_here == block)
             def _():
                 total[...] += wide(terms[1 - source, block * rows : (block + 1) * rows, :])
 
-    product = jnp.dot(last_rows[...], terms[(TAYLOR - 1) % 2], preferred_element_type=jnp.float32)
-    out_ref[...] = (total[...] + wide((product / TAYLOR).astype(jnp.bfloat16))).astype(out_ref.dtype)
-
-
-def call(kernel, outs, args, name, scratch=(), idle=0, limit=16):
+    last = jnp.where(base == low * NC + core, last0[...], last1[...])
+    product = jnp.dot(last, terms[(TAYLOR - 1) % 2], preferred_element_type=jnp.float32)
+    out_ref[...] = (total[...] + wide((product / TAYLOR).astype(jnp.bfloat16))).T.astype(out_ref.dtype)
+
+
+def call(kernel, outs, args, name, scratch=(), idle=0, limit=16, flops=None):
     specs = [VMEM] * (len(args) - idle) + [FAR] * idle
     return pl.pallas_call(
         kernel,
@@ -392,6 +390,7 @@
         out_specs=[VMEM] * len(outs) if isinstance(outs, (list, tuple)) else VMEM,
         scratch_shapes=list(scratch),
         compiler_params=pltpu.CompilerParams(vmem_limit_bytes=limit * 2**20),
+        cost_estimate=None if flops is None else pl.CostEstimate(flops=flops, bytes_accessed=0, transcendentals=0),
         name=name,
     )(*args)
 
@@ -404,9 +403,10 @@
     shaped = jax.ShapeDtypeStruct
     own = jnp.transpose(cholesky, (1, 0, 2))
     other = swap_core(own)
-    rotated, walker = call(
+    rows_here = exchange(walkers[0].T)
+    rotated = call(
         rotate_kernel,
-        [shaped((rows + -rows % GROUP, occupied), bf16), shaped((rows, occupied), bf16)],
+        shaped((rows + -rows % GROUP, occupied), bf16),
         (walkers[0].T, inv_correlation[0]),
         "rotate",
     )
@@ -414,17 +414,17 @@
     both, trial = call(
         order_kernel,
         [shaped((NL,) + rotated.shape, bf16), shaped((occupied, orbitals), bf16)],
-        (rotated, partner, trial_orbitals.T),
+        (rotated, partner, trial_orbitals.T, rows_here),
         "order",
-    )
-    rows_here = exchange(walker)
+        idle=1,
+    )
     met = [both] + [send_x(both, -step) for step in range(1, NX)]
     factor = call(
         factor_kernel,
         shaped((rows, vectors, occupied), bf16),
-        (trial, other, *met[1:], rows_here),
+        (trial, other, *met[1:]),
         "vector_factor",
-        idle=4,
+        idle=3,
     )
     bias, aux_here, rows_here, other = pl.pallas_call(
         bias_kernel,
@@ -484,42 +484,38 @@
     block0, block1 = call(choose_kernel, [piece] * 2, (second, got, more), "choose")
     pair0 = call(stack_kernel, two, (block0, swap_low(block0)), "stack_low")
     block1s = [block1] + [send_y(block1, step) for step in range(1, NY)]
-    quad1, mine = call(
-        stack_y_kernel, [quad, shaped((6 * half, orbitals), bf16)], (*block1s, pair0, far_rows), "stack_y", idle=1
-    )
-    mine = swap_core(mine)
-    arrived = [send_y(pair0, step) for step in range(1, NY)] + [swap_low(quad1)]
-    arrived = pl.pallas_call(
-        pass_kernel,
-        out_shape=[two] * 3 + [quad],
-        in_specs=[FAR] * 5,
-        out_specs=[FAR] * 4,
-        input_output_aliases={at: at for at in range(4)},
-        compiler_params=pltpu.CompilerParams(vmem_limit_bytes=4 * 2**20),
-        name="gathered",
-    )(*arrived, mine)
-    held = pltpu.VMEM((NH * NY, half, orbitals), bf16)
-    own_rows, last_rows, start = call(
-        assemble_kernel,
-        [shaped((orbitals // 2, orbitals), bf16), two, shaped((orbitals, occupied), bf16)],
-        (pair0, *arrived[:3], quad1, arrived[3], eight_rows, far_rows),
-        "assemble",
+    quad1 = call(stack_y_kernel, quad, (*block1s, far_rows), "stack_y", idle=1)
+    stretch = shaped((NY * rows, orbitals), bf16)
+    held = pltpu.VMEM((NY * NL, half, orbitals), bf16)
+    rows0, last0, start = call(
+        first_rows_kernel,
+        [stretch, two, shaped((orbitals, occupied), bf16)],
+        (pair0, *[send_y(pair0, step) for step in range(1, NY)], eight_rows, far_rows),
+        "first_rows",
         scratch=[held, pltpu.VMEM((2, 2, NL * NC, rows, occupied), bf16)],
+        flops=4 * 10**9,
+    )
+    rows1, last1 = call(
+        second_rows_kernel,
+        [stretch, two],
+        (quad1, swap_low(quad1), rows0),
+        "second_rows",
+        scratch=[held],
+        idle=1,
     )
     updated = call(
         taylor_kernel,
-        shaped((rows, occupied), bf16),
-        (own_rows, last_rows, start, mine, *[swap_core(a) for a in arrived], eight_rows),
+        shaped((occupied, rows), bf16),
+        (rows0, rows1, swap_core(rows0), swap_core(rows1), last0, last1, start, eight_rows),
         "taylor",
         scratch=[
-            held,
-            pltpu.VMEM((orbitals // 2, orbitals), bf16),
+            pltpu.VMEM((orbitals, orbitals), bf16),
             pltpu.VMEM((2, orbitals, occupied), bf16),
             pltpu.VMEM((rows, occupied), f32),
         ],
         limit=24,
     )
-    return (exchange(updated)[None], fields)
+    return (exchange(updated).T[None], fields)
 
 
 def solution(mesh):

time: 165 us -> 154 us (0.933)
  waiting for transfers between devices: 76.1 us -> 59.7 us
  starting transfers between devices: 58.5 us -> 71.9 us
  Pallas kernels: 26 us -> 17.8 us
    ppermute x9, waiting for transfers between devices: 26.9 us -> 17.4 us  [send_y(): lax.ppermute(array, 'pair', [(h * NY + y, h * NY + (y + step) % NY) for h...]
    pallas_call x13 -> x14, Pallas kernels: 24.5 us -> 16.2 us  [call(): pl.pallas_call(kernel, out_shape=outs, in_specs=specs, out_specs=[VMEM] *...]
    ppermute x6, starting transfers between devices: 6.67 us -> 11.9 us  [swap_low(): lax.ppermute(array, 'vec', [(vec_of(*p), vec_of(p[0], 1 - p[1], p[2])) fo...]
    ppermute x9, starting transfers between devices: 10.1 us -> 14.8 us  [send_x(): lax.ppermute(array, 'vec', [(vec_of(*p), vec_of(p[0] + step, p[1], p[2]))...]
    ppermute x6, waiting for transfers between devices: 6.58 us -> 2.7 us  [swap_low(): lax.ppermute(array, 'vec', [(vec_of(*p), vec_of(p[0], 1 - p[1], p[2])) fo...]
    ppermute x9, waiting for transfers between devices: 15.9 us -> 12.4 us  [send_x(): lax.ppermute(array, 'vec', [(vec_of(*p), vec_of(p[0] + step, p[1], p[2]))...]
    ppermute x9, starting transfers between devices: 7.89 us -> 10.9 us  [send_y(): lax.ppermute(array, 'pair', [(h * NY + y, h * NY + (y + step) % NY) for h...]
    ppermute x11 -> x8, waiting for transfers between devices: 4.22 us -> 5.02 us  [swap_core(): lax.ppermute(array, 'vec', [(vec_of(*p), vec_of(p[0], p[1], 1 - p[2])) fo...]
  transfers between devices with their start and end apart: 44 -> 41, of which waited for: 26 -> 23; matrix products, arithmetic and copies ran while one was open for 0% -> 0% of each run, Pallas kernels for 1% -> 1%
where the time goes in v1:
time: 154 us
  starting transfers between devices  71.9 us (47%)
  waiting for transfers between devices  59.7 us (39%)
  Pallas kernels  17.8 us (12%)
  local copies, waits for them, and re-layouts  3.45 us (2%)
    ppermute x4, waiting for transfers between devices, everywhere(): return lax.ppermute(array, ('vec', 'pair'), pairs)  17.6 us
    ppermute x9, waiting for transfers between devices, send_y(): lax.ppermute(array, 'pair', [(h * NY + y, h * NY + (y + step) % NY) for h...  17.4 us
    pallas_call x14, Pallas kernels, call(): pl.pallas_call(kernel, out_shape=outs, in_specs=specs, out_specs=[VMEM] *...  16.2 us
    ppermute x4, starting transfers between devices, everywhere(): return lax.ppermute(array, ('vec', 'pair'), pairs)  15.2 us
    ppermute x9, starting transfers between devices, send_x(): lax.ppermute(array, 'vec', [(vec_of(*p), vec_of(p[0] + step, p[1], p[2]))...  14.8 us
    ppermute x8, starting transfers between devices, swap_core(): lax.ppermute(array, 'vec', [(vec_of(*p), vec_of(p[0], p[1], 1 - p[2])) fo...  13.1 us
    ppermute x9, waiting for transfers between devices, send_x(): lax.ppermute(array, 'vec', [(vec_of(*p), vec_of(p[0] + step, p[1], p[2]))...  12.4 us
    ppermute x6, starting transfers between devices, swap_low(): lax.ppermute(array, 'vec', [(vec_of(*p), vec_of(p[0], 1 - p[1], p[2])) fo...  11.9 us
  transfers between devices with their start and end apart: 41, of which 23 were waited for; matrix products, arithmetic and copies ran while one was open for 0% of the time, Pallas kernels for 1%

profile of v1, /device:TPU:33, one launch (start us, length us, event | category | flops | bytes accessed | tf_op | source)
XLA Modules:
  0.0 153.6 jit_solution(15576768025237871440)
XLA Ops:
  0.6 0.8 collective-permute-start.5
  1.4 0.9 copy-done.1
  2.3 0.8 copy-done.2
  3.4 1.7 %collective-permute-start = (bf16[112,200]{1,0:T(8,128)(2,1)S(1)}, bf16[112,200]{1,0:T(8,128)(2,1)S(1)}, u32[]{:S(2)}, u32[]{:S(2)}) collective-permute-start(bf16[112,200]{1,0:T(8,128)(2,1)S(1)} %rotate.1.rotated), channel_id=1, source_target_pairs={{0,32},{16,48},{32,0},{48,16},{64,96},{80,112},{96,64},{112,80},{1... | collective-permute-start | bytes 134408 | tf_op jit(solution)/shard_map/ppermute | solution.py:35
  5.1 6.8 %collective-permute-start.1 = (bf16[200,100]{1,0:T(8,128)(2,1)}, bf16[200,100]{1,0:T(8,128)(2,1)S(1)}, u32[]{:S(2)}, u32[]{:S(2)}) collective-permute-start(bf16[200,100]{1,0:T(8,128)(2,1)} %bitcast.11), channel_id=1, source_target_pairs={{0,0},{1,1},{2,2},{3,3},{4,16},{5,17},{6,18},{7,19},{8,32},{9,33},... | collective-permute-start | bytes 120008 | tf_op jit(solution)/shard_map/ppermute | solution.py:64
  11.9 2.3 %collective-permute-done.1.after.walkers = bf16[200,100]{1,0:T(8,128)(2,1)S(1)} collective-permute-done((bf16[200,100]{1,0:T(8,128)(2,1)}, bf16[200,100]{1,0:T(8,128)(2,1)S(1)}, u32[]{:S(2)}, u32[]{:S(2)}) %collective-permute-start.1) | collective-permute-done | bytes 40032 | tf_op jit(solution)/shard_map/ppermute | solution.py:64
  14.2 1.1 copy-done
  15.4 1.3 collective-permute-start.4
  16.6 2.4 %collective-permute-start.3 = (bf16[2,112,200]{2,1,0:T(8,128)(2,1)S(1)}, bf16[2,112,200]{2,1,0:T(8,128)(2,1)S(1)}, u32[]{:S(2)}, u32[]{:S(2)}) collective-permute-start(bf16[2,112,200]{2,1,0:T(8,128)(2,1)S(1)} %get-tuple-element.36.r0), channel_id=1, source_target_pairs={{0,128},{16,144},{32,160},{48,176},{64,192},{80,208},{96,224},{112... | collective-permute-start | bytes 268808 | tf_op jit(solution)/shard_map/ppermute | solution.py:31
  19.1 1.2 collective-permute-start.2
  20.3 3.1 %collective-permute-done.3.a2.r2 = bf16[2,112,200]{2,1,0:T(8,128)(2,1)S(1)} collective-permute-done((bf16[2,112,200]{2,1,0:T(8,128)(2,1)S(1)}, bf16[2,112,200]{2,1,0:T(8,128)(2,1)S(1)}, u32[]{:S(2)}, u32[]{:S(2)}) %collective-permute-start.3) | collective-permute-done | bytes 89632 | tf_op jit(solution)/shard_map/ppermute | solution.py:31
  23.4 0.8 collective-permute-done.2.a1.r1
  24.3 1.7 %vector_factor.1.other = bf16[100,16,200]{2,1,0:T(8,128)(2,1)S(1)} custom-call(bf16[200,1600]{1,0:T(8,128)(2,1)S(1)} %get-tuple-element.37.trial, bf16[100,16,1600]{2,1,0:T(8,128)(2,1)S(1)} %collective-permute-done.5.block.passed, bf16[2,112,200]{2,1,0:T(8,128)(2,1)S(1)} %collective-permute-done.2.a1.r1, ...), custom_call_target="tpu_custom_call" | custom-call | tf_op jit(solution)/shard_map/vector_factor/pallas_call | solution.py:386
  26.0 1.6 %collective-permute-start.6 = (bf16[100,16,200]{2,1,0:T(8,128)(2,1)S(1)}, bf16[100,16,200]{2,1,0:T(8,128)(2,1)S(1)}, u32[]{:S(2)}, u32[]{:S(2)}) collective-permute-start(bf16[100,16,200]{2,1,0:T(8,128)(2,1)S(1)} %vector_factor.1.other), channel_id=1, source_target_pairs={{0,16},{16,0},{32,48},{48,32},{64,80},{80,64},{96,112},{112,96},{1... | collective-permute-start | bytes 1920008 | tf_op jit(solution)/shard_map/ppermute | solution.py:39
  27.5 2.0 %collective-permute-done.6.own = bf16[100,16,200]{2,1,0:T(8,128)(2,1)S(1)} collective-permute-done((bf16[100,16,200]{2,1,0:T(8,128)(2,1)S(1)}, bf16[100,16,200]{2,1,0:T(8,128)(2,1)S(1)}, u32[]{:S(2)}, u32[]{:S(2)}) %collective-permute-start.6) | collective-permute-done | bytes 640032 | tf_op jit(solution)/shard_map/ppermute | solution.py:39
  29.5 1.6 %force_bias.1 = (f32[8,32]{1,0:T(8,128)S(1)}, f32[16,16]{1,0:T(8,128)S(1)}, bf16[100,200]{1,0:T(8,128)(2,1)S(1)}, bf16[100,16,1600]{2,1,0:T(8,128)(2,1)S(1)}) custom-call(bf16[2,112,200]{2,1,0:T(8,128)(2,1)S(1)} %get-tuple-element.36.r0, bf16[2,112,200]{2,1,0:T(8,128)(2,1)S(1)} %collective-permute-done.2.a1.r1, ...), custom_call_target="tpu_custom_call", output_to_operand_aliasing={{3}: (8, {})} | custom-call | tf_op jit(solution)/shard_map/force_bias/pallas_call | solution.py:429
  31.1 0.5 collective-permute-start.15
  31.7 2.7 %collective-permute-start.9 = (f32[8,32]{1,0:T(8,128)S(1)}, f32[8,32]{1,0:T(8,128)S(1)}, u32[]{:S(2)}, u32[]{:S(2)}) collective-permute-start(f32[8,32]{1,0:T(8,128)S(1)} %get-tuple-element.38.b0), channel_id=1, source_target_pairs={{0,3},{1,0},{2,1},{3,2},{4,7},{5,4},{6,5},{7,6},{8,11},{9,8},{10,9... | collective-permute-start | bytes 3080 | tf_op jit(solution)/shard_map/ppermute | solution.py:43
  34.8 0.7 collective-permute-start.7
  35.5 1.2 collective-permute-start.13
  36.7 1.7 %collective-permute-done.8.b2 = f32[8,32]{1,0:T(8,128)S(1)} collective-permute-done((f32[8,32]{1,0:T(8,128)S(1)}, f32[8,32]{1,0:T(8,128)S(1)}, u32[]{:S(2)}, u32[]{:S(2)}) %collective-permute-start.8) | collective-permute-done | bytes 1056 | tf_op jit(solution)/shard_map/ppermute | solution.py:43
  38.4 0.7 collective-permute-start.12
  39.1 3.0 %collective-permute-start.11 = (f32[8,32]{1,0:T(8,128)S(1)}, f32[8,32]{1,0:T(8,128)S(1)}, u32[]{:S(2)}, u32[]{:S(2)}) collective-permute-start(f32[8,32]{1,0:T(8,128)S(1)} %sum_y.1.b0), channel_id=1, source_target_pairs={{0,8},{1,9},{2,10},{3,11},{4,12},{5,13},{6,14},{7,15},{8,0},{9,1},... | collective-permute-start | bytes 3080 | tf_op jit(solution)/shard_map/ppermute | solution.py:51
  42.2 3.4 %collective-permute-done.11.b2 = f32[8,32]{1,0:T(8,128)S(1)} collective-permute-done((f32[8,32]{1,0:T(8,128)S(1)}, f32[8,32]{1,0:T(8,128)S(1)}, u32[]{:S(2)}, u32[]{:S(2)}) %collective-permute-start.11) | collective-permute-done | bytes 1056 | tf_op jit(solution)/shard_map/ppermute | solution.py:51
  45.5 1.2 collective-permute-done.10.b1
  46.7 2.5 %field_operator.1 = (f32[8,32]{1,0:T(8,128)S(1)}, f32[8,16]{1,0:T(8,128)S(1)}, bf16[100,1600]{1,0:T(8,128)(2,1)S(1)}, bf16[100,1600]{1,0:T(8,128)(2,1)S(1)}, bf1...) custom-call(f32[8,32]{1,0:T(8,128)S(1)} %sum_y.1.b0, ...), custom_call_target="tpu_custom_call" | custom-call | tf_op jit(solution)/shard_map/field_operator/pallas_call | solution.py:386
  49.2 2.5 %collective-permute-start.20 = (bf16[224,1600]{1,0:T(8,128)(2,1)S(1)}, bf16[224,1600]{1,0:T(8,128)(2,1)S(1)}, u32[]{:S(2)}, u32[]{:S(2)}) collective-permute-start(bf16[224,1600]{1,0:T(8,128)(2,1)S(1)} %get-tuple-element.50), channel_id=1, source_target_pairs={{0,32},{16,48},{32,0},{48,16},{64,96},{80,112},{96,64},{112,80},{1... | collective-permute-start | bytes 2150408 | tf_op jit(solution)/shard_map/ppermute | solution.py:35
  51.8 1.1 collective-permute-start.16
  52.8 2.1 %collective-permute-start.17 = (bf16[100,1600]{1,0:T(8,128)(2,1)S(1)}, bf16[100,1600]{1,0:T(8,128)(2,1)S(1)}, u32[]{:S(2)}, u32[]{:S(2)}) collective-permute-start(bf16[100,1600]{1,0:T(8,128)(2,1)S(1)} %get-tuple-element.44), channel_id=1, source_target_pairs={{0,128},{16,144},{32,160},{48,176},{64,192},{80,208},{96,224},{112... | collective-permute-start | bytes 960008 | tf_op jit(solution)/shard_map/ppermute | solution.py:31
  54.9 1.3 collective-permute-start.18
  56.3 2.8 %collective-permute-done.16.p1 = bf16[100,1600]{1,0:T(8,128)(2,1)S(1)} collective-permute-done((bf16[100,1600]{1,0:T(8,128)(2,1)S(1)}, bf16[100,1600]{1,0:T(8,128)(2,1)S(1)}, u32[]{:S(2)}, u32[]{:S(2)}) %collective-permute-start.16) | collective-permute-done | bytes 320032 | tf_op jit(solution)/shard_map/ppermute | solution.py:31
  59.1 8.6 %collective-permute-start.21 = (f32[8,16]{1,0:T(8,128)S(1)}, f32[8,16]{1,0:T(8,128)S(1)}, u32[]{:S(2)}, u32[]{:S(2)}) collective-permute-start(f32[8,16]{1,0:T(8,128)S(1)} %get-tuple-element.52), channel_id=1, source_target_pairs={{0,16},{16,0},{32,48},{48,32},{64,80},{80,64},{96,112},{112,96},{1... | collective-permute-start | bytes 1544 | tf_op jit(solution)/shard_map/ppermute | solution.py:39
  67.7 0.6 collective-permute-done.18.p3
  68.4 0.5 collective-permute-start.19
  68.9 0.7 pair_sum.1
  69.6 3.1 %collective-permute-start.23 = (bf16[50,1600]{1,0:T(8,128)(2,1)S(1)}, bf16[50,1600]{1,0:T(8,128)(2,1)S(1)}, u32[]{:S(2)}, u32[]{:S(2)}) collective-permute-start(bf16[50,1600]{1,0:T(8,128)(2,1)S(1)} %get-tuple-element.55), channel_id=1, source_target_pairs={{0,64},{16,80},{32,96},{48,112},{64,128},{80,144},{96,160},{112,17... | collective-permute-start | bytes 480008 | tf_op jit(solution)/shard_map/ppermute | solution.py:31
  72.7 1.5 collective-permute-start.24
  74.2 0.9 collective-permute-start.25
  75.4 0.5 collective-permute-done.23.q1
  75.9 4.5 %collective-permute-done.24.q2 = bf16[50,1600]{1,0:T(8,128)(2,1)S(1)} collective-permute-done((bf16[50,1600]{1,0:T(8,128)(2,1)S(1)}, bf16[50,1600]{1,0:T(8,128)(2,1)S(1)}, u32[]{:S(2)}, u32[]{:S(2)}) %collective-permute-start.24) | collective-permute-done | bytes 160032 | tf_op jit(solution)/shard_map/ppermute | solution.py:31
  80.7 4.5 %collective-permute-start.27 = (bf16[50,1600]{1,0:T(8,128)(2,1)S(1)}, bf16[50,1600]{1,0:T(8,128)(2,1)S(1)}, u32[]{:S(2)}, u32[]{:S(2)}) collective-permute-start(bf16[50,1600]{1,0:T(8,128)(2,1)S(1)} %get-tuple-element.60), channel_id=1, source_target_pairs={{0,8},{1,9},{2,10},{3,11},{4,16},{5,17},{6,18},{7,19},{8,0},{9,1},... | collective-permute-start | bytes 480008 | tf_op jit(solution)/shard_map/ppermute | solution.py:64
  85.2 1.9 %collective-permute-start.28 = (bf16[50,1600]{1,0:T(8,128)(2,1)S(1)}, bf16[50,1600]{1,0:T(8,128)(2,1)S(1)}, u32[]{:S(2)}, u32[]{:S(2)}) collective-permute-start(bf16[50,1600]{1,0:T(8,128)(2,1)S(1)} %get-tuple-element.59.second), channel_id=1, source_target_pairs={{4,24},{5,25},{6,26},{7,27},{12,16},{13,17},{14,18},{15,19},{16,4}... | collective-permute-start | bytes 480008 | tf_op jit(solution)/shard_map/ppermute | solution.py:64
  87.2 2.0 %collective-permute-start.33 = (bf16[800,200]{1,0:T(8,128)(2,1)S(1)}, bf16[800,200]{1,0:T(8,128)(2,1)S(1)}, u32[]{:S(2)}, u32[]{:S(2)}) collective-permute-start(bf16[800,200]{1,0:T(8,128)(2,1)S(1)} %get-tuple-element.62.near.walkers), channel_id=1, source_target_pairs={{0,2},{1,3},{2,0},{3,1},{4,6},{5,7},{6,4},{7,5},{8,10},{9,11},{10,... | collective-permute-start | bytes 960008 | tf_op jit(solution)/shard_map/ppermute | solution.py:47
  89.2 1.9 %collective-permute-done.27.got = bf16[50,1600]{1,0:T(8,128)(2,1)S(1)} collective-permute-done((bf16[50,1600]{1,0:T(8,128)(2,1)S(1)}, bf16[50,1600]{1,0:T(8,128)(2,1)S(1)}, u32[]{:S(2)}, u32[]{:S(2)}) %collective-permute-start.27) | collective-permute-done | bytes 160032 | tf_op jit(solution)/shard_map/ppermute | solution.py:64
  91.1 6.5 %collective-permute-done.28.more = bf16[50,1600]{1,0:T(8,128)(2,1)S(1)} collective-permute-done((bf16[50,1600]{1,0:T(8,128)(2,1)S(1)}, bf16[50,1600]{1,0:T(8,128)(2,1)S(1)}, u32[]{:S(2)}, u32[]{:S(2)}) %collective-permute-start.28) | collective-permute-done | bytes 160032 | tf_op jit(solution)/shard_map/ppermute | solution.py:64
  97.7 2.1 %collective-permute-start.29 = (bf16[50,1600]{1,0:T(8,128)(2,1)S(1)}, bf16[50,1600]{1,0:T(8,128)(2,1)S(1)}, u32[]{:S(2)}, u32[]{:S(2)}) collective-permute-start(bf16[50,1600]{1,0:T(8,128)(2,1)S(1)} %get-tuple-element.61.low), channel_id=1, source_target_pairs={{0,32},{16,48},{32,0},{48,16},{64,96},{80,112},{96,64},{112,80},{1... | collective-permute-start | bytes 480008 | tf_op jit(solution)/shard_map/ppermute | solution.py:35
  99.8 2.9 %collective-permute-start.36 = (bf16[50,1600]{1,0:T(8,128)(2,1)S(1)}, bf16[50,1600]{1,0:T(8,128)(2,1)S(1)}, u32[]{:S(2)}, u32[]{:S(2)}) collective-permute-start(bf16[50,1600]{1,0:T(8,128)(2,1)S(1)} %get-tuple-element.64.b0), channel_id=1, source_target_pairs={{0,3},{1,0},{2,1},{3,2},{4,7},{5,4},{6,5},{7,6},{8,11},{9,8},{10,9... | collective-permute-start | bytes 480008 | tf_op jit(solution)/shard_map/ppermute | solution.py:43
  102.7 0.6 collective-permute-start.34
  103.3 0.4 collective-permute-done.29.high
  103.7 2.7 %collective-permute-start.32 = (bf16[100,1600]{1,0:T(8,128)(2,1)S(1)}, bf16[100,1600]{1,0:T(8,128)(2,1)S(1)}, u32[]{:S(2)}, u32[]{:S(2)}) collective-permute-start(bf16[100,1600]{1,0:T(8,128)(2,1)S(1)} %stack_low.1.p0), channel_id=1, source_target_pairs={{0,3},{1,0},{2,1},{3,2},{4,7},{5,4},{6,5},{7,6},{8,11},{9,8},{10,9... | collective-permute-start | bytes 960008 | tf_op jit(solution)/shard_map/ppermute | solution.py:43
  106.4 0.9 collective-permute-start.31
  107.3 3.6 %collective-permute-done.36.b3 = bf16[50,1600]{1,0:T(8,128)(2,1)S(1)} collective-permute-done((bf16[50,1600]{1,0:T(8,128)(2,1)S(1)}, bf16[50,1600]{1,0:T(8,128)(2,1)S(1)}, u32[]{:S(2)}, u32[]{:S(2)}) %collective-permute-start.36) | collective-permute-done | bytes 160032 | tf_op jit(solution)/shard_map/ppermute | solution.py:43
  110.8 4.2 %collective-permute-done.34.b1 = bf16[50,1600]{1,0:T(8,128)(2,1)S(1)} collective-permute-done((bf16[50,1600]{1,0:T(8,128)(2,1)S(1)}, bf16[50,1600]{1,0:T(8,128)(2,1)S(1)}, u32[]{:S(2)}, u32[]{:S(2)}) %collective-permute-start.34) | collective-permute-done | bytes 160032 | tf_op jit(solution)/shard_map/ppermute | solution.py:43
  115.1 5.0 %collective-permute-start.37 = (bf16[200,1600]{1,0:T(8,128)(2,1)S(1)}, bf16[200,1600]{1,0:T(8,128)(2,1)S(1)}, u32[]{:S(2)}, u32[]{:S(2)}) collective-permute-start(bf16[200,1600]{1,0:T(8,128)(2,1)S(1)} %stack_y.1.mine), channel_id=1, source_target_pairs={{0,32},{16,48},{32,0},{48,16},{64,96},{80,112},{96,64},{112,80},{1... | collective-permute-start | bytes 1920008 | tf_op jit(solution)/shard_map/ppermute | solution.py:35
  120.1 4.5 %collective-permute-done.32.p3 = bf16[100,1600]{1,0:T(8,128)(2,1)S(1)} collective-permute-done((bf16[100,1600]{1,0:T(8,128)(2,1)S(1)}, bf16[100,1600]{1,0:T(8,128)(2,1)S(1)}, u32[]{:S(2)}, u32[]{:S(2)}) %collective-permute-start.32) | collective-permute-done | bytes 320032 | tf_op jit(solution)/shard_map/ppermute | solution.py:43
  124.6 3.4 %collective-permute-done.30.p1 = bf16[100,1600]{1,0:T(8,128)(2,1)S(1)} collective-permute-done((bf16[100,1600]{1,0:T(8,128)(2,1)S(1)}, bf16[100,1600]{1,0:T(8,128)(2,1)S(1)}, u32[]{:S(2)}, u32[]{:S(2)}) %collective-permute-start.30) | collective-permute-done | bytes 320032 | tf_op jit(solution)/shard_map/ppermute | solution.py:43
  128.0 0.5 first_rows.1
  128.8 2.3 %collective-permute-done.37.partner = bf16[200,1600]{1,0:T(8,128)(2,1)S(1)} collective-permute-done((bf16[200,1600]{1,0:T(8,128)(2,1)S(1)}, bf16[200,1600]{1,0:T(8,128)(2,1)S(1)}, u32[]{:S(2)}, u32[]{:S(2)}) %collective-permute-start.37) | collective-permute-done | bytes 640032 | tf_op jit(solution)/shard_map/ppermute | solution.py:35
  131.1 0.4 second_rows.1
  131.7 3.0 %collective-permute-done.39.other1 = bf16[400,1600]{1,0:T(8,128)(2,1)S(1)} collective-permute-done((bf16[400,1600]{1,0:T(8,128)(2,1)S(1)}, bf16[400,1600]{1,0:T(8,128)(2,1)S(1)}, u32[]{:S(2)}, u32[]{:S(2)}) %collective-permute-start.39) | collective-permute-done | bytes 1280032 | tf_op jit(solution)/shard_map/ppermute | solution.py:39
  134.7 9.6 %taylor.1 = bf16[200,100]{1,0:T(8,128)(2,1)S(1)} custom-call(bf16[400,1600]{1,0:T(8,128)(2,1)S(1)} %get-tuple-element.63.after.rows0, bf16[400,1600]{1,0:T(8,128)(2,1)S(1)} %get-tuple-element.65.rows1, bf16[400,1600]{1,0:T(8,128)(2,1)S(1)} %collective-permute-done.38.other0, bf16[400,1600]{1,0:T(8,128)(2,1)S(1)} %collective-permute-done.39.other1, ...), custom_call_target="tpu_custom_call" | custom-call | tf_op jit(solution)/shard_map/taylor/pallas_call | solution.py:386
  144.3 1.9 %collective-permute-start.40 = (bf16[200,100]{1,0:T(8,128)(2,1)S(1)}, bf16[200,100]{1,0:T(8,128)(2,1)S(1)}, u32[]{:S(2)}, u32[]{:S(2)}) collective-permute-start(bf16[200,100]{1,0:T(8,128)(2,1)S(1)} %taylor.1), channel_id=1, source_target_pairs={{0,0},{1,1},{2,2},{3,3},{4,16},{5,17},{6,18},{7,19},{8,32},{9,33},... | collective-permute-start | bytes 120008 | tf_op jit(solution)/shard_map/ppermute | solution.py:64
  146.2 6.8 %collective-permute-done.40 = bf16[200,100]{1,0:T(8,128)(2,1)S(1)} collective-permute-done((bf16[200,100]{1,0:T(8,128)(2,1)S(1)}, bf16[200,100]{1,0:T(8,128)(2,1)S(1)}, u32[]{:S(2)}, u32[]{:S(2)}) %collective-permute-start.40) | collective-permute-done | bytes 40032 | tf_op jit(solution)/shard_map/ppermute | solution.py:64
  153.0 0.6 copy.10
  (42 shorter events, 2.4 us)
Async XLA Ops:
  0.6 23.6 %collective-permute-start.5 = (bf16[100,16,1600]{2,1,0:T(8,128)(2,1)}, bf16[100,16,1600]{2,1,0:T(8,128)(2,1)S(1)}, u32[]{:S(2)}, u32[]{:S(2)}) collective-permute-start(bf16[100,16,1600]{2,1,0:T(8,128)(2,1)} %bitcast.14), channel_id=1, source_target_pairs={{0,16},{16,0},{32,48},{48,32},{64,80},{80,64},{96,112},{112,96},{1... | collective-permute-start | bytes 15360008 | tf_op jit(solution)/shard_map/ppermute | solution.py:39
  1.4 0.9 copy-start.1
  2.3 0.8 copy-start.2
  3.1 26.4 %copy-start.3 = (f32[16,16]{1,0:T(8,128)S(1)}, f32[16,16]{1,0:T(8,128)}, u32[]{:S(2)}) copy-start(f32[16,16]{1,0:T(8,128)} %aux.3) | copy-start | bytes 3076
  3.4 10.8 %collective-permute-start = (bf16[112,200]{1,0:T(8,128)(2,1)S(1)}, bf16[112,200]{1,0:T(8,128)(2,1)S(1)}, u32[]{:S(2)}, u32[]{:S(2)}) collective-permute-start(bf16[112,200]{1,0:T(8,128)(2,1)S(1)} %rotate.1.rotated), channel_id=1, source_target_pairs={{0,32},{16,48},{32,0},{48,16},{64,96},{80,112},{96,64},{112,80},{1... | collective-permute-start | bytes 134408 | tf_op jit(solution)/shard_map/ppermute | solution.py:35
  5.1 9.1 %collective-permute-start.1 = (bf16[200,100]{1,0:T(8,128)(2,1)}, bf16[200,100]{1,0:T(8,128)(2,1)S(1)}, u32[]{:S(2)}, u32[]{:S(2)}) collective-permute-start(bf16[200,100]{1,0:T(8,128)(2,1)} %bitcast.11), channel_id=1, source_target_pairs={{0,0},{1,1},{2,2},{3,3},{4,16},{5,17},{6,18},{7,19},{8,32},{9,33},... | collective-permute-start | bytes 120008 | tf_op jit(solution)/shard_map/ppermute | solution.py:64
  14.2 1.1 copy-start
  15.4 4.9 %collective-permute-start.4 = (bf16[2,112,200]{2,1,0:T(8,128)(2,1)S(1)}, bf16[2,112,200]{2,1,0:T(8,128)(2,1)S(1)}, u32[]{:S(2)}, u32[]{:S(2)}) collective-permute-start(bf16[2,112,200]{2,1,0:T(8,128)(2,1)S(1)} %get-tuple-element.36.r0), channel_id=1, source_target_pairs={{0,64},{16,80},{32,96},{48,112},{64,128},{80,144},{96,160},{112,17... | collective-permute-start | bytes 268808 | tf_op jit(solution)/shard_map/ppermute | solution.py:31
  16.6 6.8 %collective-permute-start.3 = (bf16[2,112,200]{2,1,0:T(8,128)(2,1)S(1)}, bf16[2,112,200]{2,1,0:T(8,128)(2,1)S(1)}, u32[]{:S(2)}, u32[]{:S(2)}) collective-permute-start(bf16[2,112,200]{2,1,0:T(8,128)(2,1)S(1)} %get-tuple-element.36.r0), channel_id=1, source_target_pairs={{0,128},{16,144},{32,160},{48,176},{64,192},{80,208},{96,224},{112... | collective-permute-start | bytes 268808 | tf_op jit(solution)/shard_map/ppermute | solution.py:31
  19.1 5.2 %collective-permute-start.2 = (bf16[2,112,200]{2,1,0:T(8,128)(2,1)S(1)}, bf16[2,112,200]{2,1,0:T(8,128)(2,1)S(1)}, u32[]{:S(2)}, u32[]{:S(2)}) collective-permute-start(bf16[2,112,200]{2,1,0:T(8,128)(2,1)S(1)} %get-tuple-element.36.r0), channel_id=1, source_target_pairs={{0,192},{16,208},{32,224},{48,240},{64,0},{80,16},{96,32},{112,48}... | collective-permute-start | bytes 268808 | tf_op jit(solution)/shard_map/ppermute | solution.py:31
  26.0 3.5 %collective-permute-start.6 = (bf16[100,16,200]{2,1,0:T(8,128)(2,1)S(1)}, bf16[100,16,200]{2,1,0:T(8,128)(2,1)S(1)}, u32[]{:S(2)}, u32[]{:S(2)}) collective-permute-start(bf16[100,16,200]{2,1,0:T(8,128)(2,1)S(1)} %vector_factor.1.other), channel_id=1, source_target_pairs={{0,16},{16,0},{32,48},{48,32},{64,80},{80,64},{96,112},{112,96},{1... | collective-permute-start | bytes 1920008 | tf_op jit(solution)/shard_map/ppermute | solution.py:39
  31.1 15.7 %collective-permute-start.15 = (bf16[100,16,1600]{2,1,0:T(8,128)(2,1)S(1)}, bf16[100,16,1600]{2,1,0:T(8,128)(2,1)S(1)}, u32[]{:S(2)}, u32[]{:S(2)}) collective-permute-start(bf16[100,16,1600]{2,1,0:T(8,128)(2,1)S(1)} %get-tuple-element.41.other), channel_id=1, source_target_pairs={{0,16},{16,0},{32,48},{48,32},{64,80},{80,64},{96,112},{112,96},{1... | collective-permute-start | bytes 15360008 | tf_op jit(solution)/shard_map/ppermute | solution.py:39
  31.5 15.2 %collective-permute-start.14 = (bf16[100,200]{1,0:T(8,128)(2,1)S(1)}, bf16[100,200]{1,0:T(8,128)(2,1)S(1)}, u32[]{:S(2)}, u32[]{:S(2)}) collective-permute-start(bf16[100,200]{1,0:T(8,128)(2,1)S(1)} %get-tuple-element.40.walkers), channel_id=1, source_target_pairs={{0,16},{16,0},{32,48},{48,32},{64,80},{80,64},{96,112},{112,96},{1... | collective-permute-start | bytes 120008 | tf_op jit(solution)/shard_map/ppermute | solution.py:39
  31.7 3.8 %collective-permute-start.9 = (f32[8,32]{1,0:T(8,128)S(1)}, f32[8,32]{1,0:T(8,128)S(1)}, u32[]{:S(2)}, u32[]{:S(2)}) collective-permute-start(f32[8,32]{1,0:T(8,128)S(1)} %get-tuple-element.38.b0), channel_id=1, source_target_pairs={{0,3},{1,0},{2,1},{3,2},{4,7},{5,4},{6,5},{7,6},{8,11},{9,8},{10,9... | collective-permute-start | bytes 3080 | tf_op jit(solution)/shard_map/ppermute | solution.py:43
  34.4 4.0 %collective-permute-start.8 = (f32[8,32]{1,0:T(8,128)S(1)}, f32[8,32]{1,0:T(8,128)S(1)}, u32[]{:S(2)}, u32[]{:S(2)}) collective-permute-start(f32[8,32]{1,0:T(8,128)S(1)} %get-tuple-element.38.b0), channel_id=1, source_target_pairs={{0,2},{1,3},{2,0},{3,1},{4,6},{5,7},{6,4},{7,5},{8,10},{9,11},{10,... | collective-permute-start | bytes 3080 | tf_op jit(solution)/shard_map/ppermute | solution.py:43
  34.8 3.7 %collective-permute-start.7 = (f32[8,32]{1,0:T(8,128)S(1)}, f32[8,32]{1,0:T(8,128)S(1)}, u32[]{:S(2)}, u32[]{:S(2)}) collective-permute-start(f32[8,32]{1,0:T(8,128)S(1)} %get-tuple-element.38.b0), channel_id=1, source_target_pairs={{0,1},{1,2},{2,3},{3,0},{4,5},{5,6},{6,7},{7,4},{8,9},{9,10},{10,1... | collective-permute-start | bytes 3080 | tf_op jit(solution)/shard_map/ppermute | solution.py:43
  35.5 6.7 %collective-permute-start.13 = (f32[16,16]{1,0:T(8,128)S(1)}, f32[16,16]{1,0:T(8,128)S(1)}, u32[]{:S(2)}, u32[]{:S(2)}) collective-permute-start(f32[16,16]{1,0:T(8,128)S(1)} %get-tuple-element.39), channel_id=1, source_target_pairs={{0,16},{16,0},{32,48},{48,32},{64,80},{80,64},{96,112},{112,96},{1... | collective-permute-start | bytes 3080 | tf_op jit(solution)/shard_map/ppermute | solution.py:39
  38.4 3.7 %collective-permute-start.12 = (f32[8,32]{1,0:T(8,128)S(1)}, f32[8,32]{1,0:T(8,128)S(1)}, u32[]{:S(2)}, u32[]{:S(2)}) collective-permute-start(f32[8,32]{1,0:T(8,128)S(1)} %sum_y.1.b0), channel_id=1, source_target_pairs={{0,12},{1,13},{2,14},{3,15},{4,0},{5,1},{6,2},{7,3},{8,4},{9,5},{1... | collective-permute-start | bytes 3080 | tf_op jit(solution)/shard_map/ppermute | solution.py:51
  39.1 6.4 %collective-permute-start.11 = (f32[8,32]{1,0:T(8,128)S(1)}, f32[8,32]{1,0:T(8,128)S(1)}, u32[]{:S(2)}, u32[]{:S(2)}) collective-permute-start(f32[8,32]{1,0:T(8,128)S(1)} %sum_y.1.b0), channel_id=1, source_target_pairs={{0,8},{1,9},{2,10},{3,11},{4,12},{5,13},{6,14},{7,15},{8,0},{9,1},... | collective-permute-start | bytes 3080 | tf_op jit(solution)/shard_map/ppermute | solution.py:51
  42.1 4.6 %collective-permute-start.10 = (f32[8,32]{1,0:T(8,128)S(1)}, f32[8,32]{1,0:T(8,128)S(1)}, u32[]{:S(2)}, u32[]{:S(2)}) collective-permute-start(f32[8,32]{1,0:T(8,128)S(1)} %sum_y.1.b0), channel_id=1, source_target_pairs={{0,4},{1,5},{2,6},{3,7},{4,8},{5,9},{6,10},{7,11},{8,12},{9,13},{1... | collective-permute-start | bytes 3080 | tf_op jit(solution)/shard_map/ppermute | solution.py:51
  49.2 19.7 %collective-permute-start.20 = (bf16[224,1600]{1,0:T(8,128)(2,1)S(1)}, bf16[224,1600]{1,0:T(8,128)(2,1)S(1)}, u32[]{:S(2)}, u32[]{:S(2)}) collective-permute-start(bf16[224,1600]{1,0:T(8,128)(2,1)S(1)} %get-tuple-element.50), channel_id=1, source_target_pairs={{0,32},{16,48},{32,0},{48,16},{64,96},{80,112},{96,64},{112,80},{1... | collective-permute-start | bytes 2150408 | tf_op jit(solution)/shard_map/ppermute | solution.py:35
  51.8 7.3 %collective-permute-start.16 = (bf16[100,1600]{1,0:T(8,128)(2,1)S(1)}, bf16[100,1600]{1,0:T(8,128)(2,1)S(1)}, u32[]{:S(2)}, u32[]{:S(2)}) collective-permute-start(bf16[100,1600]{1,0:T(8,128)(2,1)S(1)} %get-tuple-element.43), channel_id=1, source_target_pairs={{0,64},{16,80},{32,96},{48,112},{64,128},{80,144},{96,160},{112,17... | collective-permute-start | bytes 960008 | tf_op jit(solution)/shard_map/ppermute | solution.py:31
  52.8 14.9 %collective-permute-start.17 = (bf16[100,1600]{1,0:T(8,128)(2,1)S(1)}, bf16[100,1600]{1,0:T(8,128)(2,1)S(1)}, u32[]{:S(2)}, u32[]{:S(2)}) collective-permute-start(bf16[100,1600]{1,0:T(8,128)(2,1)S(1)} %get-tuple-element.44), channel_id=1, source_target_pairs={{0,128},{16,144},{32,160},{48,176},{64,192},{80,208},{96,224},{112... | collective-permute-start | bytes 960008 | tf_op jit(solution)/shard_map/ppermute | solution.py:31
  54.9 13.4 %collective-permute-start.18 = (bf16[100,1600]{1,0:T(8,128)(2,1)S(1)}, bf16[100,1600]{1,0:T(8,128)(2,1)S(1)}, u32[]{:S(2)}, u32[]{:S(2)}) collective-permute-start(bf16[100,1600]{1,0:T(8,128)(2,1)S(1)} %get-tuple-element.45), channel_id=1, source_target_pairs={{0,192},{16,208},{32,224},{48,240},{64,0},{80,16},{96,32},{112,48}... | collective-permute-start | bytes 960008 | tf_op jit(solution)/shard_map/ppermute | solution.py:31
  56.2 12.7 %collective-permute-start.22 = (bf16[200,200]{1,0:T(8,128)(2,1)S(1)}, bf16[200,200]{1,0:T(8,128)(2,1)S(1)}, u32[]{:S(2)}, u32[]{:S(2)}) collective-permute-start(bf16[200,200]{1,0:T(8,128)(2,1)S(1)} %get-tuple-element.53.walkers), channel_id=1, source_target_pairs={{0,32},{16,48},{32,0},{48,16},{64,96},{80,112},{96,64},{112,80},{1... | collective-permute-start | bytes 240008 | tf_op jit(solution)/shard_map/ppermute | solution.py:35
  59.1 9.8 %collective-permute-start.21 = (f32[8,16]{1,0:T(8,128)S(1)}, f32[8,16]{1,0:T(8,128)S(1)}, u32[]{:S(2)}, u32[]{:S(2)}) collective-permute-start(f32[8,16]{1,0:T(8,128)S(1)} %get-tuple-element.52), channel_id=1, source_target_pairs={{0,16},{16,0},{32,48},{48,32},{64,80},{80,64},{96,112},{112,96},{1... | collective-permute-start | bytes 1544 | tf_op jit(solution)/shard_map/ppermute | solution.py:39
  68.4 7.0 %collective-permute-start.19 = (bf16[50,1600]{1,0:T(8,128)(2,1)S(1)}, bf16[50,1600]{1,0:T(8,128)(2,1)S(1)}, u32[]{:S(2)}, u32[]{:S(2)}) collective-permute-start(bf16[50,1600]{1,0:T(8,128)(2,1)S(1)} %x_sum.1), channel_id=1, source_target_pairs={{0,32},{16,48},{32,0},{48,16},{64,96},{80,112},{96,64},{112,80},{1... | collective-permute-start | bytes 480008 | tf_op jit(solution)/shard_map/ppermute | solution.py:35
  69.6 6.4 %collective-permute-start.23 = (bf16[50,1600]{1,0:T(8,128)(2,1)S(1)}, bf16[50,1600]{1,0:T(8,128)(2,1)S(1)}, u32[]{:S(2)}, u32[]{:S(2)}) collective-permute-start(bf16[50,1600]{1,0:T(8,128)(2,1)S(1)} %get-tuple-element.55), channel_id=1, source_target_pairs={{0,64},{16,80},{32,96},{48,112},{64,128},{80,144},{96,160},{112,17... | collective-permute-start | bytes 480008 | tf_op jit(solution)/shard_map/ppermute | solution.py:31
  72.7 7.7 %collective-permute-start.24 = (bf16[50,1600]{1,0:T(8,128)(2,1)S(1)}, bf16[50,1600]{1,0:T(8,128)(2,1)S(1)}, u32[]{:S(2)}, u32[]{:S(2)}) collective-permute-start(bf16[50,1600]{1,0:T(8,128)(2,1)S(1)} %get-tuple-element.56), channel_id=1, source_target_pairs={{0,128},{16,144},{32,160},{48,176},{64,192},{80,208},{96,224},{112... | collective-permute-start | bytes 480008 | tf_op jit(solution)/shard_map/ppermute | solution.py:31
  74.2 6.2 %collective-permute-start.25 = (bf16[50,1600]{1,0:T(8,128)(2,1)S(1)}, bf16[50,1600]{1,0:T(8,128)(2,1)S(1)}, u32[]{:S(2)}, u32[]{:S(2)}) collective-permute-start(bf16[50,1600]{1,0:T(8,128)(2,1)S(1)} %get-tuple-element.57), channel_id=1, source_target_pairs={{0,192},{16,208},{32,224},{48,240},{64,0},{80,16},{96,32},{112,48}... | collective-permute-start | bytes 480008 | tf_op jit(solution)/shard_map/ppermute | solution.py:31
  75.1 5.3 %collective-permute-start.26 = (bf16[400,200]{1,0:T(8,128)(2,1)S(1)}, bf16[400,200]{1,0:T(8,128)(2,1)S(1)}, u32[]{:S(2)}, u32[]{:S(2)}) collective-permute-start(bf16[400,200]{1,0:T(8,128)(2,1)S(1)} %get-tuple-element.58.walkers), channel_id=1, source_target_pairs={{0,1},{1,0},{2,3},{3,2},{4,5},{5,4},{6,7},{7,6},{8,9},{9,8},{10,11... | collective-permute-start | bytes 480008 | tf_op jit(solution)/shard_map/ppermute | solution.py:47
  80.7 10.4 %collective-permute-start.27 = (bf16[50,1600]{1,0:T(8,128)(2,1)S(1)}, bf16[50,1600]{1,0:T(8,128)(2,1)S(1)}, u32[]{:S(2)}, u32[]{:S(2)}) collective-permute-start(bf16[50,1600]{1,0:T(8,128)(2,1)S(1)} %get-tuple-element.60), channel_id=1, source_target_pairs={{0,8},{1,9},{2,10},{3,11},{4,16},{5,17},{6,18},{7,19},{8,0},{9,1},... | collective-permute-start | bytes 480008 | tf_op jit(solution)/shard_map/ppermute | solution.py:64
  85.2 12.4 %collective-permute-start.28 = (bf16[50,1600]{1,0:T(8,128)(2,1)S(1)}, bf16[50,1600]{1,0:T(8,128)(2,1)S(1)}, u32[]{:S(2)}, u32[]{:S(2)}) collective-permute-start(bf16[50,1600]{1,0:T(8,128)(2,1)S(1)} %get-tuple-element.59.second), channel_id=1, source_target_pairs={{4,24},{5,25},{6,26},{7,27},{12,16},{13,17},{14,18},{15,19},{16,4}... | collective-permute-start | bytes 480008 | tf_op jit(solution)/shard_map/ppermute | solution.py:64
  87.2 19.2 %collective-permute-start.33 = (bf16[800,200]{1,0:T(8,128)(2,1)S(1)}, bf16[800,200]{1,0:T(8,128)(2,1)S(1)}, u32[]{:S(2)}, u32[]{:S(2)}) collective-permute-start(bf16[800,200]{1,0:T(8,128)(2,1)S(1)} %get-tuple-element.62.near.walkers), channel_id=1, source_target_pairs={{0,2},{1,3},{2,0},{3,1},{4,6},{5,7},{6,4},{7,5},{8,10},{9,11},{10,... | collective-permute-start | bytes 960008 | tf_op jit(solution)/shard_map/ppermute | solution.py:47
  97.7 6.0 %collective-permute-start.29 = (bf16[50,1600]{1,0:T(8,128)(2,1)S(1)}, bf16[50,1600]{1,0:T(8,128)(2,1)S(1)}, u32[]{:S(2)}, u32[]{:S(2)}) collective-permute-start(bf16[50,1600]{1,0:T(8,128)(2,1)S(1)} %get-tuple-element.61.low), channel_id=1, source_target_pairs={{0,32},{16,48},{32,0},{48,16},{64,96},{80,112},{96,64},{112,80},{1... | collective-permute-start | bytes 480008 | tf_op jit(solution)/shard_map/ppermute | solution.py:35
  99.8 11.0 %collective-permute-start.36 = (bf16[50,1600]{1,0:T(8,128)(2,1)S(1)}, bf16[50,1600]{1,0:T(8,128)(2,1)S(1)}, u32[]{:S(2)}, u32[]{:S(2)}) collective-permute-start(bf16[50,1600]{1,0:T(8,128)(2,1)S(1)} %get-tuple-element.64.b0), channel_id=1, source_target_pairs={{0,3},{1,0},{2,1},{3,2},{4,7},{5,4},{6,5},{7,6},{8,11},{9,8},{10,9... | collective-permute-start | bytes 480008 | tf_op jit(solution)/shard_map/ppermute | solution.py:43
  102.7 8.1 %collective-permute-start.35 = (bf16[50,1600]{1,0:T(8,128)(2,1)S(1)}, bf16[50,1600]{1,0:T(8,128)(2,1)S(1)}, u32[]{:S(2)}, u32[]{:S(2)}) collective-permute-start(bf16[50,1600]{1,0:T(8,128)(2,1)S(1)} %get-tuple-element.64.b0), channel_id=1, source_target_pairs={{0,2},{1,3},{2,0},{3,1},{4,6},{5,7},{6,4},{7,5},{8,10},{9,11},{10,... | collective-permute-start | bytes 480008 | tf_op jit(solution)/shard_map/ppermute | solution.py:43
  102.7 12.3 %collective-permute-start.34 = (bf16[50,1600]{1,0:T(8,128)(2,1)S(1)}, bf16[50,1600]{1,0:T(8,128)(2,1)S(1)}, u32[]{:S(2)}, u32[]{:S(2)}) collective-permute-start(bf16[50,1600]{1,0:T(8,128)(2,1)S(1)} %get-tuple-element.64.b0), channel_id=1, source_target_pairs={{0,1},{1,2},{2,3},{3,0},{4,5},{5,6},{6,7},{7,4},{8,9},{9,10},{10,1... | collective-permute-start | bytes 480008 | tf_op jit(solution)/shard_map/ppermute | solution.py:43
  103.7 20.9 %collective-permute-start.32 = (bf16[100,1600]{1,0:T(8,128)(2,1)S(1)}, bf16[100,1600]{1,0:T(8,128)(2,1)S(1)}, u32[]{:S(2)}, u32[]{:S(2)}) collective-permute-start(bf16[100,1600]{1,0:T(8,128)(2,1)S(1)} %stack_low.1.p0), channel_id=1, source_target_pairs={{0,3},{1,0},{2,1},{3,2},{4,7},{5,4},{6,5},{7,6},{8,11},{9,8},{10,9... | collective-permute-start | bytes 960008 | tf_op jit(solution)/shard_map/ppermute | solution.py:43
  106.4 18.3 %collective-permute-start.31 = (bf16[100,1600]{1,0:T(8,128)(2,1)S(1)}, bf16[100,1600]{1,0:T(8,128)(2,1)S(1)}, u32[]{:S(2)}, u32[]{:S(2)}) collective-permute-start(bf16[100,1600]{1,0:T(8,128)(2,1)S(1)} %stack_low.1.p0), channel_id=1, source_target_pairs={{0,2},{1,3},{2,0},{3,1},{4,6},{5,7},{6,4},{7,5},{8,10},{9,11},{10,... | collective-permute-start | bytes 960008 | tf_op jit(solution)/shard_map/ppermute | solution.py:43
  110.8 17.2 %collective-permute-start.30 = (bf16[100,1600]{1,0:T(8,128)(2,1)S(1)}, bf16[100,1600]{1,0:T(8,128)(2,1)S(1)}, u32[]{:S(2)}, u32[]{:S(2)}) collective-permute-start(bf16[100,1600]{1,0:T(8,128)(2,1)S(1)} %stack_low.1.p0), channel_id=1, source_target_pairs={{0,1},{1,2},{2,3},{3,0},{4,5},{5,6},{6,7},{7,4},{8,9},{9,10},{10,1... | collective-permute-start | bytes 960008 | tf_op jit(solution)/shard_map/ppermute | solution.py:43
  115.1 16.1 %collective-permute-start.37 = (bf16[200,1600]{1,0:T(8,128)(2,1)S(1)}, bf16[200,1600]{1,0:T(8,128)(2,1)S(1)}, u32[]{:S(2)}, u32[]{:S(2)}) collective-permute-start(bf16[200,1600]{1,0:T(8,128)(2,1)S(1)} %stack_y.1.mine), channel_id=1, source_target_pairs={{0,32},{16,48},{32,0},{48,16},{64,96},{80,112},{96,64},{112,80},{1... | collective-permute-start | bytes 1920008 | tf_op jit(solution)/shard_map/ppermute | solution.py:35
  128.5 3.2 %collective-permute-start.38 = (bf16[400,1600]{1,0:T(8,128)(2,1)S(1)}, bf16[400,1600]{1,0:T(8,128)(2,1)S(1)}, u32[]{:S(2)}, u32[]{:S(2)}) collective-permute-start(bf16[400,1600]{1,0:T(8,128)(2,1)S(1)} %get-tuple-element.63.after.rows0), channel_id=1, source_target_pairs={{0,16},{16,0},{32,48},{48,32},{64,80},{80,64},{96,112},{112,96},{1... | collective-permute-start | bytes 3840008 | tf_op jit(solution)/shard_map/ppermute | solution.py:39
  131.5 3.2 %collective-permute-start.39 = (bf16[400,1600]{1,0:T(8,128)(2,1)S(1)}, bf16[400,1600]{1,0:T(8,128)(2,1)S(1)}, u32[]{:S(2)}, u32[]{:S(2)}) collective-permute-start(bf16[400,1600]{1,0:T(8,128)(2,1)S(1)} %get-tuple-element.65.rows1), channel_id=1, source_target_pairs={{0,16},{16,0},{32,48},{48,32},{64,80},{80,64},{96,112},{112,96},{1... | collective-permute-start | bytes 3840008 | tf_op jit(solution)/shard_map/ppermute | solution.py:39
  144.3 8.7 %collective-permute-start.40 = (bf16[200,100]{1,0:T(8,128)(2,1)S(1)}, bf16[200,100]{1,0:T(8,128)(2,1)S(1)}, u32[]{:S(2)}, u32[]{:S(2)}) collective-permute-start(bf16[200,100]{1,0:T(8,128)(2,1)S(1)} %taylor.1), channel_id=1, source_target_pairs={{0,0},{1,1},{2,2},{3,3},{4,16},{5,17},{6,18},{7,19},{8,32},{9,33},... | collective-permute-start | bytes 120008 | tf_op jit(solution)/shard_map/ppermute | solution.py:64

commit v2 on v1

--- a/solution.py
+++ b/solution.py
@@ -102,7 +102,7 @@
     ).astype(jnp.bfloat16)
 
 
-def order_kernel(rotated, partner, trial, after, out_ref, trial_out):
+def order_kernel(rotated, partner, trial, out_ref, trial_out):
     at = position()
     trial_out[...] = trial[...]
     out_ref[at[0]] = rotated[...]
@@ -131,9 +131,8 @@
     out_ref[...] = product.reshape(count, vectors, trial.shape[0])
 
 
-def bias_kernel(r0, r1, r2, r3, own, other, aux, walkers, passed, out_ref, aux_out, walkers_out, passed_out):
+def bias_kernel(r0, r1, r2, r3, own, other, aux, passed, out_ref, aux_out, passed_out):
     aux_out[...] = aux[...]
-    walkers_out[...] = walkers[...].astype(jnp.float32).T.astype(walkers_out.dtype)
     rows, vectors, depth = own.shape
     parts = []
     for factor in (own, other):
@@ -221,11 +220,11 @@
 
 
 def operator_kernel(
-    b0, b1, b2, b3, aux, aux_other, walkers, neighbours, own, other,
-    fields_ref, swap_ref, e0, e1, e2, e3, away_ref, o0, o1, o2, o3, two_rows, gathered,
+    b0, b1, b2, b3, aux, aux_other, walkers, own, other,
+    fields_ref, swap_ref, e0, e1, e2, e3, away_ref, o0, o1, o2, o3, walkers_out, gathered,
 ):
     at = position()
-    stack(two_rows, walkers, neighbours)
+    walkers_out[...] = walkers[...].astype(jnp.float32).T.astype(walkers_out.dtype)
     half = o0.shape[0]
     fields = fields_of((b0, b1, b2, b3), at, aux, aux_other, gathered)
     fields_ref[...] = fields
@@ -287,7 +286,7 @@
     second[...] = jnp.where(pick, odd, even).astype(second.dtype)
 
 
-def choose_kernel(second, got, more, block0, block1):
+def choose_kernel(second, got, more, after, block0, block1):
     at = position()
     active = (at[2] + at[3]) % 2 == 0
 
@@ -306,7 +305,8 @@
     stack(out, low, high)
 
 
-def stack_y_kernel(b0, b1, b2, b3, after, quad):
+def stack_y_kernel(b0, b1, b2, b3, near, far, quad, stacked):
+    stack(stacked, near, far)
     half = b0.shape[0]
     for step, ref in enumerate((b0, b1, b2, b3)):
         quad[step * half : (step + 1) * half, :] = ref[...]
@@ -326,7 +326,7 @@
         last[part * half : (part + 1) * half, :] = held[y * NL + part]
 
 
-def first_rows_kernel(p0, p1, p2, p3, near, far, out, last, start, held, total):
+def first_rows_kernel(p0, p1, p2, p3, walkers, swapped, out, last, start, held, total):
     low, _, core, _, y = position()
     half = held.shape[1]
     for step, ref in enumerate((p0, p1, p2, p3)):
@@ -335,13 +335,13 @@
         held[row + 1 - low] = ref[half:, :]
     compact(held, out, last)
     rows = 2 * half
-    for step, ref in enumerate((near, far)):
-        for index in range(2 * NL * NC):
-            total[step, index // (NL * NC), index % (NL * NC)] = ref[index * rows : (index + 1) * rows, :]
+    for step, ref in enumerate((walkers, swapped)):
+        for index in range(NY * NL):
+            total[step, index] = ref[index * rows : (index + 1) * rows, :]
     for block in range(NH * NY):
-        turn = y ^ (block % NY)
-        index = ((block // NY // NC) ^ low) * NC + ((block // NY % NC) ^ core)
-        start[block * rows : (block + 1) * rows, :] = total[turn // 2, turn % 2, index]
+        row, column = block // NY, block % NY
+        piece = total[(row % NC) ^ core, (y ^ column) * NL + ((row // NC) ^ low)]
+        start[block * rows : (block + 1) * rows, :] = piece
 
 
 def second_rows_kernel(mine, partner, after, out, last, held):
@@ -414,9 +414,8 @@
     both, trial = call(
         order_kernel,
         [shaped((NL,) + rotated.shape, bf16), shaped((occupied, orbitals), bf16)],
-        (rotated, partner, trial_orbitals.T, rows_here),
+        (rotated, partner, trial_orbitals.T),
         "order",
-        idle=1,
     )
     met = [both] + [send_x(both, -step) for step in range(1, NX)]
     factor = call(
@@ -426,20 +425,15 @@
         "vector_factor",
         idle=3,
     )
-    bias, aux_here, rows_here, other = pl.pallas_call(
+    bias, aux_here, other = pl.pallas_call(
         bias_kernel,
-        out_shape=[
-            shaped((8, 2 * vectors), f32),
-            shaped(aux_fields.shape, f32),
-            shaped((rows, occupied), bf16),
-            shaped(other.shape, bf16),
-        ],
-        in_specs=[VMEM] * 8 + [FAR],
-        out_specs=[VMEM] * 3 + [FAR],
-        input_output_aliases={8: 3},
+        out_shape=[shaped((8, 2 * vectors), f32), shaped(aux_fields.shape, f32), shaped(other.shape, bf16)],
+        in_specs=[VMEM] * 7 + [FAR],
+        out_specs=[VMEM] * 2 + [FAR],
+        input_output_aliases={7: 2},
         compiler_params=pltpu.CompilerParams(vmem_limit_bytes=16 * 2**20),
         name="force_bias",
-    )(*met, swap_core(factor), factor, aux_fields, rows_here, other)
+    )(*met, swap_core(factor), factor, aux_fields, other)
     near = swap_core(other)
     aux_other = swap_core(aux_here)
     from_y = [bias] + [send_y(bias, step) for step in range(1, NY)]
@@ -447,14 +441,14 @@
     from_h = [bias] + [send_h(bias, step) for step in range(1, NH)]
 
     piece, two, quad = [shaped((n * half, orbitals), bf16) for n in (1, 2, 4)]
-    shifted, shifted_other, *parts, two_rows = call(
+    shifted, shifted_other, *parts, rows_here = call(
         operator_kernel,
         [shaped((8, 2 * vectors), f32), shaped((8, vectors), f32)]
         + [two] * NX
         + [shaped((NX * PITCH, orbitals), bf16)]
         + [piece] * NX
-        + [shaped((NC * rows, occupied), bf16)],
-        (*from_h, aux_fields, aux_other, rows_here, swap_core(rows_here), near, other),
+        + [shaped((rows, occupied), bf16)],
+        (*from_h, aux_fields, aux_other, rows_here, near, other),
         "field_operator",
         scratch=[pltpu.VMEM((8, 2 * vectors), f32)],
     )
@@ -462,37 +456,42 @@
     shifted_other = swap_core(shifted_other)
     away = swap_low(away)
     even = [even[0]] + [send_x(even[step], step) for step in range(1, NX)]
-    low_rows = swap_low(two_rows)
+    low_rows = swap_low(rows_here)
     arrived = swap_low(call(x_sum_kernel, piece, tuple(even), "x_sum"))
-    *odd, fields, four_rows = call(
+    *odd, fields, two_rows = call(
         pair_sum_kernel,
-        [piece] * NX + [shaped(aux_fields.shape, f32), shaped((NL * NC * rows, occupied), bf16)],
-        (*odd, away, shifted, shifted_other, two_rows, low_rows),
+        [piece] * NX + [shaped(aux_fields.shape, f32), shaped((NL * rows, occupied), bf16)],
+        (*odd, away, shifted, shifted_other, rows_here, low_rows),
         "pair_sum",
     )
     odd = [odd[0]] + [send_x(odd[step], step) for step in range(1, NX)]
-    first, second, eight_rows = call(
+    first, second, four_rows = call(
         last_sum_kernel,
-        [piece] * 2 + [shaped((2 * NL * NC * rows, occupied), bf16)],
-        (*even, arrived, *odd, four_rows, flip_y(four_rows, 1)),
+        [piece] * 2 + [shaped((2 * NL * rows, occupied), bf16)],
+        (*even, arrived, *odd, two_rows, flip_y(two_rows, 1)),
         "last_sum",
     )
-    far_rows = flip_y(eight_rows, 2)
+    far_rows = flip_y(four_rows, 2)
 
     got = everywhere(first, first_target)
     more = everywhere(second, second_target)
-    block0, block1 = call(choose_kernel, [piece] * 2, (second, got, more), "choose")
+    block0, block1 = call(choose_kernel, [piece] * 2, (second, got, more, far_rows), "choose", idle=1)
     pair0 = call(stack_kernel, two, (block0, swap_low(block0)), "stack_low")
     block1s = [block1] + [send_y(block1, step) for step in range(1, NY)]
-    quad1 = call(stack_y_kernel, quad, (*block1s, far_rows), "stack_y", idle=1)
+    quad1, eight_rows = call(
+        stack_y_kernel,
+        [quad, shaped((4 * NL * rows, occupied), bf16)],
+        (*block1s, four_rows, far_rows),
+        "stack_y",
+    )
     stretch = shaped((NY * rows, orbitals), bf16)
     held = pltpu.VMEM((NY * NL, half, orbitals), bf16)
     rows0, last0, start = call(
         first_rows_kernel,
         [stretch, two, shaped((orbitals, occupied), bf16)],
-        (pair0, *[send_y(pair0, step) for step in range(1, NY)], eight_rows, far_rows),
+        (pair0, *[send_y(pair0, step) for step in range(1, NY)], eight_rows, swap_core(eight_rows)),
         "first_rows",
-        scratch=[held, pltpu.VMEM((2, 2, NL * NC, rows, occupied), bf16)],
+        scratch=[held, pltpu.VMEM((NC, NY * NL, rows, occupied), bf16)],
         flops=4 * 10**9,
     )
     rows1, last1 = call(

time: 154 us -> 153 us (level)
  starting transfers between devices: 71.9 us -> 63.4 us
  waiting for transfers between devices: 59.7 us -> 66.1 us
    ppermute x4, waiting for transfers between devices: 17.6 us -> 10.9 us  [everywhere(): return lax.ppermute(array, ('vec', 'pair'), pairs)]
    ppermute x6, starting transfers between devices: 11.9 us -> 7.2 us  [swap_low(): lax.ppermute(array, 'vec', [(vec_of(*p), vec_of(p[0], 1 - p[1], p[2])) fo...]
    ppermute x9, waiting for transfers between devices: 17.4 us -> 22 us  [send_y(): lax.ppermute(array, 'pair', [(h * NY + y, h * NY + (y + step) % NY) for h...]
    ppermute x2, waiting for transfers between devices: 0.01 us -> 3.8 us  [flip_y(): lax.ppermute(array, 'pair', [(h * NY + y, h * NY + (y ^ bit)) for h in ra...]
    ppermute x6, waiting for transfers between devices: 2.7 us -> 5.9 us  [swap_low(): lax.ppermute(array, 'vec', [(vec_of(*p), vec_of(p[0], 1 - p[1], p[2])) fo...]
    ppermute x9, starting transfers between devices: 10.9 us -> 8.28 us  [send_y(): lax.ppermute(array, 'pair', [(h * NY + y, h * NY + (y + step) % NY) for h...]
    ppermute x4, starting transfers between devices: 15.2 us -> 17.6 us  [everywhere(): return lax.ppermute(array, ('vec', 'pair'), pairs)]
    ppermute x8, starting transfers between devices: 13.1 us -> 11 us  [swap_core(): lax.ppermute(array, 'vec', [(vec_of(*p), vec_of(p[0], p[1], 1 - p[2])) fo...]
  transfers between devices with their start and end apart: 41 -> 41, of which waited for: 23 -> 24; matrix products, arithmetic and copies ran while one was open for 0% -> 0% of each run, Pallas kernels for 1% -> 1%
where the time goes in v2:
time: 153 us; the launch traced here: 152 us
  waiting for transfers between devices  66.1 us (43%)
  starting transfers between devices  63.4 us (41%)
  Pallas kernels  17.8 us (12%)
  local copies, waits for them, and re-layouts  3.45 us (2%)
    ppermute x9, waiting for transfers between devices, send_y(): lax.ppermute(array, 'pair', [(h * NY + y, h * NY + (y + step) % NY) for h...  22 us
    ppermute x4, starting transfers between devices, everywhere(): return lax.ppermute(array, ('vec', 'pair'), pairs)  17.6 us
    pallas_call x14, Pallas kernels, call(): pl.pallas_call(kernel, out_shape=outs, in_specs=specs, out_specs=[VMEM] *...  16.3 us
    ppermute x9, starting transfers between devices, send_x(): lax.ppermute(array, 'vec', [(vec_of(*p), vec_of(p[0] + step, p[1], p[2]))...  14.2 us
    ppermute x9, waiting for transfers between devices, send_x(): lax.ppermute(array, 'vec', [(vec_of(*p), vec_of(p[0] + step, p[1], p[2]))...  14.1 us
    ppermute x8, starting transfers between devices, swap_core(): lax.ppermute(array, 'vec', [(vec_of(*p), vec_of(p[0], p[1], 1 - p[2])) fo...  11 us
    ppermute x4, waiting for transfers between devices, everywhere(): return lax.ppermute(array, ('vec', 'pair'), pairs)  10.9 us
    ppermute x9, starting transfers between devices, send_y(): lax.ppermute(array, 'pair', [(h * NY + y, h * NY + (y + step) % NY) for h...  8.28 us
  transfers between devices with their start and end apart: 41, of which 24 were waited for; matrix products, arithmetic and copies ran while one was open for 0% of the time, Pallas kernels for 1%

profile of v2, /device:TPU:33, one launch (start us, length us, event | category | flops | bytes accessed | tf_op | source)
XLA Modules:
  0.0 151.6 jit_solution(12364191488954659801)
XLA Ops:
  0.6 0.8 collective-permute-start.4
  1.4 0.9 copy-done.1
  2.3 0.8 copy-done.2
  3.4 1.7 %collective-permute-start = (bf16[112,200]{1,0:T(8,128)(2,1)S(1)}, bf16[112,200]{1,0:T(8,128)(2,1)S(1)}, u32[]{:S(2)}, u32[]{:S(2)}) collective-permute-start(bf16[112,200]{1,0:T(8,128)(2,1)S(1)} %rotate.1.rotated), channel_id=1, source_target_pairs={{0,32},{16,48},{32,0},{48,16},{64,96},{80,112},{96,64},{112,80},{1... | collective-permute-start | bytes 134408 | tf_op jit(solution)/shard_map/ppermute | solution.py:35
  5.1 2.2 %collective-permute-done.partner = bf16[112,200]{1,0:T(8,128)(2,1)S(1)} collective-permute-done((bf16[112,200]{1,0:T(8,128)(2,1)S(1)}, bf16[112,200]{1,0:T(8,128)(2,1)S(1)}, u32[]{:S(2)}, u32[]{:S(2)}) %collective-permute-start) | collective-permute-done | bytes 44832 | tf_op jit(solution)/shard_map/ppermute | solution.py:35
  7.3 1.1 copy-done
  8.4 1.1 collective-permute-start.3
  9.5 2.5 %collective-permute-start.2 = (bf16[2,112,200]{2,1,0:T(8,128)(2,1)S(1)}, bf16[2,112,200]{2,1,0:T(8,128)(2,1)S(1)}, u32[]{:S(2)}, u32[]{:S(2)}) collective-permute-start(bf16[2,112,200]{2,1,0:T(8,128)(2,1)S(1)} %get-tuple-element.37.r0), channel_id=1, source_target_pairs={{0,128},{16,144},{32,160},{48,176},{64,192},{80,208},{96,224},{112... | collective-permute-start | bytes 268808 | tf_op jit(solution)/shard_map/ppermute | solution.py:31
  11.9 1.2 collective-permute-start.1
  13.1 0.6 collective-permute-done.3.a3.r3
  13.7 2.8 %collective-permute-done.2.a2.r2 = bf16[2,112,200]{2,1,0:T(8,128)(2,1)S(1)} collective-permute-done((bf16[2,112,200]{2,1,0:T(8,128)(2,1)S(1)}, bf16[2,112,200]{2,1,0:T(8,128)(2,1)S(1)}, u32[]{:S(2)}, u32[]{:S(2)}) %collective-permute-start.2) | collective-permute-done | bytes 89632 | tf_op jit(solution)/shard_map/ppermute | solution.py:31
  16.5 0.6 collective-permute-done.1.a1.r1
  17.1 1.7 %vector_factor.1.other = bf16[100,16,200]{2,1,0:T(8,128)(2,1)S(1)} custom-call(bf16[200,1600]{1,0:T(8,128)(2,1)S(1)} %get-tuple-element.38.trial, bf16[100,16,1600]{2,1,0:T(8,128)(2,1)S(1)} %collective-permute-done.4.block.passed, bf16[2,112,200]{2,1,0:T(8,128)(2,1)S(1)} %collective-permute-done.1.a1.r1, ...), custom_call_target="tpu_custom_call" | custom-call | tf_op jit(solution)/shard_map/vector_factor/pallas_call | solution.py:386
  18.8 1.5 collective-permute-start.5
  20.3 2.0 %collective-permute-done.5.own = bf16[100,16,200]{2,1,0:T(8,128)(2,1)S(1)} collective-permute-done((bf16[100,16,200]{2,1,0:T(8,128)(2,1)S(1)}, bf16[100,16,200]{2,1,0:T(8,128)(2,1)S(1)}, u32[]{:S(2)}, u32[]{:S(2)}) %collective-permute-start.5) | collective-permute-done | bytes 640032 | tf_op jit(solution)/shard_map/ppermute | solution.py:39
  22.3 1.5 force_bias.1
  24.2 7.5 %collective-permute-start.13 = (bf16[200,100]{1,0:T(8,128)(2,1)S(1)}, bf16[200,100]{1,0:T(8,128)(2,1)S(1)}, u32[]{:S(2)}, u32[]{:S(2)}) collective-permute-start(bf16[200,100]{1,0:T(8,128)(2,1)S(1)} %bitcast.12), channel_id=1, source_target_pairs={{0,0},{1,1},{2,2},{3,3},{4,16},{5,17},{6,18},{7,19},{8,32},{9,33},... | collective-permute-start | bytes 120008 | tf_op jit(solution)/shard_map/ppermute | solution.py:64
  31.7 2.8 %collective-permute-start.8 = (f32[8,32]{1,0:T(8,128)S(1)}, f32[8,32]{1,0:T(8,128)S(1)}, u32[]{:S(2)}, u32[]{:S(2)}) collective-permute-start(f32[8,32]{1,0:T(8,128)S(1)} %get-tuple-element.39.b0), channel_id=1, source_target_pairs={{0,3},{1,0},{2,1},{3,2},{4,7},{5,4},{6,5},{7,6},{8,11},{9,8},{10,9... | collective-permute-start | bytes 3080 | tf_op jit(solution)/shard_map/ppermute | solution.py:43
  34.8 0.7 collective-permute-start.6
  35.5 1.2 collective-permute-start.12
  36.8 1.7 %collective-permute-done.7.b2 = f32[8,32]{1,0:T(8,128)S(1)} collective-permute-done((f32[8,32]{1,0:T(8,128)S(1)}, f32[8,32]{1,0:T(8,128)S(1)}, u32[]{:S(2)}, u32[]{:S(2)}) %collective-permute-start.7) | collective-permute-done | bytes 1056 | tf_op jit(solution)/shard_map/ppermute | solution.py:43
  38.5 4.7 %collective-permute-start.10 = (f32[8,32]{1,0:T(8,128)S(1)}, f32[8,32]{1,0:T(8,128)S(1)}, u32[]{:S(2)}, u32[]{:S(2)}) collective-permute-start(f32[8,32]{1,0:T(8,128)S(1)} %sum_y.1.b0), channel_id=1, source_target_pairs={{0,8},{1,9},{2,10},{3,11},{4,12},{5,13},{6,14},{7,15},{8,0},{9,1},... | collective-permute-start | bytes 3080 | tf_op jit(solution)/shard_map/ppermute | solution.py:51
  43.3 1.7 %collective-permute-done.10.b2 = f32[8,32]{1,0:T(8,128)S(1)} collective-permute-done((f32[8,32]{1,0:T(8,128)S(1)}, f32[8,32]{1,0:T(8,128)S(1)}, u32[]{:S(2)}, u32[]{:S(2)}) %collective-permute-start.10) | collective-permute-done | bytes 1056 | tf_op jit(solution)/shard_map/ppermute | solution.py:51
  45.0 3.1 %collective-permute-done.9.b1 = f32[8,32]{1,0:T(8,128)S(1)} collective-permute-done((f32[8,32]{1,0:T(8,128)S(1)}, f32[8,32]{1,0:T(8,128)S(1)}, u32[]{:S(2)}, u32[]{:S(2)}) %collective-permute-start.9) | collective-permute-done | bytes 1056 | tf_op jit(solution)/shard_map/ppermute | solution.py:51
  48.1 2.5 %field_operator.1 = (f32[8,32]{1,0:T(8,128)S(1)}, f32[8,16]{1,0:T(8,128)S(1)}, bf16[100,1600]{1,0:T(8,128)(2,1)S(1)}, bf16[100,1600]{1,0:T(8,128)(2,1)S(1)}, bf1...) custom-call(f32[8,32]{1,0:T(8,128)S(1)} %sum_y.1.b0, ...), custom_call_target="tpu_custom_call" | custom-call | tf_op jit(solution)/shard_map/field_operator/pallas_call | solution.py:386
  50.7 1.1 collective-permute-start.15
  51.8 2.4 %collective-permute-start.16 = (bf16[100,1600]{1,0:T(8,128)(2,1)S(1)}, bf16[100,1600]{1,0:T(8,128)(2,1)S(1)}, u32[]{:S(2)}, u32[]{:S(2)}) collective-permute-start(bf16[100,1600]{1,0:T(8,128)(2,1)S(1)} %get-tuple-element.44), channel_id=1, source_target_pairs={{0,128},{16,144},{32,160},{48,176},{64,192},{80,208},{96,224},{112... | collective-permute-start | bytes 960008 | tf_op jit(solution)/shard_map/ppermute | solution.py:31
  54.2 1.0 collective-permute-start.17
  55.2 1.4 collective-permute-start.21
  56.6 2.7 %collective-permute-done.15.p1 = bf16[100,1600]{1,0:T(8,128)(2,1)S(1)} collective-permute-done((bf16[100,1600]{1,0:T(8,128)(2,1)S(1)}, bf16[100,1600]{1,0:T(8,128)(2,1)S(1)}, u32[]{:S(2)}, u32[]{:S(2)}) %collective-permute-start.15) | collective-permute-done | bytes 320032 | tf_op jit(solution)/shard_map/ppermute | solution.py:31
  59.2 5.3 %collective-permute-start.20 = (f32[8,16]{1,0:T(8,128)S(1)}, f32[8,16]{1,0:T(8,128)S(1)}, u32[]{:S(2)}, u32[]{:S(2)}) collective-permute-start(f32[8,16]{1,0:T(8,128)S(1)} %get-tuple-element.52), channel_id=1, source_target_pairs={{0,16},{16,0},{32,48},{48,32},{64,80},{80,64},{96,112},{112,96},{1... | collective-permute-start | bytes 1544 | tf_op jit(solution)/shard_map/ppermute | solution.py:39
  64.5 2.9 %collective-permute-done.16.p2 = bf16[100,1600]{1,0:T(8,128)(2,1)S(1)} collective-permute-done((bf16[100,1600]{1,0:T(8,128)(2,1)S(1)}, bf16[100,1600]{1,0:T(8,128)(2,1)S(1)}, u32[]{:S(2)}, u32[]{:S(2)}) %collective-permute-start.16) | collective-permute-done | bytes 320032 | tf_op jit(solution)/shard_map/ppermute | solution.py:31
  67.4 1.3 collective-permute-done.17.p3
  68.9 1.1 collective-permute-start.18
  70.1 0.7 pair_sum.1
  70.8 2.6 %collective-permute-start.22 = (bf16[50,1600]{1,0:T(8,128)(2,1)S(1)}, bf16[50,1600]{1,0:T(8,128)(2,1)S(1)}, u32[]{:S(2)}, u32[]{:S(2)}) collective-permute-start(bf16[50,1600]{1,0:T(8,128)(2,1)S(1)} %get-tuple-element.55), channel_id=1, source_target_pairs={{0,64},{16,80},{32,96},{48,112},{64,128},{80,144},{96,160},{112,17... | collective-permute-start | bytes 480008 | tf_op jit(solution)/shard_map/ppermute | solution.py:31
  73.4 2.0 %collective-permute-start.23 = (bf16[50,1600]{1,0:T(8,128)(2,1)S(1)}, bf16[50,1600]{1,0:T(8,128)(2,1)S(1)}, u32[]{:S(2)}, u32[]{:S(2)}) collective-permute-start(bf16[50,1600]{1,0:T(8,128)(2,1)S(1)} %get-tuple-element.56), channel_id=1, source_target_pairs={{0,128},{16,144},{32,160},{48,176},{64,192},{80,208},{96,224},{112... | collective-permute-start | bytes 480008 | tf_op jit(solution)/shard_map/ppermute | solution.py:31
  75.4 0.4 collective-permute-start.24
  75.8 3.8 %collective-permute-done.25.partners = bf16[200,200]{1,0:T(8,128)(2,1)S(1)} collective-permute-done((bf16[200,200]{1,0:T(8,128)(2,1)S(1)}, bf16[200,200]{1,0:T(8,128)(2,1)S(1)}, u32[]{:S(2)}, u32[]{:S(2)}) %collective-permute-start.25) | collective-permute-done | bytes 80032 | tf_op jit(solution)/shard_map/ppermute | solution.py:47
  79.6 3.2 %collective-permute-done.23.q2 = bf16[50,1600]{1,0:T(8,128)(2,1)S(1)} collective-permute-done((bf16[50,1600]{1,0:T(8,128)(2,1)S(1)}, bf16[50,1600]{1,0:T(8,128)(2,1)S(1)}, u32[]{:S(2)}, u32[]{:S(2)}) %collective-permute-start.23) | collective-permute-done | bytes 160032 | tf_op jit(solution)/shard_map/ppermute | solution.py:31
  83.1 0.7 collective-permute-start.26
  83.8 3.9 %collective-permute-start.27 = (bf16[50,1600]{1,0:T(8,128)(2,1)S(1)}, bf16[50,1600]{1,0:T(8,128)(2,1)S(1)}, u32[]{:S(2)}, u32[]{:S(2)}) collective-permute-start(bf16[50,1600]{1,0:T(8,128)(2,1)S(1)} %get-tuple-element.59.second), channel_id=1, source_target_pairs={{4,24},{5,25},{6,26},{7,27},{12,16},{13,17},{14,18},{15,19},{16,4}... | collective-permute-start | bytes 480008 | tf_op jit(solution)/shard_map/ppermute | solution.py:64
  88.0 1.2 collective-permute-done.26.got
  89.2 6.5 %collective-permute-done.27.more = bf16[50,1600]{1,0:T(8,128)(2,1)S(1)} collective-permute-done((bf16[50,1600]{1,0:T(8,128)(2,1)S(1)}, bf16[50,1600]{1,0:T(8,128)(2,1)S(1)}, u32[]{:S(2)}, u32[]{:S(2)}) %collective-permute-start.27) | collective-permute-done | bytes 160032 | tf_op jit(solution)/shard_map/ppermute | solution.py:64
  95.7 2.5 %collective-permute-start.29 = (bf16[50,1600]{1,0:T(8,128)(2,1)S(1)}, bf16[50,1600]{1,0:T(8,128)(2,1)S(1)}, u32[]{:S(2)}, u32[]{:S(2)}) collective-permute-start(bf16[50,1600]{1,0:T(8,128)(2,1)S(1)} %get-tuple-element.62.low), channel_id=1, source_target_pairs={{0,32},{16,48},{32,0},{48,16},{64,96},{80,112},{96,64},{112,80},{1... | collective-permute-start | bytes 480008 | tf_op jit(solution)/shard_map/ppermute | solution.py:35
  98.3 1.3 collective-permute-start.35
  99.6 1.0 collective-permute-start.34
  100.6 0.6 collective-permute-start.33
  101.1 2.1 %collective-permute-done.29.high = bf16[50,1600]{1,0:T(8,128)(2,1)S(1)} collective-permute-done((bf16[50,1600]{1,0:T(8,128)(2,1)S(1)}, bf16[50,1600]{1,0:T(8,128)(2,1)S(1)}, u32[]{:S(2)}, u32[]{:S(2)}) %collective-permute-start.29) | collective-permute-done | bytes 160032 | tf_op jit(solution)/shard_map/ppermute | solution.py:35
  103.3 1.5 %collective-permute-start.32 = (bf16[100,1600]{1,0:T(8,128)(2,1)S(1)}, bf16[100,1600]{1,0:T(8,128)(2,1)S(1)}, u32[]{:S(2)}, u32[]{:S(2)}) collective-permute-start(bf16[100,1600]{1,0:T(8,128)(2,1)S(1)} %stack_low.1.p0), channel_id=1, source_target_pairs={{0,3},{1,0},{2,1},{3,2},{4,7},{5,4},{6,5},{7,6},{8,11},{9,8},{10,9... | collective-permute-start | bytes 960008 | tf_op jit(solution)/shard_map/ppermute | solution.py:43
  104.8 2.8 %collective-permute-done.35.b3 = bf16[50,1600]{1,0:T(8,128)(2,1)S(1)} collective-permute-done((bf16[50,1600]{1,0:T(8,128)(2,1)S(1)}, bf16[50,1600]{1,0:T(8,128)(2,1)S(1)}, u32[]{:S(2)}, u32[]{:S(2)}) %collective-permute-start.35) | collective-permute-done | bytes 160032 | tf_op jit(solution)/shard_map/ppermute | solution.py:43
  107.7 4.1 %collective-permute-done.33.b1 = bf16[50,1600]{1,0:T(8,128)(2,1)S(1)} collective-permute-done((bf16[50,1600]{1,0:T(8,128)(2,1)S(1)}, bf16[50,1600]{1,0:T(8,128)(2,1)S(1)}, u32[]{:S(2)}, u32[]{:S(2)}) %collective-permute-start.33) | collective-permute-done | bytes 160032 | tf_op jit(solution)/shard_map/ppermute | solution.py:43
  112.0 0.4 collective-permute-start.37
  112.4 9.7 %collective-permute-done.32.p3 = bf16[100,1600]{1,0:T(8,128)(2,1)S(1)} collective-permute-done((bf16[100,1600]{1,0:T(8,128)(2,1)S(1)}, bf16[100,1600]{1,0:T(8,128)(2,1)S(1)}, u32[]{:S(2)}, u32[]{:S(2)}) %collective-permute-start.32) | collective-permute-done | bytes 320032 | tf_op jit(solution)/shard_map/ppermute | solution.py:43
  122.2 3.5 %collective-permute-done.30.p1 = bf16[100,1600]{1,0:T(8,128)(2,1)S(1)} collective-permute-done((bf16[100,1600]{1,0:T(8,128)(2,1)S(1)}, bf16[100,1600]{1,0:T(8,128)(2,1)S(1)}, u32[]{:S(2)}, u32[]{:S(2)}) %collective-permute-start.30) | collective-permute-done | bytes 320032 | tf_op jit(solution)/shard_map/ppermute | solution.py:43
  125.7 0.5 first_rows.1
  126.2 0.4 collective-permute-start.38
  126.6 1.6 %collective-permute-done.37.partner = bf16[200,1600]{1,0:T(8,128)(2,1)S(1)} collective-permute-done((bf16[200,1600]{1,0:T(8,128)(2,1)S(1)}, bf16[200,1600]{1,0:T(8,128)(2,1)S(1)}, u32[]{:S(2)}, u32[]{:S(2)}) %collective-permute-start.37) | collective-permute-done | bytes 640032 | tf_op jit(solution)/shard_map/ppermute | solution.py:35
  128.6 1.3 collective-permute-start.39
  130.0 2.7 %collective-permute-done.39.other1 = bf16[400,1600]{1,0:T(8,128)(2,1)S(1)} collective-permute-done((bf16[400,1600]{1,0:T(8,128)(2,1)S(1)}, bf16[400,1600]{1,0:T(8,128)(2,1)S(1)}, u32[]{:S(2)}, u32[]{:S(2)}) %collective-permute-start.39) | collective-permute-done | bytes 1280032 | tf_op jit(solution)/shard_map/ppermute | solution.py:39
  132.6 9.6 %taylor.1 = bf16[200,100]{1,0:T(8,128)(2,1)S(1)} custom-call(bf16[400,1600]{1,0:T(8,128)(2,1)S(1)} %get-tuple-element.65.after.rows0, bf16[400,1600]{1,0:T(8,128)(2,1)S(1)} %get-tuple-element.67.rows1, bf16[400,1600]{1,0:T(8,128)(2,1)S(1)} %collective-permute-done.38.other0, bf16[400,1600]{1,0:T(8,128)(2,1)S(1)} %collective-permute-done.39.other1, ...), custom_call_target="tpu_custom_call" | custom-call | tf_op jit(solution)/shard_map/taylor/pallas_call | solution.py:386
  142.2 5.5 %collective-permute-start.40 = (bf16[200,100]{1,0:T(8,128)(2,1)S(1)}, bf16[200,100]{1,0:T(8,128)(2,1)S(1)}, u32[]{:S(2)}, u32[]{:S(2)}) collective-permute-start(bf16[200,100]{1,0:T(8,128)(2,1)S(1)} %taylor.1), channel_id=1, source_target_pairs={{0,0},{1,1},{2,2},{3,3},{4,16},{5,17},{6,18},{7,19},{8,32},{9,33},... | collective-permute-start | bytes 120008 | tf_op jit(solution)/shard_map/ppermute | solution.py:64
  147.8 3.2 %collective-permute-done.40 = bf16[200,100]{1,0:T(8,128)(2,1)S(1)} collective-permute-done((bf16[200,100]{1,0:T(8,128)(2,1)S(1)}, bf16[200,100]{1,0:T(8,128)(2,1)S(1)}, u32[]{:S(2)}, u32[]{:S(2)}) %collective-permute-start.40) | collective-permute-done | bytes 40032 | tf_op jit(solution)/shard_map/ppermute | solution.py:64
  150.9 0.6 copy.10
  (44 shorter events, 2.7 us)
Async XLA Ops:
  0.6 16.5 %collective-permute-start.4 = (bf16[100,16,1600]{2,1,0:T(8,128)(2,1)}, bf16[100,16,1600]{2,1,0:T(8,128)(2,1)S(1)}, u32[]{:S(2)}, u32[]{:S(2)}) collective-permute-start(bf16[100,16,1600]{2,1,0:T(8,128)(2,1)} %bitcast.14), channel_id=1, source_target_pairs={{0,16},{16,0},{32,48},{48,32},{64,80},{80,64},{96,112},{112,96},{1... | collective-permute-start | bytes 15360008 | tf_op jit(solution)/shard_map/ppermute | solution.py:39
  1.4 0.9 copy-start.1
  2.3 0.8 copy-start.2
  3.1 19.1 %copy-start.4 = (f32[16,16]{1,0:T(8,128)S(1)}, f32[16,16]{1,0:T(8,128)}, u32[]{:S(2)}) copy-start(f32[16,16]{1,0:T(8,128)} %aux.3) | copy-start | bytes 3076
  3.4 3.9 %collective-permute-start = (bf16[112,200]{1,0:T(8,128)(2,1)S(1)}, bf16[112,200]{1,0:T(8,128)(2,1)S(1)}, u32[]{:S(2)}, u32[]{:S(2)}) collective-permute-start(bf16[112,200]{1,0:T(8,128)(2,1)S(1)} %rotate.1.rotated), channel_id=1, source_target_pairs={{0,32},{16,48},{32,0},{48,16},{64,96},{80,112},{96,64},{112,80},{1... | collective-permute-start | bytes 134408 | tf_op jit(solution)/shard_map/ppermute | solution.py:35
  7.3 1.1 copy-start
  8.4 5.3 %collective-permute-start.3 = (bf16[2,112,200]{2,1,0:T(8,128)(2,1)S(1)}, bf16[2,112,200]{2,1,0:T(8,128)(2,1)S(1)}, u32[]{:S(2)}, u32[]{:S(2)}) collective-permute-start(bf16[2,112,200]{2,1,0:T(8,128)(2,1)S(1)} %get-tuple-element.37.r0), channel_id=1, source_target_pairs={{0,64},{16,80},{32,96},{48,112},{64,128},{80,144},{96,160},{112,17... | collective-permute-start | bytes 268808 | tf_op jit(solution)/shard_map/ppermute | solution.py:31
  9.5 7.0 %collective-permute-start.2 = (bf16[2,112,200]{2,1,0:T(8,128)(2,1)S(1)}, bf16[2,112,200]{2,1,0:T(8,128)(2,1)S(1)}, u32[]{:S(2)}, u32[]{:S(2)}) collective-permute-start(bf16[2,112,200]{2,1,0:T(8,128)(2,1)S(1)} %get-tuple-element.37.r0), channel_id=1, source_target_pairs={{0,128},{16,144},{32,160},{48,176},{64,192},{80,208},{96,224},{112... | collective-permute-start | bytes 268808 | tf_op jit(solution)/shard_map/ppermute | solution.py:31
  11.9 5.2 %collective-permute-start.1 = (bf16[2,112,200]{2,1,0:T(8,128)(2,1)S(1)}, bf16[2,112,200]{2,1,0:T(8,128)(2,1)S(1)}, u32[]{:S(2)}, u32[]{:S(2)}) collective-permute-start(bf16[2,112,200]{2,1,0:T(8,128)(2,1)S(1)} %get-tuple-element.37.r0), channel_id=1, source_target_pairs={{0,192},{16,208},{32,224},{48,240},{64,0},{80,16},{96,32},{112,48}... | collective-permute-start | bytes 268808 | tf_op jit(solution)/shard_map/ppermute | solution.py:31
  18.8 5.4 %copy-start.3 = (bf16[1,100,200]{1,2,0:T(8,128)(2,1)S(1)}, bf16[1,100,200]{1,2,0:T(8,128)(2,1)}, u32[]{:S(2)}) copy-start(bf16[1,100,200]{1,2,0:T(8,128)(2,1)} %param.6) | copy-start | bytes 120004
  18.8 3.4 %collective-permute-start.5 = (bf16[100,16,200]{2,1,0:T(8,128)(2,1)S(1)}, bf16[100,16,200]{2,1,0:T(8,128)(2,1)S(1)}, u32[]{:S(2)}, u32[]{:S(2)}) collective-permute-start(bf16[100,16,200]{2,1,0:T(8,128)(2,1)S(1)} %vector_factor.1.other), channel_id=1, source_target_pairs={{0,16},{16,0},{32,48},{48,32},{64,80},{80,64},{96,112},{112,96},{1... | collective-permute-start | bytes 1920008 | tf_op jit(solution)/shard_map/ppermute | solution.py:39
  23.8 24.3 %collective-permute-start.14 = (bf16[100,16,1600]{2,1,0:T(8,128)(2,1)S(1)}, bf16[100,16,1600]{2,1,0:T(8,128)(2,1)S(1)}, u32[]{:S(2)}, u32[]{:S(2)}) collective-permute-start(bf16[100,16,1600]{2,1,0:T(8,128)(2,1)S(1)} %get-tuple-element.41.other), channel_id=1, source_target_pairs={{0,16},{16,0},{32,48},{48,32},{64,80},{80,64},{96,112},{112,96},{1... | collective-permute-start | bytes 15360008 | tf_op jit(solution)/shard_map/ppermute | solution.py:39
  24.2 19.1 %collective-permute-start.13 = (bf16[200,100]{1,0:T(8,128)(2,1)S(1)}, bf16[200,100]{1,0:T(8,128)(2,1)S(1)}, u32[]{:S(2)}, u32[]{:S(2)}) collective-permute-start(bf16[200,100]{1,0:T(8,128)(2,1)S(1)} %bitcast.12), channel_id=1, source_target_pairs={{0,0},{1,1},{2,2},{3,3},{4,16},{5,17},{6,18},{7,19},{8,32},{9,33},... | collective-permute-start | bytes 120008 | tf_op jit(solution)/shard_map/ppermute | solution.py:64
  31.7 3.9 %collective-permute-start.8 = (f32[8,32]{1,0:T(8,128)S(1)}, f32[8,32]{1,0:T(8,128)S(1)}, u32[]{:S(2)}, u32[]{:S(2)}) collective-permute-start(f32[8,32]{1,0:T(8,128)S(1)} %get-tuple-element.39.b0), channel_id=1, source_target_pairs={{0,3},{1,0},{2,1},{3,2},{4,7},{5,4},{6,5},{7,6},{8,11},{9,8},{10,9... | collective-permute-start | bytes 3080 | tf_op jit(solution)/shard_map/ppermute | solution.py:43
  34.5 4.0 %collective-permute-start.7 = (f32[8,32]{1,0:T(8,128)S(1)}, f32[8,32]{1,0:T(8,128)S(1)}, u32[]{:S(2)}, u32[]{:S(2)}) collective-permute-start(f32[8,32]{1,0:T(8,128)S(1)} %get-tuple-element.39.b0), channel_id=1, source_target_pairs={{0,2},{1,3},{2,0},{3,1},{4,6},{5,7},{6,4},{7,5},{8,10},{9,11},{10,... | collective-permute-start | bytes 3080 | tf_op jit(solution)/shard_map/ppermute | solution.py:43
  34.8 3.7 %collective-permute-start.6 = (f32[8,32]{1,0:T(8,128)S(1)}, f32[8,32]{1,0:T(8,128)S(1)}, u32[]{:S(2)}, u32[]{:S(2)}) collective-permute-start(f32[8,32]{1,0:T(8,128)S(1)} %get-tuple-element.39.b0), channel_id=1, source_target_pairs={{0,1},{1,2},{2,3},{3,0},{4,5},{5,6},{6,7},{7,4},{8,9},{9,10},{10,1... | collective-permute-start | bytes 3080 | tf_op jit(solution)/shard_map/ppermute | solution.py:43
  35.5 7.7 %collective-permute-start.12 = (f32[16,16]{1,0:T(8,128)S(1)}, f32[16,16]{1,0:T(8,128)S(1)}, u32[]{:S(2)}, u32[]{:S(2)}) collective-permute-start(f32[16,16]{1,0:T(8,128)S(1)} %get-tuple-element.40), channel_id=1, source_target_pairs={{0,16},{16,0},{32,48},{48,32},{64,80},{80,64},{96,112},{112,96},{1... | collective-permute-start | bytes 3080 | tf_op jit(solution)/shard_map/ppermute | solution.py:39
  38.5 4.8 %collective-permute-start.11 = (f32[8,32]{1,0:T(8,128)S(1)}, f32[8,32]{1,0:T(8,128)S(1)}, u32[]{:S(2)}, u32[]{:S(2)}) collective-permute-start(f32[8,32]{1,0:T(8,128)S(1)} %sum_y.1.b0), channel_id=1, source_target_pairs={{0,12},{1,13},{2,14},{3,15},{4,0},{5,1},{6,2},{7,3},{8,4},{9,5},{1... | collective-permute-start | bytes 3080 | tf_op jit(solution)/shard_map/ppermute | solution.py:51
  38.5 6.5 %collective-permute-start.10 = (f32[8,32]{1,0:T(8,128)S(1)}, f32[8,32]{1,0:T(8,128)S(1)}, u32[]{:S(2)}, u32[]{:S(2)}) collective-permute-start(f32[8,32]{1,0:T(8,128)S(1)} %sum_y.1.b0), channel_id=1, source_target_pairs={{0,8},{1,9},{2,10},{3,11},{4,12},{5,13},{6,14},{7,15},{8,0},{9,1},... | collective-permute-start | bytes 3080 | tf_op jit(solution)/shard_map/ppermute | solution.py:51
  43.3 4.9 %collective-permute-start.9 = (f32[8,32]{1,0:T(8,128)S(1)}, f32[8,32]{1,0:T(8,128)S(1)}, u32[]{:S(2)}, u32[]{:S(2)}) collective-permute-start(f32[8,32]{1,0:T(8,128)S(1)} %sum_y.1.b0), channel_id=1, source_target_pairs={{0,4},{1,5},{2,6},{3,7},{4,8},{5,9},{6,10},{7,11},{8,12},{9,13},{1... | collective-permute-start | bytes 3080 | tf_op jit(solution)/shard_map/ppermute | solution.py:51
  50.6 19.5 %collective-permute-start.19 = (bf16[224,1600]{1,0:T(8,128)(2,1)S(1)}, bf16[224,1600]{1,0:T(8,128)(2,1)S(1)}, u32[]{:S(2)}, u32[]{:S(2)}) collective-permute-start(bf16[224,1600]{1,0:T(8,128)(2,1)S(1)} %get-tuple-element.50), channel_id=1, source_target_pairs={{0,32},{16,48},{32,0},{48,16},{64,96},{80,112},{96,64},{112,80},{1... | collective-permute-start | bytes 2150408 | tf_op jit(solution)/shard_map/ppermute | solution.py:35
  50.7 8.6 %collective-permute-start.15 = (bf16[100,1600]{1,0:T(8,128)(2,1)S(1)}, bf16[100,1600]{1,0:T(8,128)(2,1)S(1)}, u32[]{:S(2)}, u32[]{:S(2)}) collective-permute-start(bf16[100,1600]{1,0:T(8,128)(2,1)S(1)} %get-tuple-element.43), channel_id=1, source_target_pairs={{0,64},{16,80},{32,96},{48,112},{64,128},{80,144},{96,160},{112,17... | collective-permute-start | bytes 960008 | tf_op jit(solution)/shard_map/ppermute | solution.py:31
  51.8 15.6 %collective-permute-start.16 = (bf16[100,1600]{1,0:T(8,128)(2,1)S(1)}, bf16[100,1600]{1,0:T(8,128)(2,1)S(1)}, u32[]{:S(2)}, u32[]{:S(2)}) collective-permute-start(bf16[100,1600]{1,0:T(8,128)(2,1)S(1)} %get-tuple-element.44), channel_id=1, source_target_pairs={{0,128},{16,144},{32,160},{48,176},{64,192},{80,208},{96,224},{112... | collective-permute-start | bytes 960008 | tf_op jit(solution)/shard_map/ppermute | solution.py:31
  54.2 14.6 %collective-permute-start.17 = (bf16[100,1600]{1,0:T(8,128)(2,1)S(1)}, bf16[100,1600]{1,0:T(8,128)(2,1)S(1)}, u32[]{:S(2)}, u32[]{:S(2)}) collective-permute-start(bf16[100,1600]{1,0:T(8,128)(2,1)S(1)} %get-tuple-element.45), channel_id=1, source_target_pairs={{0,192},{16,208},{32,224},{48,240},{64,0},{80,16},{96,32},{112,48}... | collective-permute-start | bytes 960008 | tf_op jit(solution)/shard_map/ppermute | solution.py:31
  55.2 14.8 %collective-permute-start.21 = (bf16[100,200]{1,0:T(8,128)(2,1)S(1)}, bf16[100,200]{1,0:T(8,128)(2,1)S(1)}, u32[]{:S(2)}, u32[]{:S(2)}) collective-permute-start(bf16[100,200]{1,0:T(8,128)(2,1)S(1)} %get-tuple-element.53.walkers), channel_id=1, source_target_pairs={{0,32},{16,48},{32,0},{48,16},{64,96},{80,112},{96,64},{112,80},{1... | collective-permute-start | bytes 120008 | tf_op jit(solution)/shard_map/ppermute | solution.py:35
  59.2 10.8 %collective-permute-start.20 = (f32[8,16]{1,0:T(8,128)S(1)}, f32[8,16]{1,0:T(8,128)S(1)}, u32[]{:S(2)}, u32[]{:S(2)}) collective-permute-start(f32[8,16]{1,0:T(8,128)S(1)} %get-tuple-element.52), channel_id=1, source_target_pairs={{0,16},{16,0},{32,48},{48,32},{64,80},{80,64},{96,112},{112,96},{1... | collective-permute-start | bytes 1544 | tf_op jit(solution)/shard_map/ppermute | solution.py:39
  68.9 6.9 %collective-permute-start.18 = (bf16[50,1600]{1,0:T(8,128)(2,1)S(1)}, bf16[50,1600]{1,0:T(8,128)(2,1)S(1)}, u32[]{:S(2)}, u32[]{:S(2)}) collective-permute-start(bf16[50,1600]{1,0:T(8,128)(2,1)S(1)} %x_sum.1), channel_id=1, source_target_pairs={{0,32},{16,48},{32,0},{48,16},{64,96},{80,112},{96,64},{112,80},{1... | collective-permute-start | bytes 480008 | tf_op jit(solution)/shard_map/ppermute | solution.py:35
  70.8 8.8 %collective-permute-start.22 = (bf16[50,1600]{1,0:T(8,128)(2,1)S(1)}, bf16[50,1600]{1,0:T(8,128)(2,1)S(1)}, u32[]{:S(2)}, u32[]{:S(2)}) collective-permute-start(bf16[50,1600]{1,0:T(8,128)(2,1)S(1)} %get-tuple-element.55), channel_id=1, source_target_pairs={{0,64},{16,80},{32,96},{48,112},{64,128},{80,144},{96,160},{112,17... | collective-permute-start | bytes 480008 | tf_op jit(solution)/shard_map/ppermute | solution.py:31
  73.4 9.4 %collective-permute-start.23 = (bf16[50,1600]{1,0:T(8,128)(2,1)S(1)}, bf16[50,1600]{1,0:T(8,128)(2,1)S(1)}, u32[]{:S(2)}, u32[]{:S(2)}) collective-permute-start(bf16[50,1600]{1,0:T(8,128)(2,1)S(1)} %get-tuple-element.56), channel_id=1, source_target_pairs={{0,128},{16,144},{32,160},{48,176},{64,192},{80,208},{96,224},{112... | collective-permute-start | bytes 480008 | tf_op jit(solution)/shard_map/ppermute | solution.py:31
  75.4 7.4 %collective-permute-start.24 = (bf16[50,1600]{1,0:T(8,128)(2,1)S(1)}, bf16[50,1600]{1,0:T(8,128)(2,1)S(1)}, u32[]{:S(2)}, u32[]{:S(2)}) collective-permute-start(bf16[50,1600]{1,0:T(8,128)(2,1)S(1)} %get-tuple-element.57), channel_id=1, source_target_pairs={{0,192},{16,208},{32,224},{48,240},{64,0},{80,16},{96,32},{112,48}... | collective-permute-start | bytes 480008 | tf_op jit(solution)/shard_map/ppermute | solution.py:31
  75.8 3.8 %collective-permute-start.25 = (bf16[200,200]{1,0:T(8,128)(2,1)S(1)}, bf16[200,200]{1,0:T(8,128)(2,1)S(1)}, u32[]{:S(2)}, u32[]{:S(2)}) collective-permute-start(bf16[200,200]{1,0:T(8,128)(2,1)S(1)} %get-tuple-element.58.walkers), channel_id=1, source_target_pairs={{0,1},{1,0},{2,3},{3,2},{4,5},{5,4},{6,7},{7,6},{8,9},{9,8},{10,11... | collective-permute-start | bytes 240008 | tf_op jit(solution)/shard_map/ppermute | solution.py:47
  83.1 6.1 %collective-permute-start.26 = (bf16[50,1600]{1,0:T(8,128)(2,1)S(1)}, bf16[50,1600]{1,0:T(8,128)(2,1)S(1)}, u32[]{:S(2)}, u32[]{:S(2)}) collective-permute-start(bf16[50,1600]{1,0:T(8,128)(2,1)S(1)} %get-tuple-element.60), channel_id=1, source_target_pairs={{0,8},{1,9},{2,10},{3,11},{4,16},{5,17},{6,18},{7,19},{8,0},{9,1},... | collective-permute-start | bytes 480008 | tf_op jit(solution)/shard_map/ppermute | solution.py:64
  83.8 11.9 %collective-permute-start.27 = (bf16[50,1600]{1,0:T(8,128)(2,1)S(1)}, bf16[50,1600]{1,0:T(8,128)(2,1)S(1)}, u32[]{:S(2)}, u32[]{:S(2)}) collective-permute-start(bf16[50,1600]{1,0:T(8,128)(2,1)S(1)} %get-tuple-element.59.second), channel_id=1, source_target_pairs={{4,24},{5,25},{6,26},{7,27},{12,16},{13,17},{14,18},{15,19},{16,4}... | collective-permute-start | bytes 480008 | tf_op jit(solution)/shard_map/ppermute | solution.py:64
  87.7 8.0 %collective-permute-start.28 = (bf16[400,200]{1,0:T(8,128)(2,1)S(1)}, bf16[400,200]{1,0:T(8,128)(2,1)S(1)}, u32[]{:S(2)}, u32[]{:S(2)}) collective-permute-start(bf16[400,200]{1,0:T(8,128)(2,1)S(1)} %get-tuple-element.61.near), channel_id=1, source_target_pairs={{0,2},{1,3},{2,0},{3,1},{4,6},{5,7},{6,4},{7,5},{8,10},{9,11},{10,... | collective-permute-start | bytes 480008 | tf_op jit(solution)/shard_map/ppermute | solution.py:47
  95.7 7.5 %collective-permute-start.29 = (bf16[50,1600]{1,0:T(8,128)(2,1)S(1)}, bf16[50,1600]{1,0:T(8,128)(2,1)S(1)}, u32[]{:S(2)}, u32[]{:S(2)}) collective-permute-start(bf16[50,1600]{1,0:T(8,128)(2,1)S(1)} %get-tuple-element.62.low), channel_id=1, source_target_pairs={{0,32},{16,48},{32,0},{48,16},{64,96},{80,112},{96,64},{112,80},{1... | collective-permute-start | bytes 480008 | tf_op jit(solution)/shard_map/ppermute | solution.py:35
  98.3 9.4 %collective-permute-start.35 = (bf16[50,1600]{1,0:T(8,128)(2,1)S(1)}, bf16[50,1600]{1,0:T(8,128)(2,1)S(1)}, u32[]{:S(2)}, u32[]{:S(2)}) collective-permute-start(bf16[50,1600]{1,0:T(8,128)(2,1)S(1)} %get-tuple-element.63.b0), channel_id=1, source_target_pairs={{0,3},{1,0},{2,1},{3,2},{4,7},{5,4},{6,5},{7,6},{8,11},{9,8},{10,9... | collective-permute-start | bytes 480008 | tf_op jit(solution)/shard_map/ppermute | solution.py:43
  99.6 8.1 %collective-permute-start.34 = (bf16[50,1600]{1,0:T(8,128)(2,1)S(1)}, bf16[50,1600]{1,0:T(8,128)(2,1)S(1)}, u32[]{:S(2)}, u32[]{:S(2)}) collective-permute-start(bf16[50,1600]{1,0:T(8,128)(2,1)S(1)} %get-tuple-element.63.b0), channel_id=1, source_target_pairs={{0,2},{1,3},{2,0},{3,1},{4,6},{5,7},{6,4},{7,5},{8,10},{9,11},{10,... | collective-permute-start | bytes 480008 | tf_op jit(solution)/shard_map/ppermute | solution.py:43
  100.6 11.2 %collective-permute-start.33 = (bf16[50,1600]{1,0:T(8,128)(2,1)S(1)}, bf16[50,1600]{1,0:T(8,128)(2,1)S(1)}, u32[]{:S(2)}, u32[]{:S(2)}) collective-permute-start(bf16[50,1600]{1,0:T(8,128)(2,1)S(1)} %get-tuple-element.63.b0), channel_id=1, source_target_pairs={{0,1},{1,2},{2,3},{3,0},{4,5},{5,6},{6,7},{7,4},{8,9},{9,10},{10,1... | collective-permute-start | bytes 480008 | tf_op jit(solution)/shard_map/ppermute | solution.py:43
  103.3 18.9 %collective-permute-start.32 = (bf16[100,1600]{1,0:T(8,128)(2,1)S(1)}, bf16[100,1600]{1,0:T(8,128)(2,1)S(1)}, u32[]{:S(2)}, u32[]{:S(2)}) collective-permute-start(bf16[100,1600]{1,0:T(8,128)(2,1)S(1)} %stack_low.1.p0), channel_id=1, source_target_pairs={{0,3},{1,0},{2,1},{3,2},{4,7},{5,4},{6,5},{7,6},{8,11},{9,8},{10,9... | collective-permute-start | bytes 960008 | tf_op jit(solution)/shard_map/ppermute | solution.py:43
  104.8 17.3 %collective-permute-start.31 = (bf16[100,1600]{1,0:T(8,128)(2,1)S(1)}, bf16[100,1600]{1,0:T(8,128)(2,1)S(1)}, u32[]{:S(2)}, u32[]{:S(2)}) collective-permute-start(bf16[100,1600]{1,0:T(8,128)(2,1)S(1)} %stack_low.1.p0), channel_id=1, source_target_pairs={{0,2},{1,3},{2,0},{3,1},{4,6},{5,7},{6,4},{7,5},{8,10},{9,11},{10,... | collective-permute-start | bytes 960008 | tf_op jit(solution)/shard_map/ppermute | solution.py:43
  107.7 18.0 %collective-permute-start.30 = (bf16[100,1600]{1,0:T(8,128)(2,1)S(1)}, bf16[100,1600]{1,0:T(8,128)(2,1)S(1)}, u32[]{:S(2)}, u32[]{:S(2)}) collective-permute-start(bf16[100,1600]{1,0:T(8,128)(2,1)S(1)} %stack_low.1.p0), channel_id=1, source_target_pairs={{0,1},{1,2},{2,3},{3,0},{4,5},{5,6},{6,7},{7,4},{8,9},{9,10},{10,1... | collective-permute-start | bytes 960008 | tf_op jit(solution)/shard_map/ppermute | solution.py:43
  111.9 13.8 %collective-permute-start.36 = (bf16[800,200]{1,0:T(8,128)(2,1)S(1)}, bf16[800,200]{1,0:T(8,128)(2,1)S(1)}, u32[]{:S(2)}, u32[]{:S(2)}) collective-permute-start(bf16[800,200]{1,0:T(8,128)(2,1)S(1)} %get-tuple-element.64.walkers), channel_id=1, source_target_pairs={{0,16},{16,0},{32,48},{48,32},{64,80},{80,64},{96,112},{112,96},{1... | collective-permute-start | bytes 960008 | tf_op jit(solution)/shard_map/ppermute | solution.py:39
  112.0 16.2 %collective-permute-start.37 = (bf16[200,1600]{1,0:T(8,128)(2,1)S(1)}, bf16[200,1600]{1,0:T(8,128)(2,1)S(1)}, u32[]{:S(2)}, u32[]{:S(2)}) collective-permute-start(bf16[200,1600]{1,0:T(8,128)(2,1)S(1)} %get-tuple-element.66.mine), channel_id=1, source_target_pairs={{0,32},{16,48},{32,0},{48,16},{64,96},{80,112},{96,64},{112,80},{1... | collective-permute-start | bytes 1920008 | tf_op jit(solution)/shard_map/ppermute | solution.py:35
  126.2 3.7 %collective-permute-start.38 = (bf16[400,1600]{1,0:T(8,128)(2,1)S(1)}, bf16[400,1600]{1,0:T(8,128)(2,1)S(1)}, u32[]{:S(2)}, u32[]{:S(2)}) collective-permute-start(bf16[400,1600]{1,0:T(8,128)(2,1)S(1)} %get-tuple-element.65.after.rows0), channel_id=1, source_target_pairs={{0,16},{16,0},{32,48},{48,32},{64,80},{80,64},{96,112},{112,96},{1... | collective-permute-start | bytes 3840008 | tf_op jit(solution)/shard_map/ppermute | solution.py:39
  128.6 4.0 %collective-permute-start.39 = (bf16[400,1600]{1,0:T(8,128)(2,1)S(1)}, bf16[400,1600]{1,0:T(8,128)(2,1)S(1)}, u32[]{:S(2)}, u32[]{:S(2)}) collective-permute-start(bf16[400,1600]{1,0:T(8,128)(2,1)S(1)} %get-tuple-element.67.rows1), channel_id=1, source_target_pairs={{0,16},{16,0},{32,48},{48,32},{64,80},{80,64},{96,112},{112,96},{1... | collective-permute-start | bytes 3840008 | tf_op jit(solution)/shard_map/ppermute | solution.py:39
  142.2 8.7 %collective-permute-start.40 = (bf16[200,100]{1,0:T(8,128)(2,1)S(1)}, bf16[200,100]{1,0:T(8,128)(2,1)S(1)}, u32[]{:S(2)}, u32[]{:S(2)}) collective-permute-start(bf16[200,100]{1,0:T(8,128)(2,1)S(1)} %taylor.1), channel_id=1, source_target_pairs={{0,0},{1,1},{2,2},{3,3},{4,16},{5,17},{6,18},{7,19},{8,32},{9,33},... | collective-permute-start | bytes 120008 | tf_op jit(solution)/shard_map/ppermute | solution.py:64

commit v3 on v2

--- a/solution.py
+++ b/solution.py
@@ -286,7 +286,7 @@
     second[...] = jnp.where(pick, odd, even).astype(second.dtype)
 
 
-def choose_kernel(second, got, more, after, block0, block1):
+def choose_kernel(second, got, more, after, block0, block1, blocks):
     at = position()
     active = (at[2] + at[3]) % 2 == 0
 
@@ -294,22 +294,24 @@
     def _():
         block0[...] = second[...]
         block1[...] = got[...]
+        stack(blocks, second, got)
 
     @pl.when(jnp.logical_not(active))
     def _():
         block0[...] = got[...]
         block1[...] = more[...]
-
-
-def stack_kernel(low, high, out):
-    stack(out, low, high)
-
-
-def stack_y_kernel(b0, b1, b2, b3, near, far, quad, stacked):
+        stack(blocks, got, more)
+
+
+def stack_low_kernel(block, partners, out):
+    stack(out, block[...], partners[: block.shape[0], :])
+
+
+def stack_y_kernel(b1, b2, b3, near, far, three, stacked):
     stack(stacked, near, far)
-    half = b0.shape[0]
-    for step, ref in enumerate((b0, b1, b2, b3)):
-        quad[step * half : (step + 1) * half, :] = ref[...]
+    half = b1.shape[0]
+    for step, ref in enumerate((b1, b2, b3)):
+        three[step * half : (step + 1) * half, :] = ref[...]
 
 
 def own_base():
@@ -326,32 +328,38 @@
         last[part * half : (part + 1) * half, :] = held[y * NL + part]
 
 
-def first_rows_kernel(p0, p1, p2, p3, walkers, swapped, out, last, start, held, total):
-    low, _, core, _, y = position()
+def first_rows_kernel(p0, p1, p2, p3, walkers, out, last, walkers_out, held):
+    low, _, _, _, y = position()
+    walkers_out[...] = walkers[...]
     half = held.shape[1]
     for step, ref in enumerate((p0, p1, p2, p3)):
         row = ((y - step + NY) % NY) * NL
         held[row + low] = ref[:half, :]
         held[row + 1 - low] = ref[half:, :]
     compact(held, out, last)
+
+
+def second_rows_kernel(block, three, low_blocks, low_three, walkers, swapped, out, last, start, held, total):
+    low, _, core, _, y = position()
+    half = held.shape[1]
+    for step in range(NY):
+        row = ((y - step + NY) % NY) * NL
+        if step == 0:
+            held[row + low] = block[...]
+            held[row + 1 - low] = low_blocks[half:, :]
+        else:
+            place = slice((step - 1) * half, step * half)
+            held[row + low] = three[place, :]
+            held[row + 1 - low] = low_three[place, :]
+    compact(held, out, last)
     rows = 2 * half
     for step, ref in enumerate((walkers, swapped)):
         for index in range(NY * NL):
             total[step, index] = ref[index * rows : (index + 1) * rows, :]
-    for block in range(NH * NY):
-        row, column = block // NY, block % NY
+    for at in range(NH * NY):
+        row, column = at // NY, at % NY
         piece = total[(row % NC) ^ core, (y ^ column) * NL + ((row // NC) ^ low)]
-        start[block * rows : (block + 1) * rows, :] = piece
-
-
-def second_rows_kernel(mine, partner, after, out, last, held):
-    low, _, _, _, y = position()
-    half = held.shape[1]
-    for step in range(NY):
-        row = ((y - step + NY) % NY) * NL
-        held[row + low] = mine[step * half : (step + 1) * half, :]
-        held[row + 1 - low] = partner[step * half : (step + 1) * half, :]
-    compact(held, out, last)
+        start[at * rows : (at + 1) * rows, :] = piece
 
 
 def taylor_kernel(rows0, rows1, other0, other1, last0, last1, start, walkers, out_ref, operator, terms, total):
@@ -475,32 +483,33 @@
 
     got = everywhere(first, first_target)
     more = everywhere(second, second_target)
-    block0, block1 = call(choose_kernel, [piece] * 2, (second, got, more, far_rows), "choose", idle=1)
-    pair0 = call(stack_kernel, two, (block0, swap_low(block0)), "stack_low")
-    block1s = [block1] + [send_y(block1, step) for step in range(1, NY)]
-    quad1, eight_rows = call(
+    block0, block1, blocks = call(
+        choose_kernel, [piece] * 2 + [two], (second, got, more, far_rows), "choose", idle=1
+    )
+    low_blocks = swap_low(blocks)
+    pair0 = call(stack_low_kernel, two, (block0, low_blocks), "stack_low")
+    three, eight_rows = call(
         stack_y_kernel,
-        [quad, shaped((4 * NL * rows, occupied), bf16)],
-        (*block1s, four_rows, far_rows),
+        [shaped((3 * half, orbitals), bf16), shaped((4 * NL * rows, occupied), bf16)],
+        (*[send_y(block1, step) for step in range(1, NY)], four_rows, far_rows),
         "stack_y",
     )
     stretch = shaped((NY * rows, orbitals), bf16)
     held = pltpu.VMEM((NY * NL, half, orbitals), bf16)
-    rows0, last0, start = call(
+    rows0, last0, eight_rows = call(
         first_rows_kernel,
+        [stretch, two, shaped(eight_rows.shape, bf16)],
+        (pair0, *[send_y(pair0, step) for step in range(1, NY)], eight_rows),
+        "first_rows",
+        scratch=[held],
+        flops=None,
+    )
+    rows1, last1, start = call(
+        second_rows_kernel,
         [stretch, two, shaped((orbitals, occupied), bf16)],
-        (pair0, *[send_y(pair0, step) for step in range(1, NY)], eight_rows, swap_core(eight_rows)),
-        "first_rows",
+        (block1, three, low_blocks, swap_low(three), eight_rows, swap_core(eight_rows)),
+        "second_rows",
         scratch=[held, pltpu.VMEM((NC, NY * NL, rows, occupied), bf16)],
-        flops=4 * 10**9,
-    )
-    rows1, last1 = call(
-        second_rows_kernel,
-        [stretch, two],
-        (quad1, swap_low(quad1), rows0),
-        "second_rows",
-        scratch=[held],
-        idle=1,
     )
     updated = call(
         taylor_kernel,

time: 153 us -> 152 us (level)
  waiting for transfers between devices: 66.1 us -> 69.3 us
  starting transfers between devices: 63.4 us -> 60.7 us
    ppermute x9, waiting for transfers between devices: 22 us -> 18.3 us  [send_y(): lax.ppermute(array, 'pair', [(h * NY + y, h * NY + (y + step) % NY) for h...]
    ppermute x4, starting transfers between devices: 17.6 us -> 14 us  [everywhere(): return lax.ppermute(array, ('vec', 'pair'), pairs)]
    ppermute x4, waiting for transfers between devices: 10.9 us -> 14.5 us  [everywhere(): return lax.ppermute(array, ('vec', 'pair'), pairs)]
    ppermute x6, waiting for transfers between devices: 5.9 us -> 7.73 us  [swap_low(): lax.ppermute(array, 'vec', [(vec_of(*p), vec_of(p[0], 1 - p[1], p[2])) fo...]
  transfers between devices with their start and end apart: 41 -> 41, of which waited for: 24 -> 25; matrix products, arithmetic and copies ran while one was open for 0% -> 0% of each run, Pallas kernels for 1% -> 1%
where the time goes in v3:
time: 152 us
  waiting for transfers between devices  69.3 us (46%)
  starting transfers between devices  60.7 us (40%)
  Pallas kernels  17.8 us (12%)
  local copies, waits for them, and re-layouts  3.45 us (2%)
    ppermute x9, waiting for transfers between devices, send_y(): lax.ppermute(array, 'pair', [(h * NY + y, h * NY + (y + step) % NY) for h...  18.3 us
    pallas_call x14, Pallas kernels, call(): pl.pallas_call(kernel, out_shape=outs, in_specs=specs, out_specs=[VMEM] *...  16.3 us
    ppermute x4, waiting for transfers between devices, everywhere(): return lax.ppermute(array, ('vec', 'pair'), pairs)  14.5 us
    ppermute x9, starting transfers between devices, send_x(): lax.ppermute(array, 'vec', [(vec_of(*p), vec_of(p[0] + step, p[1], p[2]))...  14.2 us
    ppermute x9, waiting for transfers between devices, send_x(): lax.ppermute(array, 'vec', [(vec_of(*p), vec_of(p[0] + step, p[1], p[2]))...  14.1 us
    ppermute x4, starting transfers between devices, everywhere(): return lax.ppermute(array, ('vec', 'pair'), pairs)  14 us
    ppermute x8, starting transfers between devices, swap_core(): lax.ppermute(array, 'vec', [(vec_of(*p), vec_of(p[0], p[1], 1 - p[2])) fo...  10.6 us
    ppermute x9, starting transfers between devices, send_y(): lax.ppermute(array, 'pair', [(h * NY + y, h * NY + (y + step) % NY) for h...  8.96 us
  transfers between devices with their start and end apart: 41, of which 25 were waited for; matrix products, arithmetic and copies ran while one was open for 0% of the time, Pallas kernels for 1%

profile of v3, /device:TPU:33, one launch (start us, length us, event | category | flops | bytes accessed | tf_op | source)
XLA Modules:
  0.0 152.0 jit_solution(1497105645366333609)
XLA Ops:
  0.6 0.8 collective-permute-start.4
  1.4 0.9 copy-done.1
  2.3 0.8 copy-done.2
  3.4 1.7 %collective-permute-start = (bf16[112,200]{1,0:T(8,128)(2,1)S(1)}, bf16[112,200]{1,0:T(8,128)(2,1)S(1)}, u32[]{:S(2)}, u32[]{:S(2)}) collective-permute-start(bf16[112,200]{1,0:T(8,128)(2,1)S(1)} %rotate.1.rotated), channel_id=1, source_target_pairs={{0,32},{16,48},{32,0},{48,16},{64,96},{80,112},{96,64},{112,80},{1... | collective-permute-start | bytes 134408 | tf_op jit(solution)/shard_map/ppermute | solution.py:35
  5.1 2.2 %collective-permute-done.partner = bf16[112,200]{1,0:T(8,128)(2,1)S(1)} collective-permute-done((bf16[112,200]{1,0:T(8,128)(2,1)S(1)}, bf16[112,200]{1,0:T(8,128)(2,1)S(1)}, u32[]{:S(2)}, u32[]{:S(2)}) %collective-permute-start) | collective-permute-done | bytes 44832 | tf_op jit(solution)/shard_map/ppermute | solution.py:35
  7.3 1.1 copy-done
  8.4 1.1 collective-permute-start.3
  9.5 2.5 %collective-permute-start.2 = (bf16[2,112,200]{2,1,0:T(8,128)(2,1)S(1)}, bf16[2,112,200]{2,1,0:T(8,128)(2,1)S(1)}, u32[]{:S(2)}, u32[]{:S(2)}) collective-permute-start(bf16[2,112,200]{2,1,0:T(8,128)(2,1)S(1)} %get-tuple-element.39.r0), channel_id=1, source_target_pairs={{0,128},{16,144},{32,160},{48,176},{64,192},{80,208},{96,224},{112... | collective-permute-start | bytes 268808 | tf_op jit(solution)/shard_map/ppermute | solution.py:31
  11.9 1.2 collective-permute-start.1
  13.1 0.6 collective-permute-done.3.a3.r3
  13.7 2.8 %collective-permute-done.2.a2.r2 = bf16[2,112,200]{2,1,0:T(8,128)(2,1)S(1)} collective-permute-done((bf16[2,112,200]{2,1,0:T(8,128)(2,1)S(1)}, bf16[2,112,200]{2,1,0:T(8,128)(2,1)S(1)}, u32[]{:S(2)}, u32[]{:S(2)}) %collective-permute-start.2) | collective-permute-done | bytes 89632 | tf_op jit(solution)/shard_map/ppermute | solution.py:31
  16.5 0.6 collective-permute-done.1.a1.r1
  17.1 1.7 %vector_factor.1.other = bf16[100,16,200]{2,1,0:T(8,128)(2,1)S(1)} custom-call(bf16[200,1600]{1,0:T(8,128)(2,1)S(1)} %get-tuple-element.40.trial, bf16[100,16,1600]{2,1,0:T(8,128)(2,1)S(1)} %collective-permute-done.4.block.passed, bf16[2,112,200]{2,1,0:T(8,128)(2,1)S(1)} %collective-permute-done.1.a1.r1, ...), custom_call_target="tpu_custom_call" | custom-call | tf_op jit(solution)/shard_map/vector_factor/pallas_call | solution.py:394
  18.8 1.5 collective-permute-start.5
  20.3 2.0 %collective-permute-done.5.own = bf16[100,16,200]{2,1,0:T(8,128)(2,1)S(1)} collective-permute-done((bf16[100,16,200]{2,1,0:T(8,128)(2,1)S(1)}, bf16[100,16,200]{2,1,0:T(8,128)(2,1)S(1)}, u32[]{:S(2)}, u32[]{:S(2)}) %collective-permute-start.5) | collective-permute-done | bytes 640032 | tf_op jit(solution)/shard_map/ppermute | solution.py:39
  22.3 1.5 force_bias.1
  24.2 7.5 %collective-permute-start.13 = (bf16[200,100]{1,0:T(8,128)(2,1)S(1)}, bf16[200,100]{1,0:T(8,128)(2,1)S(1)}, u32[]{:S(2)}, u32[]{:S(2)}) collective-permute-start(bf16[200,100]{1,0:T(8,128)(2,1)S(1)} %bitcast.12), channel_id=1, source_target_pairs={{0,0},{1,1},{2,2},{3,3},{4,16},{5,17},{6,18},{7,19},{8,32},{9,33},... | collective-permute-start | bytes 120008 | tf_op jit(solution)/shard_map/ppermute | solution.py:64
  31.7 2.8 %collective-permute-start.8 = (f32[8,32]{1,0:T(8,128)S(1)}, f32[8,32]{1,0:T(8,128)S(1)}, u32[]{:S(2)}, u32[]{:S(2)}) collective-permute-start(f32[8,32]{1,0:T(8,128)S(1)} %get-tuple-element.41.b0), channel_id=1, source_target_pairs={{0,3},{1,0},{2,1},{3,2},{4,7},{5,4},{6,5},{7,6},{8,11},{9,8},{10,9... | collective-permute-start | bytes 3080 | tf_op jit(solution)/shard_map/ppermute | solution.py:43
  34.8 0.7 collective-permute-start.6
  35.5 1.2 collective-permute-start.12
  36.8 1.7 %collective-permute-done.7.b2 = f32[8,32]{1,0:T(8,128)S(1)} collective-permute-done((f32[8,32]{1,0:T(8,128)S(1)}, f32[8,32]{1,0:T(8,128)S(1)}, u32[]{:S(2)}, u32[]{:S(2)}) %collective-permute-start.7) | collective-permute-done | bytes 1056 | tf_op jit(solution)/shard_map/ppermute | solution.py:43
  38.5 4.7 %collective-permute-start.10 = (f32[8,32]{1,0:T(8,128)S(1)}, f32[8,32]{1,0:T(8,128)S(1)}, u32[]{:S(2)}, u32[]{:S(2)}) collective-permute-start(f32[8,32]{1,0:T(8,128)S(1)} %sum_y.1.b0), channel_id=1, source_target_pairs={{0,8},{1,9},{2,10},{3,11},{4,12},{5,13},{6,14},{7,15},{8,0},{9,1},... | collective-permute-start | bytes 3080 | tf_op jit(solution)/shard_map/ppermute | solution.py:51
  43.3 1.7 %collective-permute-done.10.b2 = f32[8,32]{1,0:T(8,128)S(1)} collective-permute-done((f32[8,32]{1,0:T(8,128)S(1)}, f32[8,32]{1,0:T(8,128)S(1)}, u32[]{:S(2)}, u32[]{:S(2)}) %collective-permute-start.10) | collective-permute-done | bytes 1056 | tf_op jit(solution)/shard_map/ppermute | solution.py:51
  45.0 3.1 %collective-permute-done.9.b1 = f32[8,32]{1,0:T(8,128)S(1)} collective-permute-done((f32[8,32]{1,0:T(8,128)S(1)}, f32[8,32]{1,0:T(8,128)S(1)}, u32[]{:S(2)}, u32[]{:S(2)}) %collective-permute-start.9) | collective-permute-done | bytes 1056 | tf_op jit(solution)/shard_map/ppermute | solution.py:51
  48.1 2.5 %field_operator.1 = (f32[8,32]{1,0:T(8,128)S(1)}, f32[8,16]{1,0:T(8,128)S(1)}, bf16[100,1600]{1,0:T(8,128)(2,1)S(1)}, bf16[100,1600]{1,0:T(8,128)(2,1)S(1)}, bf1...) custom-call(f32[8,32]{1,0:T(8,128)S(1)} %sum_y.1.b0, ...), custom_call_target="tpu_custom_call" | custom-call | tf_op jit(solution)/shard_map/field_operator/pallas_call | solution.py:394
  50.7 1.1 collective-permute-start.15
  51.8 2.4 %collective-permute-start.16 = (bf16[100,1600]{1,0:T(8,128)(2,1)S(1)}, bf16[100,1600]{1,0:T(8,128)(2,1)S(1)}, u32[]{:S(2)}, u32[]{:S(2)}) collective-permute-start(bf16[100,1600]{1,0:T(8,128)(2,1)S(1)} %get-tuple-element.46), channel_id=1, source_target_pairs={{0,128},{16,144},{32,160},{48,176},{64,192},{80,208},{96,224},{112... | collective-permute-start | bytes 960008 | tf_op jit(solution)/shard_map/ppermute | solution.py:31
  54.2 1.0 collective-permute-start.17
  55.2 1.4 collective-permute-start.21
  56.6 2.7 %collective-permute-done.15.p1 = bf16[100,1600]{1,0:T(8,128)(2,1)S(1)} collective-permute-done((bf16[100,1600]{1,0:T(8,128)(2,1)S(1)}, bf16[100,1600]{1,0:T(8,128)(2,1)S(1)}, u32[]{:S(2)}, u32[]{:S(2)}) %collective-permute-start.15) | collective-permute-done | bytes 320032 | tf_op jit(solution)/shard_map/ppermute | solution.py:31
  59.2 5.3 %collective-permute-start.20 = (f32[8,16]{1,0:T(8,128)S(1)}, f32[8,16]{1,0:T(8,128)S(1)}, u32[]{:S(2)}, u32[]{:S(2)}) collective-permute-start(f32[8,16]{1,0:T(8,128)S(1)} %get-tuple-element.54), channel_id=1, source_target_pairs={{0,16},{16,0},{32,48},{48,32},{64,80},{80,64},{96,112},{112,96},{1... | collective-permute-start | bytes 1544 | tf_op jit(solution)/shard_map/ppermute | solution.py:39
  64.5 2.9 %collective-permute-done.16.p2 = bf16[100,1600]{1,0:T(8,128)(2,1)S(1)} collective-permute-done((bf16[100,1600]{1,0:T(8,128)(2,1)S(1)}, bf16[100,1600]{1,0:T(8,128)(2,1)S(1)}, u32[]{:S(2)}, u32[]{:S(2)}) %collective-permute-start.16) | collective-permute-done | bytes 320032 | tf_op jit(solution)/shard_map/ppermute | solution.py:31
  67.4 1.3 collective-permute-done.17.p3
  68.9 1.1 collective-permute-start.18
  70.1 0.7 pair_sum.1
  70.8 2.6 %collective-permute-start.22 = (bf16[50,1600]{1,0:T(8,128)(2,1)S(1)}, bf16[50,1600]{1,0:T(8,128)(2,1)S(1)}, u32[]{:S(2)}, u32[]{:S(2)}) collective-permute-start(bf16[50,1600]{1,0:T(8,128)(2,1)S(1)} %get-tuple-element.57), channel_id=1, source_target_pairs={{0,64},{16,80},{32,96},{48,112},{64,128},{80,144},{96,160},{112,17... | collective-permute-start | bytes 480008 | tf_op jit(solution)/shard_map/ppermute | solution.py:31
  73.4 2.0 %collective-permute-start.23 = (bf16[50,1600]{1,0:T(8,128)(2,1)S(1)}, bf16[50,1600]{1,0:T(8,128)(2,1)S(1)}, u32[]{:S(2)}, u32[]{:S(2)}) collective-permute-start(bf16[50,1600]{1,0:T(8,128)(2,1)S(1)} %get-tuple-element.58), channel_id=1, source_target_pairs={{0,128},{16,144},{32,160},{48,176},{64,192},{80,208},{96,224},{112... | collective-permute-start | bytes 480008 | tf_op jit(solution)/shard_map/ppermute | solution.py:31
  75.8 3.8 %collective-permute-done.25.partners = bf16[200,200]{1,0:T(8,128)(2,1)S(1)} collective-permute-done((bf16[200,200]{1,0:T(8,128)(2,1)S(1)}, bf16[200,200]{1,0:T(8,128)(2,1)S(1)}, u32[]{:S(2)}, u32[]{:S(2)}) %collective-permute-start.25) | collective-permute-done | bytes 80032 | tf_op jit(solution)/shard_map/ppermute | solution.py:47
  79.6 3.2 %collective-permute-done.23.q2 = bf16[50,1600]{1,0:T(8,128)(2,1)S(1)} collective-permute-done((bf16[50,1600]{1,0:T(8,128)(2,1)S(1)}, bf16[50,1600]{1,0:T(8,128)(2,1)S(1)}, u32[]{:S(2)}, u32[]{:S(2)}) %collective-permute-start.23) | collective-permute-done | bytes 160032 | tf_op jit(solution)/shard_map/ppermute | solution.py:31
  83.1 0.7 collective-permute-start.26
  83.8 3.9 %collective-permute-start.27 = (bf16[50,1600]{1,0:T(8,128)(2,1)S(1)}, bf16[50,1600]{1,0:T(8,128)(2,1)S(1)}, u32[]{:S(2)}, u32[]{:S(2)}) collective-permute-start(bf16[50,1600]{1,0:T(8,128)(2,1)S(1)} %get-tuple-element.61.second), channel_id=1, source_target_pairs={{4,24},{5,25},{6,26},{7,27},{12,16},{13,17},{14,18},{15,19},{16,4}... | collective-permute-start | bytes 480008 | tf_op jit(solution)/shard_map/ppermute | solution.py:64
  88.0 1.2 collective-permute-done.26.got
  89.2 6.5 %collective-permute-done.27.more = bf16[50,1600]{1,0:T(8,128)(2,1)S(1)} collective-permute-done((bf16[50,1600]{1,0:T(8,128)(2,1)S(1)}, bf16[50,1600]{1,0:T(8,128)(2,1)S(1)}, u32[]{:S(2)}, u32[]{:S(2)}) %collective-permute-start.27) | collective-permute-done | bytes 160032 | tf_op jit(solution)/shard_map/ppermute | solution.py:64
  95.8 2.5 %collective-permute-start.29 = (bf16[100,1600]{1,0:T(8,128)(2,1)S(1)}, bf16[100,1600]{1,0:T(8,128)(2,1)S(1)}, u32[]{:S(2)}, u32[]{:S(2)}) collective-permute-start(bf16[100,1600]{1,0:T(8,128)(2,1)S(1)} %get-tuple-element.65), channel_id=1, source_target_pairs={{0,32},{16,48},{32,0},{48,16},{64,96},{80,112},{96,64},{112,80},{1... | collective-permute-start | bytes 960008 | tf_op jit(solution)/shard_map/ppermute | solution.py:35
  98.3 1.3 collective-permute-start.35
  99.6 1.0 collective-permute-start.34
  100.6 0.6 collective-permute-start.33
  101.2 5.5 %collective-permute-done.29.partners.low_blocks = bf16[100,1600]{1,0:T(8,128)(2,1)S(1)} collective-permute-done((bf16[100,1600]{1,0:T(8,128)(2,1)S(1)}, bf16[100,1600]{1,0:T(8,128)(2,1)S(1)}, u32[]{:S(2)}, u32[]{:S(2)}) %collective-permute-start.29) | collective-permute-done | bytes 320032 | tf_op jit(solution)/shard_map/ppermute | solution.py:35
  106.7 1.5 %collective-permute-start.32 = (bf16[100,1600]{1,0:T(8,128)(2,1)S(1)}, bf16[100,1600]{1,0:T(8,128)(2,1)S(1)}, u32[]{:S(2)}, u32[]{:S(2)}) collective-permute-start(bf16[100,1600]{1,0:T(8,128)(2,1)S(1)} %stack_low.1.p0), channel_id=1, source_target_pairs={{0,3},{1,0},{2,1},{3,2},{4,7},{5,4},{6,5},{7,6},{8,11},{9,8},{10,9... | collective-permute-start | bytes 960008 | tf_op jit(solution)/shard_map/ppermute | solution.py:43
  108.3 0.7 collective-permute-start.30
  109.0 2.0 %collective-permute-done.33.b1 = bf16[50,1600]{1,0:T(8,128)(2,1)S(1)} collective-permute-done((bf16[50,1600]{1,0:T(8,128)(2,1)S(1)}, bf16[50,1600]{1,0:T(8,128)(2,1)S(1)}, u32[]{:S(2)}, u32[]{:S(2)}) %collective-permute-start.33) | collective-permute-done | bytes 160032 | tf_op jit(solution)/shard_map/ppermute | solution.py:43
  111.0 1.0 collective-permute-start.36
  112.0 4.3 %collective-permute-done.32.p3 = bf16[100,1600]{1,0:T(8,128)(2,1)S(1)} collective-permute-done((bf16[100,1600]{1,0:T(8,128)(2,1)S(1)}, bf16[100,1600]{1,0:T(8,128)(2,1)S(1)}, u32[]{:S(2)}, u32[]{:S(2)}) %collective-permute-start.32) | collective-permute-done | bytes 320032 | tf_op jit(solution)/shard_map/ppermute | solution.py:43
  116.4 2.6 %collective-permute-done.31.p2 = bf16[100,1600]{1,0:T(8,128)(2,1)S(1)} collective-permute-done((bf16[100,1600]{1,0:T(8,128)(2,1)S(1)}, bf16[100,1600]{1,0:T(8,128)(2,1)S(1)}, u32[]{:S(2)}, u32[]{:S(2)}) %collective-permute-start.31) | collective-permute-done | bytes 320032 | tf_op jit(solution)/shard_map/ppermute | solution.py:43
  119.0 7.7 %collective-permute-done.30.p1 = bf16[100,1600]{1,0:T(8,128)(2,1)S(1)} collective-permute-done((bf16[100,1600]{1,0:T(8,128)(2,1)S(1)}, bf16[100,1600]{1,0:T(8,128)(2,1)S(1)}, u32[]{:S(2)}, u32[]{:S(2)}) %collective-permute-start.30) | collective-permute-done | bytes 320032 | tf_op jit(solution)/shard_map/ppermute | solution.py:43
  127.0 0.9 collective-permute-start.37
  128.0 1.3 collective-permute-done.37.swapped
  129.3 0.5 second_rows.1
  130.3 0.9 collective-permute-done.38.other0
  131.2 1.9 %collective-permute-done.39.other1 = bf16[400,1600]{1,0:T(8,128)(2,1)S(1)} collective-permute-done((bf16[400,1600]{1,0:T(8,128)(2,1)S(1)}, bf16[400,1600]{1,0:T(8,128)(2,1)S(1)}, u32[]{:S(2)}, u32[]{:S(2)}) %collective-permute-start.39) | collective-permute-done | bytes 1280032 | tf_op jit(solution)/shard_map/ppermute | solution.py:39
  133.1 9.6 %taylor.1 = bf16[200,100]{1,0:T(8,128)(2,1)S(1)} custom-call(bf16[400,1600]{1,0:T(8,128)(2,1)S(1)} %get-tuple-element.68.rows0, bf16[400,1600]{1,0:T(8,128)(2,1)S(1)} %get-tuple-element.71.rows1, bf16[400,1600]{1,0:T(8,128)(2,1)S(1)} %collective-permute-done.38.other0, bf16[400,1600]{1,0:T(8,128)(2,1)S(1)} %collective-permute-done.39.other1, ...), custom_call_target="tpu_custom_call" | custom-call | tf_op jit(solution)/shard_map/taylor/pallas_call | solution.py:394
  142.7 1.9 %collective-permute-start.40 = (bf16[200,100]{1,0:T(8,128)(2,1)S(1)}, bf16[200,100]{1,0:T(8,128)(2,1)S(1)}, u32[]{:S(2)}, u32[]{:S(2)}) collective-permute-start(bf16[200,100]{1,0:T(8,128)(2,1)S(1)} %taylor.1), channel_id=1, source_target_pairs={{0,0},{1,1},{2,2},{3,3},{4,16},{5,17},{6,18},{7,19},{8,32},{9,33},... | collective-permute-start | bytes 120008 | tf_op jit(solution)/shard_map/ppermute | solution.py:64
  144.6 6.8 %collective-permute-done.40 = bf16[200,100]{1,0:T(8,128)(2,1)S(1)} collective-permute-done((bf16[200,100]{1,0:T(8,128)(2,1)S(1)}, bf16[200,100]{1,0:T(8,128)(2,1)S(1)}, u32[]{:S(2)}, u32[]{:S(2)}) %collective-permute-start.40) | collective-permute-done | bytes 40032 | tf_op jit(solution)/shard_map/ppermute | solution.py:64
  151.4 0.6 copy.10
  (44 shorter events, 3.6 us)
Async XLA Ops:
  0.6 16.5 %collective-permute-start.4 = (bf16[100,16,1600]{2,1,0:T(8,128)(2,1)}, bf16[100,16,1600]{2,1,0:T(8,128)(2,1)S(1)}, u32[]{:S(2)}, u32[]{:S(2)}) collective-permute-start(bf16[100,16,1600]{2,1,0:T(8,128)(2,1)} %bitcast.14), channel_id=1, source_target_pairs={{0,16},{16,0},{32,48},{48,32},{64,80},{80,64},{96,112},{112,96},{1... | collective-permute-start | bytes 15360008 | tf_op jit(solution)/shard_map/ppermute | solution.py:39
  1.4 0.9 copy-start.1
  2.3 0.8 copy-start.2
  3.1 19.1 %copy-start.4 = (f32[16,16]{1,0:T(8,128)S(1)}, f32[16,16]{1,0:T(8,128)}, u32[]{:S(2)}) copy-start(f32[16,16]{1,0:T(8,128)} %aux.3) | copy-start | bytes 3076
  3.4 3.9 %collective-permute-start = (bf16[112,200]{1,0:T(8,128)(2,1)S(1)}, bf16[112,200]{1,0:T(8,128)(2,1)S(1)}, u32[]{:S(2)}, u32[]{:S(2)}) collective-permute-start(bf16[112,200]{1,0:T(8,128)(2,1)S(1)} %rotate.1.rotated), channel_id=1, source_target_pairs={{0,32},{16,48},{32,0},{48,16},{64,96},{80,112},{96,64},{112,80},{1... | collective-permute-start | bytes 134408 | tf_op jit(solution)/shard_map/ppermute | solution.py:35
  7.3 1.1 copy-start
  8.4 5.3 %collective-permute-start.3 = (bf16[2,112,200]{2,1,0:T(8,128)(2,1)S(1)}, bf16[2,112,200]{2,1,0:T(8,128)(2,1)S(1)}, u32[]{:S(2)}, u32[]{:S(2)}) collective-permute-start(bf16[2,112,200]{2,1,0:T(8,128)(2,1)S(1)} %get-tuple-element.39.r0), channel_id=1, source_target_pairs={{0,64},{16,80},{32,96},{48,112},{64,128},{80,144},{96,160},{112,17... | collective-permute-start | bytes 268808 | tf_op jit(solution)/shard_map/ppermute | solution.py:31
  9.5 7.0 %collective-permute-start.2 = (bf16[2,112,200]{2,1,0:T(8,128)(2,1)S(1)}, bf16[2,112,200]{2,1,0:T(8,128)(2,1)S(1)}, u32[]{:S(2)}, u32[]{:S(2)}) collective-permute-start(bf16[2,112,200]{2,1,0:T(8,128)(2,1)S(1)} %get-tuple-element.39.r0), channel_id=1, source_target_pairs={{0,128},{16,144},{32,160},{48,176},{64,192},{80,208},{96,224},{112... | collective-permute-start | bytes 268808 | tf_op jit(solution)/shard_map/ppermute | solution.py:31
  11.9 5.2 %collective-permute-start.1 = (bf16[2,112,200]{2,1,0:T(8,128)(2,1)S(1)}, bf16[2,112,200]{2,1,0:T(8,128)(2,1)S(1)}, u32[]{:S(2)}, u32[]{:S(2)}) collective-permute-start(bf16[2,112,200]{2,1,0:T(8,128)(2,1)S(1)} %get-tuple-element.39.r0), channel_id=1, source_target_pairs={{0,192},{16,208},{32,224},{48,240},{64,0},{80,16},{96,32},{112,48}... | collective-permute-start | bytes 268808 | tf_op jit(solution)/shard_map/ppermute | solution.py:31
  18.8 5.4 %copy-start.3 = (bf16[1,100,200]{1,2,0:T(8,128)(2,1)S(1)}, bf16[1,100,200]{1,2,0:T(8,128)(2,1)}, u32[]{:S(2)}) copy-start(bf16[1,100,200]{1,2,0:T(8,128)(2,1)} %param.6) | copy-start | bytes 120004
  18.8 3.4 %collective-permute-start.5 = (bf16[100,16,200]{2,1,0:T(8,128)(2,1)S(1)}, bf16[100,16,200]{2,1,0:T(8,128)(2,1)S(1)}, u32[]{:S(2)}, u32[]{:S(2)}) collective-permute-start(bf16[100,16,200]{2,1,0:T(8,128)(2,1)S(1)} %vector_factor.1.other), channel_id=1, source_target_pairs={{0,16},{16,0},{32,48},{48,32},{64,80},{80,64},{96,112},{112,96},{1... | collective-permute-start | bytes 1920008 | tf_op jit(solution)/shard_map/ppermute | solution.py:39
  23.8 24.3 %collective-permute-start.14 = (bf16[100,16,1600]{2,1,0:T(8,128)(2,1)S(1)}, bf16[100,16,1600]{2,1,0:T(8,128)(2,1)S(1)}, u32[]{:S(2)}, u32[]{:S(2)}) collective-permute-start(bf16[100,16,1600]{2,1,0:T(8,128)(2,1)S(1)} %get-tuple-element.43.other), channel_id=1, source_target_pairs={{0,16},{16,0},{32,48},{48,32},{64,80},{80,64},{96,112},{112,96},{1... | collective-permute-start | bytes 15360008 | tf_op jit(solution)/shard_map/ppermute | solution.py:39
  24.2 19.1 %collective-permute-start.13 = (bf16[200,100]{1,0:T(8,128)(2,1)S(1)}, bf16[200,100]{1,0:T(8,128)(2,1)S(1)}, u32[]{:S(2)}, u32[]{:S(2)}) collective-permute-start(bf16[200,100]{1,0:T(8,128)(2,1)S(1)} %bitcast.12), channel_id=1, source_target_pairs={{0,0},{1,1},{2,2},{3,3},{4,16},{5,17},{6,18},{7,19},{8,32},{9,33},... | collective-permute-start | bytes 120008 | tf_op jit(solution)/shard_map/ppermute | solution.py:64
  31.7 3.9 %collective-permute-start.8 = (f32[8,32]{1,0:T(8,128)S(1)}, f32[8,32]{1,0:T(8,128)S(1)}, u32[]{:S(2)}, u32[]{:S(2)}) collective-permute-start(f32[8,32]{1,0:T(8,128)S(1)} %get-tuple-element.41.b0), channel_id=1, source_target_pairs={{0,3},{1,0},{2,1},{3,2},{4,7},{5,4},{6,5},{7,6},{8,11},{9,8},{10,9... | collective-permute-start | bytes 3080 | tf_op jit(solution)/shard_map/ppermute | solution.py:43
  34.5 4.0 %collective-permute-start.7 = (f32[8,32]{1,0:T(8,128)S(1)}, f32[8,32]{1,0:T(8,128)S(1)}, u32[]{:S(2)}, u32[]{:S(2)}) collective-permute-start(f32[8,32]{1,0:T(8,128)S(1)} %get-tuple-element.41.b0), channel_id=1, source_target_pairs={{0,2},{1,3},{2,0},{3,1},{4,6},{5,7},{6,4},{7,5},{8,10},{9,11},{10,... | collective-permute-start | bytes 3080 | tf_op jit(solution)/shard_map/ppermute | solution.py:43
  34.8 3.7 %collective-permute-start.6 = (f32[8,32]{1,0:T(8,128)S(1)}, f32[8,32]{1,0:T(8,128)S(1)}, u32[]{:S(2)}, u32[]{:S(2)}) collective-permute-start(f32[8,32]{1,0:T(8,128)S(1)} %get-tuple-element.41.b0), channel_id=1, source_target_pairs={{0,1},{1,2},{2,3},{3,0},{4,5},{5,6},{6,7},{7,4},{8,9},{9,10},{10,1... | collective-permute-start | bytes 3080 | tf_op jit(solution)/shard_map/ppermute | solution.py:43
  35.5 7.7 %collective-permute-start.12 = (f32[16,16]{1,0:T(8,128)S(1)}, f32[16,16]{1,0:T(8,128)S(1)}, u32[]{:S(2)}, u32[]{:S(2)}) collective-permute-start(f32[16,16]{1,0:T(8,128)S(1)} %get-tuple-element.42), channel_id=1, source_target_pairs={{0,16},{16,0},{32,48},{48,32},{64,80},{80,64},{96,112},{112,96},{1... | collective-permute-start | bytes 3080 | tf_op jit(solution)/shard_map/ppermute | solution.py:39
  38.5 4.8 %collective-permute-start.11 = (f32[8,32]{1,0:T(8,128)S(1)}, f32[8,32]{1,0:T(8,128)S(1)}, u32[]{:S(2)}, u32[]{:S(2)}) collective-permute-start(f32[8,32]{1,0:T(8,128)S(1)} %sum_y.1.b0), channel_id=1, source_target_pairs={{0,12},{1,13},{2,14},{3,15},{4,0},{5,1},{6,2},{7,3},{8,4},{9,5},{1... | collective-permute-start | bytes 3080 | tf_op jit(solution)/shard_map/ppermute | solution.py:51
  38.5 6.5 %collective-permute-start.10 = (f32[8,32]{1,0:T(8,128)S(1)}, f32[8,32]{1,0:T(8,128)S(1)}, u32[]{:S(2)}, u32[]{:S(2)}) collective-permute-start(f32[8,32]{1,0:T(8,128)S(1)} %sum_y.1.b0), channel_id=1, source_target_pairs={{0,8},{1,9},{2,10},{3,11},{4,12},{5,13},{6,14},{7,15},{8,0},{9,1},... | collective-permute-start | bytes 3080 | tf_op jit(solution)/shard_map/ppermute | solution.py:51
  43.3 4.9 %collective-permute-start.9 = (f32[8,32]{1,0:T(8,128)S(1)}, f32[8,32]{1,0:T(8,128)S(1)}, u32[]{:S(2)}, u32[]{:S(2)}) collective-permute-start(f32[8,32]{1,0:T(8,128)S(1)} %sum_y.1.b0), channel_id=1, source_target_pairs={{0,4},{1,5},{2,6},{3,7},{4,8},{5,9},{6,10},{7,11},{8,12},{9,13},{1... | collective-permute-start | bytes 3080 | tf_op jit(solution)/shard_map/ppermute | solution.py:51
  50.6 19.5 %collective-permute-start.19 = (bf16[224,1600]{1,0:T(8,128)(2,1)S(1)}, bf16[224,1600]{1,0:T(8,128)(2,1)S(1)}, u32[]{:S(2)}, u32[]{:S(2)}) collective-permute-start(bf16[224,1600]{1,0:T(8,128)(2,1)S(1)} %get-tuple-element.52), channel_id=1, source_target_pairs={{0,32},{16,48},{32,0},{48,16},{64,96},{80,112},{96,64},{112,80},{1... | collective-permute-start | bytes 2150408 | tf_op jit(solution)/shard_map/ppermute | solution.py:35
  50.7 8.6 %collective-permute-start.15 = (bf16[100,1600]{1,0:T(8,128)(2,1)S(1)}, bf16[100,1600]{1,0:T(8,128)(2,1)S(1)}, u32[]{:S(2)}, u32[]{:S(2)}) collective-permute-start(bf16[100,1600]{1,0:T(8,128)(2,1)S(1)} %get-tuple-element.45), channel_id=1, source_target_pairs={{0,64},{16,80},{32,96},{48,112},{64,128},{80,144},{96,160},{112,17... | collective-permute-start | bytes 960008 | tf_op jit(solution)/shard_map/ppermute | solution.py:31
  51.8 15.6 %collective-permute-start.16 = (bf16[100,1600]{1,0:T(8,128)(2,1)S(1)}, bf16[100,1600]{1,0:T(8,128)(2,1)S(1)}, u32[]{:S(2)}, u32[]{:S(2)}) collective-permute-start(bf16[100,1600]{1,0:T(8,128)(2,1)S(1)} %get-tuple-element.46), channel_id=1, source_target_pairs={{0,128},{16,144},{32,160},{48,176},{64,192},{80,208},{96,224},{112... | collective-permute-start | bytes 960008 | tf_op jit(solution)/shard_map/ppermute | solution.py:31
  54.2 14.6 %collective-permute-start.17 = (bf16[100,1600]{1,0:T(8,128)(2,1)S(1)}, bf16[100,1600]{1,0:T(8,128)(2,1)S(1)}, u32[]{:S(2)}, u32[]{:S(2)}) collective-permute-start(bf16[100,1600]{1,0:T(8,128)(2,1)S(1)} %get-tuple-element.47), channel_id=1, source_target_pairs={{0,192},{16,208},{32,224},{48,240},{64,0},{80,16},{96,32},{112,48}... | collective-permute-start | bytes 960008 | tf_op jit(solution)/shard_map/ppermute | solution.py:31
  55.2 14.8 %collective-permute-start.21 = (bf16[100,200]{1,0:T(8,128)(2,1)S(1)}, bf16[100,200]{1,0:T(8,128)(2,1)S(1)}, u32[]{:S(2)}, u32[]{:S(2)}) collective-permute-start(bf16[100,200]{1,0:T(8,128)(2,1)S(1)} %get-tuple-element.55.walkers), channel_id=1, source_target_pairs={{0,32},{16,48},{32,0},{48,16},{64,96},{80,112},{96,64},{112,80},{1... | collective-permute-start | bytes 120008 | tf_op jit(solution)/shard_map/ppermute | solution.py:35
  59.2 10.8 %collective-permute-start.20 = (f32[8,16]{1,0:T(8,128)S(1)}, f32[8,16]{1,0:T(8,128)S(1)}, u32[]{:S(2)}, u32[]{:S(2)}) collective-permute-start(f32[8,16]{1,0:T(8,128)S(1)} %get-tuple-element.54), channel_id=1, source_target_pairs={{0,16},{16,0},{32,48},{48,32},{64,80},{80,64},{96,112},{112,96},{1... | collective-permute-start | bytes 1544 | tf_op jit(solution)/shard_map/ppermute | solution.py:39
  68.9 6.9 %collective-permute-start.18 = (bf16[50,1600]{1,0:T(8,128)(2,1)S(1)}, bf16[50,1600]{1,0:T(8,128)(2,1)S(1)}, u32[]{:S(2)}, u32[]{:S(2)}) collective-permute-start(bf16[50,1600]{1,0:T(8,128)(2,1)S(1)} %x_sum.1), channel_id=1, source_target_pairs={{0,32},{16,48},{32,0},{48,16},{64,96},{80,112},{96,64},{112,80},{1... | collective-permute-start | bytes 480008 | tf_op jit(solution)/shard_map/ppermute | solution.py:35
  70.8 8.8 %collective-permute-start.22 = (bf16[50,1600]{1,0:T(8,128)(2,1)S(1)}, bf16[50,1600]{1,0:T(8,128)(2,1)S(1)}, u32[]{:S(2)}, u32[]{:S(2)}) collective-permute-start(bf16[50,1600]{1,0:T(8,128)(2,1)S(1)} %get-tuple-element.57), channel_id=1, source_target_pairs={{0,64},{16,80},{32,96},{48,112},{64,128},{80,144},{96,160},{112,17... | collective-permute-start | bytes 480008 | tf_op jit(solution)/shard_map/ppermute | solution.py:31
  73.4 9.4 %collective-permute-start.23 = (bf16[50,1600]{1,0:T(8,128)(2,1)S(1)}, bf16[50,1600]{1,0:T(8,128)(2,1)S(1)}, u32[]{:S(2)}, u32[]{:S(2)}) collective-permute-start(bf16[50,1600]{1,0:T(8,128)(2,1)S(1)} %get-tuple-element.58), channel_id=1, source_target_pairs={{0,128},{16,144},{32,160},{48,176},{64,192},{80,208},{96,224},{112... | collective-permute-start | bytes 480008 | tf_op jit(solution)/shard_map/ppermute | solution.py:31
  75.4 7.4 %collective-permute-start.24 = (bf16[50,1600]{1,0:T(8,128)(2,1)S(1)}, bf16[50,1600]{1,0:T(8,128)(2,1)S(1)}, u32[]{:S(2)}, u32[]{:S(2)}) collective-permute-start(bf16[50,1600]{1,0:T(8,128)(2,1)S(1)} %get-tuple-element.59), channel_id=1, source_target_pairs={{0,192},{16,208},{32,224},{48,240},{64,0},{80,16},{96,32},{112,48}... | collective-permute-start | bytes 480008 | tf_op jit(solution)/shard_map/ppermute | solution.py:31
  75.8 3.8 %collective-permute-start.25 = (bf16[200,200]{1,0:T(8,128)(2,1)S(1)}, bf16[200,200]{1,0:T(8,128)(2,1)S(1)}, u32[]{:S(2)}, u32[]{:S(2)}) collective-permute-start(bf16[200,200]{1,0:T(8,128)(2,1)S(1)} %get-tuple-element.60.walkers), channel_id=1, source_target_pairs={{0,1},{1,0},{2,3},{3,2},{4,5},{5,4},{6,7},{7,6},{8,9},{9,8},{10,11... | collective-permute-start | bytes 240008 | tf_op jit(solution)/shard_map/ppermute | solution.py:47
  83.1 6.1 %collective-permute-start.26 = (bf16[50,1600]{1,0:T(8,128)(2,1)S(1)}, bf16[50,1600]{1,0:T(8,128)(2,1)S(1)}, u32[]{:S(2)}, u32[]{:S(2)}) collective-permute-start(bf16[50,1600]{1,0:T(8,128)(2,1)S(1)} %get-tuple-element.62), channel_id=1, source_target_pairs={{0,8},{1,9},{2,10},{3,11},{4,16},{5,17},{6,18},{7,19},{8,0},{9,1},... | collective-permute-start | bytes 480008 | tf_op jit(solution)/shard_map/ppermute | solution.py:64
  83.8 11.9 %collective-permute-start.27 = (bf16[50,1600]{1,0:T(8,128)(2,1)S(1)}, bf16[50,1600]{1,0:T(8,128)(2,1)S(1)}, u32[]{:S(2)}, u32[]{:S(2)}) collective-permute-start(bf16[50,1600]{1,0:T(8,128)(2,1)S(1)} %get-tuple-element.61.second), channel_id=1, source_target_pairs={{4,24},{5,25},{6,26},{7,27},{12,16},{13,17},{14,18},{15,19},{16,4}... | collective-permute-start | bytes 480008 | tf_op jit(solution)/shard_map/ppermute | solution.py:64
  87.7 8.0 %collective-permute-start.28 = (bf16[400,200]{1,0:T(8,128)(2,1)S(1)}, bf16[400,200]{1,0:T(8,128)(2,1)S(1)}, u32[]{:S(2)}, u32[]{:S(2)}) collective-permute-start(bf16[400,200]{1,0:T(8,128)(2,1)S(1)} %get-tuple-element.63.near), channel_id=1, source_target_pairs={{0,2},{1,3},{2,0},{3,1},{4,6},{5,7},{6,4},{7,5},{8,10},{9,11},{10,... | collective-permute-start | bytes 480008 | tf_op jit(solution)/shard_map/ppermute | solution.py:47
  95.8 10.9 %collective-permute-start.29 = (bf16[100,1600]{1,0:T(8,128)(2,1)S(1)}, bf16[100,1600]{1,0:T(8,128)(2,1)S(1)}, u32[]{:S(2)}, u32[]{:S(2)}) collective-permute-start(bf16[100,1600]{1,0:T(8,128)(2,1)S(1)} %get-tuple-element.65), channel_id=1, source_target_pairs={{0,32},{16,48},{32,0},{48,16},{64,96},{80,112},{96,64},{112,80},{1... | collective-permute-start | bytes 960008 | tf_op jit(solution)/shard_map/ppermute | solution.py:35
  98.3 10.0 %collective-permute-start.35 = (bf16[50,1600]{1,0:T(8,128)(2,1)S(1)}, bf16[50,1600]{1,0:T(8,128)(2,1)S(1)}, u32[]{:S(2)}, u32[]{:S(2)}) collective-permute-start(bf16[50,1600]{1,0:T(8,128)(2,1)S(1)} %get-tuple-element.66.block), channel_id=1, source_target_pairs={{0,3},{1,0},{2,1},{3,2},{4,7},{5,4},{6,5},{7,6},{8,11},{9,8},{10,9... | collective-permute-start | bytes 480008 | tf_op jit(solution)/shard_map/ppermute | solution.py:43
  99.6 9.4 %collective-permute-start.34 = (bf16[50,1600]{1,0:T(8,128)(2,1)S(1)}, bf16[50,1600]{1,0:T(8,128)(2,1)S(1)}, u32[]{:S(2)}, u32[]{:S(2)}) collective-permute-start(bf16[50,1600]{1,0:T(8,128)(2,1)S(1)} %get-tuple-element.66.block), channel_id=1, source_target_pairs={{0,2},{1,3},{2,0},{3,1},{4,6},{5,7},{6,4},{7,5},{8,10},{9,11},{10,... | collective-permute-start | bytes 480008 | tf_op jit(solution)/shard_map/ppermute | solution.py:43
  100.6 10.3 %collective-permute-start.33 = (bf16[50,1600]{1,0:T(8,128)(2,1)S(1)}, bf16[50,1600]{1,0:T(8,128)(2,1)S(1)}, u32[]{:S(2)}, u32[]{:S(2)}) collective-permute-start(bf16[50,1600]{1,0:T(8,128)(2,1)S(1)} %get-tuple-element.66.block), channel_id=1, source_target_pairs={{0,1},{1,2},{2,3},{3,0},{4,5},{5,6},{6,7},{7,4},{8,9},{9,10},{10,1... | collective-permute-start | bytes 480008 | tf_op jit(solution)/shard_map/ppermute | solution.py:43
  106.7 9.6 %collective-permute-start.32 = (bf16[100,1600]{1,0:T(8,128)(2,1)S(1)}, bf16[100,1600]{1,0:T(8,128)(2,1)S(1)}, u32[]{:S(2)}, u32[]{:S(2)}) collective-permute-start(bf16[100,1600]{1,0:T(8,128)(2,1)S(1)} %stack_low.1.p0), channel_id=1, source_target_pairs={{0,3},{1,0},{2,1},{3,2},{4,7},{5,4},{6,5},{7,6},{8,11},{9,8},{10,9... | collective-permute-start | bytes 960008 | tf_op jit(solution)/shard_map/ppermute | solution.py:43
  108.3 10.7 %collective-permute-start.31 = (bf16[100,1600]{1,0:T(8,128)(2,1)S(1)}, bf16[100,1600]{1,0:T(8,128)(2,1)S(1)}, u32[]{:S(2)}, u32[]{:S(2)}) collective-permute-start(bf16[100,1600]{1,0:T(8,128)(2,1)S(1)} %stack_low.1.p0), channel_id=1, source_target_pairs={{0,2},{1,3},{2,0},{3,1},{4,6},{5,7},{6,4},{7,5},{8,10},{9,11},{10,... | collective-permute-start | bytes 960008 | tf_op jit(solution)/shard_map/ppermute | solution.py:43
  108.3 18.4 %collective-permute-start.30 = (bf16[100,1600]{1,0:T(8,128)(2,1)S(1)}, bf16[100,1600]{1,0:T(8,128)(2,1)S(1)}, u32[]{:S(2)}, u32[]{:S(2)}) collective-permute-start(bf16[100,1600]{1,0:T(8,128)(2,1)S(1)} %stack_low.1.p0), channel_id=1, source_target_pairs={{0,1},{1,2},{2,3},{3,0},{4,5},{5,6},{6,7},{7,4},{8,9},{9,10},{10,1... | collective-permute-start | bytes 960008 | tf_op jit(solution)/shard_map/ppermute | solution.py:43
  111.0 17.0 %collective-permute-start.36 = (bf16[150,1600]{1,0:T(8,128)(2,1)S(1)}, bf16[150,1600]{1,0:T(8,128)(2,1)S(1)}, u32[]{:S(2)}, u32[]{:S(2)}) collective-permute-start(bf16[150,1600]{1,0:T(8,128)(2,1)S(1)} %get-tuple-element.69.three), channel_id=1, source_target_pairs={{0,32},{16,48},{32,0},{48,16},{64,96},{80,112},{96,64},{112,80},{1... | collective-permute-start | bytes 1440008 | tf_op jit(solution)/shard_map/ppermute | solution.py:35
  127.0 2.2 %collective-permute-start.37 = (bf16[800,200]{1,0:T(8,128)(2,1)S(1)}, bf16[800,200]{1,0:T(8,128)(2,1)S(1)}, u32[]{:S(2)}, u32[]{:S(2)}) collective-permute-start(bf16[800,200]{1,0:T(8,128)(2,1)S(1)} %get-tuple-element.70.walkers), channel_id=1, source_target_pairs={{0,16},{16,0},{32,48},{48,32},{64,80},{80,64},{96,112},{112,96},{1... | collective-permute-start | bytes 960008 | tf_op jit(solution)/shard_map/ppermute | solution.py:39
  127.9 3.3 %collective-permute-start.38 = (bf16[400,1600]{1,0:T(8,128)(2,1)S(1)}, bf16[400,1600]{1,0:T(8,128)(2,1)S(1)}, u32[]{:S(2)}, u32[]{:S(2)}) collective-permute-start(bf16[400,1600]{1,0:T(8,128)(2,1)S(1)} %get-tuple-element.68.rows0), channel_id=1, source_target_pairs={{0,16},{16,0},{32,48},{48,32},{64,80},{80,64},{96,112},{112,96},{1... | collective-permute-start | bytes 3840008 | tf_op jit(solution)/shard_map/ppermute | solution.py:39
  129.8 3.3 %collective-permute-start.39 = (bf16[400,1600]{1,0:T(8,128)(2,1)S(1)}, bf16[400,1600]{1,0:T(8,128)(2,1)S(1)}, u32[]{:S(2)}, u32[]{:S(2)}) collective-permute-start(bf16[400,1600]{1,0:T(8,128)(2,1)S(1)} %get-tuple-element.71.rows1), channel_id=1, source_target_pairs={{0,16},{16,0},{32,48},{48,32},{64,80},{80,64},{96,112},{112,96},{1... | collective-permute-start | bytes 3840008 | tf_op jit(solution)/shard_map/ppermute | solution.py:39
  142.7 8.7 %collective-permute-start.40 = (bf16[200,100]{1,0:T(8,128)(2,1)S(1)}, bf16[200,100]{1,0:T(8,128)(2,1)S(1)}, u32[]{:S(2)}, u32[]{:S(2)}) collective-permute-start(bf16[200,100]{1,0:T(8,128)(2,1)S(1)} %taylor.1), channel_id=1, source_target_pairs={{0,0},{1,1},{2,2},{3,3},{4,16},{5,17},{6,18},{7,19},{8,32},{9,33},... | collective-permute-start | bytes 120008 | tf_op jit(solution)/shard_map/ppermute | solution.py:64

commit v4 on v3

--- a/solution.py
+++ b/solution.py
@@ -109,8 +109,8 @@
     out_ref[1 - at[0]] = partner[...]
 
 
-def sum_kernel(b0, b1, b2, b3, out_ref):
-    out_ref[...] = (b0[...] + b2[...]) + (b1[...] + b3[...])
+def sum_kernel(mine, arrived, out_ref):
+    out_ref[...] = mine[...] + arrived[...]
 
 
 def write_fields(at, shifted, swapped, out_ref):
@@ -444,8 +444,8 @@
     )(*met, swap_core(factor), factor, aux_fields, other)
     near = swap_core(other)
     aux_other = swap_core(aux_here)
-    from_y = [bias] + [send_y(bias, step) for step in range(1, NY)]
-    bias = call(sum_kernel, shaped(bias.shape, f32), tuple(from_y), "sum_y")
+    for bit in (1, 2):
+        bias = call(sum_kernel, shaped(bias.shape, f32), (bias, flip_y(bias, bit)), "sum_y")
     from_h = [bias] + [send_h(bias, step) for step in range(1, NH)]
 
     piece, two, quad = [shaped((n * half, orbitals), bf16) for n in (1, 2, 4)]

time: 152 us -> 153 us (level); the launches traced: 152 us -> 151 us
  waiting for transfers between devices: 69.3 us -> 62.1 us
  starting transfers between devices: 60.7 us -> 67.1 us
    ppermute x2 -> x4, starting transfers between devices: 0.33 us -> 7.15 us  [flip_y(): lax.ppermute(array, 'pair', [(h * NY + y, h * NY + (y ^ bit)) for h in ra...]
    ppermute x9, waiting for transfers between devices: 14.1 us -> 9.36 us  [send_x(): lax.ppermute(array, 'vec', [(vec_of(*p), vec_of(p[0] + step, p[1], p[2]))...]
    ppermute x9 -> x6, starting transfers between devices: 8.96 us -> 5.07 us  [send_y(): lax.ppermute(array, 'pair', [(h * NY + y, h * NY + (y + step) % NY) for h...]
    ppermute x8, starting transfers between devices: 10.6 us -> 12.9 us  [swap_core(): lax.ppermute(array, 'vec', [(vec_of(*p), vec_of(p[0], p[1], 1 - p[2])) fo...]
    ppermute x9 -> x6, waiting for transfers between devices: 18.3 us -> 16.4 us  [send_y(): lax.ppermute(array, 'pair', [(h * NY + y, h * NY + (y + step) % NY) for h...]
    ppermute x2 -> x4, waiting for transfers between devices: 3.8 us -> 3.67 us  [flip_y(): lax.ppermute(array, 'pair', [(h * NY + y, h * NY + (y ^ bit)) for h in ra...]
    pallas_call x14 -> x15, Pallas kernels: 16.3 us -> 16.3 us  [call(): pl.pallas_call(kernel, out_shape=outs, in_specs=specs, out_specs=[VMEM] *...]
  transfers between devices with their start and end apart: 41 -> 40, of which waited for: 25 -> 24; matrix products, arithmetic and copies ran while one was open for 0% -> 0% of each run, Pallas kernels for 1% -> 2%
where the time goes in v4:
time: 153 us; the launch traced here: 151 us
  starting transfers between devices  67.1 us (44%)
  waiting for transfers between devices  62.1 us (41%)
  Pallas kernels  17.8 us (12%)
  local copies, waits for them, and re-layouts  3.45 us (2%)
    ppermute x6, waiting for transfers between devices, send_y(): lax.ppermute(array, 'pair', [(h * NY + y, h * NY + (y + step) % NY) for h...  16.4 us
    pallas_call x15, Pallas kernels, call(): pl.pallas_call(kernel, out_shape=outs, in_specs=specs, out_specs=[VMEM] *...  16.3 us
    ppermute x4, starting transfers between devices, everywhere(): return lax.ppermute(array, ('vec', 'pair'), pairs)  15.5 us
    ppermute x4, waiting for transfers between devices, everywhere(): return lax.ppermute(array, ('vec', 'pair'), pairs)  14.9 us
    ppermute x9, starting transfers between devices, send_x(): lax.ppermute(array, 'vec', [(vec_of(*p), vec_of(p[0] + step, p[1], p[2]))...  14.7 us
    ppermute x8, starting transfers between devices, swap_core(): lax.ppermute(array, 'vec', [(vec_of(*p), vec_of(p[0], p[1], 1 - p[2])) fo...  12.9 us
    ppermute x9, waiting for transfers between devices, send_x(): lax.ppermute(array, 'vec', [(vec_of(*p), vec_of(p[0] + step, p[1], p[2]))...  9.36 us
    ppermute x6, starting transfers between devices, swap_low(): lax.ppermute(array, 'vec', [(vec_of(*p), vec_of(p[0], 1 - p[1], p[2])) fo...  7.95 us
  transfers between devices with their start and end apart: 40, of which 24 were waited for; matrix products, arithmetic and copies ran while one was open for 0% of the time, Pallas kernels for 2%

profile of v4, /device:TPU:33, one launch (start us, length us, event | category | flops | bytes accessed | tf_op | source)
XLA Modules:
  0.0 151.3 jit_solution(4621506768567270510)
XLA Ops:
  0.6 0.8 collective-permute-start.4
  1.4 0.9 copy-done.1
  2.3 0.8 copy-done.2
  3.4 1.7 %collective-permute-start = (bf16[112,200]{1,0:T(8,128)(2,1)S(1)}, bf16[112,200]{1,0:T(8,128)(2,1)S(1)}, u32[]{:S(2)}, u32[]{:S(2)}) collective-permute-start(bf16[112,200]{1,0:T(8,128)(2,1)S(1)} %rotate.1.rotated), channel_id=1, source_target_pairs={{0,32},{16,48},{32,0},{48,16},{64,96},{80,112},{96,64},{112,80},{1... | collective-permute-start | bytes 134408 | tf_op jit(solution)/shard_map/ppermute | solution.py:35
  5.1 2.2 %collective-permute-done.partner = bf16[112,200]{1,0:T(8,128)(2,1)S(1)} collective-permute-done((bf16[112,200]{1,0:T(8,128)(2,1)S(1)}, bf16[112,200]{1,0:T(8,128)(2,1)S(1)}, u32[]{:S(2)}, u32[]{:S(2)}) %collective-permute-start) | collective-permute-done | bytes 44832 | tf_op jit(solution)/shard_map/ppermute | solution.py:35
  7.3 1.1 copy-done
  8.4 1.1 collective-permute-start.3
  9.5 2.5 %collective-permute-start.2 = (bf16[2,112,200]{2,1,0:T(8,128)(2,1)S(1)}, bf16[2,112,200]{2,1,0:T(8,128)(2,1)S(1)}, u32[]{:S(2)}, u32[]{:S(2)}) collective-permute-start(bf16[2,112,200]{2,1,0:T(8,128)(2,1)S(1)} %get-tuple-element.39.r0), channel_id=1, source_target_pairs={{0,128},{16,144},{32,160},{48,176},{64,192},{80,208},{96,224},{112... | collective-permute-start | bytes 268808 | tf_op jit(solution)/shard_map/ppermute | solution.py:31
  11.9 1.2 collective-permute-start.1
  13.1 0.6 collective-permute-done.3.a3.r3
  13.7 2.8 %collective-permute-done.2.a2.r2 = bf16[2,112,200]{2,1,0:T(8,128)(2,1)S(1)} collective-permute-done((bf16[2,112,200]{2,1,0:T(8,128)(2,1)S(1)}, bf16[2,112,200]{2,1,0:T(8,128)(2,1)S(1)}, u32[]{:S(2)}, u32[]{:S(2)}) %collective-permute-start.2) | collective-permute-done | bytes 89632 | tf_op jit(solution)/shard_map/ppermute | solution.py:31
  17.1 1.7 %vector_factor.1.other = bf16[100,16,200]{2,1,0:T(8,128)(2,1)S(1)} custom-call(bf16[200,1600]{1,0:T(8,128)(2,1)S(1)} %get-tuple-element.40.trial, bf16[100,16,1600]{2,1,0:T(8,128)(2,1)S(1)} %collective-permute-done.4.block.passed, bf16[2,112,200]{2,1,0:T(8,128)(2,1)S(1)} %collective-permute-done.1.a1.r1, ...), custom_call_target="tpu_custom_call" | custom-call | tf_op jit(solution)/shard_map/vector_factor/pallas_call | solution.py:394
  18.8 1.5 collective-permute-start.5
  20.3 2.0 %collective-permute-done.5.own = bf16[100,16,200]{2,1,0:T(8,128)(2,1)S(1)} collective-permute-done((bf16[100,16,200]{2,1,0:T(8,128)(2,1)S(1)}, bf16[100,16,200]{2,1,0:T(8,128)(2,1)S(1)}, u32[]{:S(2)}, u32[]{:S(2)}) %collective-permute-start.5) | collective-permute-done | bytes 640032 | tf_op jit(solution)/shard_map/ppermute | solution.py:39
  22.3 1.5 force_bias.1
  24.2 7.5 %collective-permute-start.12 = (bf16[200,100]{1,0:T(8,128)(2,1)S(1)}, bf16[200,100]{1,0:T(8,128)(2,1)S(1)}, u32[]{:S(2)}, u32[]{:S(2)}) collective-permute-start(bf16[200,100]{1,0:T(8,128)(2,1)S(1)} %bitcast.12), channel_id=1, source_target_pairs={{0,0},{1,1},{2,2},{3,3},{4,16},{5,17},{6,18},{7,19},{8,32},{9,33},... | collective-permute-start | bytes 120008 | tf_op jit(solution)/shard_map/ppermute | solution.py:64
  31.7 1.4 collective-permute-start.6
  33.1 1.2 collective-permute-done.6.arrived
  34.2 2.9 %collective-permute-start.7 = (f32[8,32]{1,0:T(8,128)S(1)}, f32[8,32]{1,0:T(8,128)S(1)}, u32[]{:S(2)}, u32[]{:S(2)}) collective-permute-start(f32[8,32]{1,0:T(8,128)S(1)} %sum_y.2.mine), channel_id=1, source_target_pairs={{0,2},{1,3},{2,0},{3,1},{4,6},{5,7},{6,4},{7,5},{8,10},{9,11},{10,... | collective-permute-start | bytes 3080 | tf_op jit(solution)/shard_map/ppermute | solution.py:47
  37.1 1.8 %collective-permute-start.11 = (f32[16,16]{1,0:T(8,128)S(1)}, f32[16,16]{1,0:T(8,128)S(1)}, u32[]{:S(2)}, u32[]{:S(2)}) collective-permute-start(f32[16,16]{1,0:T(8,128)S(1)} %get-tuple-element.42), channel_id=1, source_target_pairs={{0,16},{16,0},{32,48},{48,32},{64,80},{80,64},{96,112},{112,96},{1... | collective-permute-start | bytes 3080 | tf_op jit(solution)/shard_map/ppermute | solution.py:39
  39.0 0.7 collective-permute-start.10
  39.7 3.2 %collective-permute-start.9 = (f32[8,32]{1,0:T(8,128)S(1)}, f32[8,32]{1,0:T(8,128)S(1)}, u32[]{:S(2)}, u32[]{:S(2)}) collective-permute-start(f32[8,32]{1,0:T(8,128)S(1)} %sum_y.3.b0), channel_id=1, source_target_pairs={{0,8},{1,9},{2,10},{3,11},{4,12},{5,13},{6,14},{7,15},{8,0},{9,1},... | collective-permute-start | bytes 3080 | tf_op jit(solution)/shard_map/ppermute | solution.py:51
  42.9 3.1 %collective-permute-done.9.b2 = f32[8,32]{1,0:T(8,128)S(1)} collective-permute-done((f32[8,32]{1,0:T(8,128)S(1)}, f32[8,32]{1,0:T(8,128)S(1)}, u32[]{:S(2)}, u32[]{:S(2)}) %collective-permute-start.9) | collective-permute-done | bytes 1056 | tf_op jit(solution)/shard_map/ppermute | solution.py:51
  46.0 1.4 collective-permute-done.8.b1
  47.5 2.5 %field_operator.1 = (f32[8,32]{1,0:T(8,128)S(1)}, f32[8,16]{1,0:T(8,128)S(1)}, bf16[100,1600]{1,0:T(8,128)(2,1)S(1)}, bf16[100,1600]{1,0:T(8,128)(2,1)S(1)}, bf1...) custom-call(f32[8,32]{1,0:T(8,128)S(1)} %sum_y.3.b0, ...), custom_call_target="tpu_custom_call" | custom-call | tf_op jit(solution)/shard_map/field_operator/pallas_call | solution.py:394
  50.0 1.1 collective-permute-start.14
  51.1 2.4 %collective-permute-start.15 = (bf16[100,1600]{1,0:T(8,128)(2,1)S(1)}, bf16[100,1600]{1,0:T(8,128)(2,1)S(1)}, u32[]{:S(2)}, u32[]{:S(2)}) collective-permute-start(bf16[100,1600]{1,0:T(8,128)(2,1)S(1)} %get-tuple-element.46), channel_id=1, source_target_pairs={{0,128},{16,144},{32,160},{48,176},{64,192},{80,208},{96,224},{112... | collective-permute-start | bytes 960008 | tf_op jit(solution)/shard_map/ppermute | solution.py:31
  53.6 1.0 collective-permute-start.16
  54.5 1.4 collective-permute-start.20
  55.9 1.5 %collective-permute-done.14.p1 = bf16[100,1600]{1,0:T(8,128)(2,1)S(1)} collective-permute-done((bf16[100,1600]{1,0:T(8,128)(2,1)S(1)}, bf16[100,1600]{1,0:T(8,128)(2,1)S(1)}, u32[]{:S(2)}, u32[]{:S(2)}) %collective-permute-start.14) | collective-permute-done | bytes 320032 | tf_op jit(solution)/shard_map/ppermute | solution.py:31
  57.4 7.4 %collective-permute-start.19 = (f32[8,16]{1,0:T(8,128)S(1)}, f32[8,16]{1,0:T(8,128)S(1)}, u32[]{:S(2)}, u32[]{:S(2)}) collective-permute-start(f32[8,16]{1,0:T(8,128)S(1)} %get-tuple-element.54), channel_id=1, source_target_pairs={{0,16},{16,0},{32,48},{48,32},{64,80},{80,64},{96,112},{112,96},{1... | collective-permute-start | bytes 1544 | tf_op jit(solution)/shard_map/ppermute | solution.py:39
  64.8 0.8 collective-permute-done.15.p2
  65.6 1.6 %collective-permute-done.16.p3 = bf16[100,1600]{1,0:T(8,128)(2,1)S(1)} collective-permute-done((bf16[100,1600]{1,0:T(8,128)(2,1)S(1)}, bf16[100,1600]{1,0:T(8,128)(2,1)S(1)}, u32[]{:S(2)}, u32[]{:S(2)}) %collective-permute-start.16) | collective-permute-done | bytes 320032 | tf_op jit(solution)/shard_map/ppermute | solution.py:31
  67.3 1.2 collective-permute-start.17
  68.5 0.7 pair_sum.1
  69.2 3.1 %collective-permute-start.21 = (bf16[50,1600]{1,0:T(8,128)(2,1)S(1)}, bf16[50,1600]{1,0:T(8,128)(2,1)S(1)}, u32[]{:S(2)}, u32[]{:S(2)}) collective-permute-start(bf16[50,1600]{1,0:T(8,128)(2,1)S(1)} %get-tuple-element.57), channel_id=1, source_target_pairs={{0,64},{16,80},{32,96},{48,112},{64,128},{80,144},{96,160},{112,17... | collective-permute-start | bytes 480008 | tf_op jit(solution)/shard_map/ppermute | solution.py:31
  72.3 1.5 collective-permute-start.22
  73.8 0.9 collective-permute-start.23
  74.7 1.3 collective-permute-start.24
  76.0 2.5 %collective-permute-done.24.partners = bf16[200,200]{1,0:T(8,128)(2,1)S(1)} collective-permute-done((bf16[200,200]{1,0:T(8,128)(2,1)S(1)}, bf16[200,200]{1,0:T(8,128)(2,1)S(1)}, u32[]{:S(2)}, u32[]{:S(2)}) %collective-permute-start.24) | collective-permute-done | bytes 80032 | tf_op jit(solution)/shard_map/ppermute | solution.py:47
  78.5 1.5 collective-permute-done.22.q2
  80.3 4.1 %collective-permute-start.25 = (bf16[50,1600]{1,0:T(8,128)(2,1)S(1)}, bf16[50,1600]{1,0:T(8,128)(2,1)S(1)}, u32[]{:S(2)}, u32[]{:S(2)}) collective-permute-start(bf16[50,1600]{1,0:T(8,128)(2,1)S(1)} %get-tuple-element.62), channel_id=1, source_target_pairs={{0,8},{1,9},{2,10},{3,11},{4,16},{5,17},{6,18},{7,19},{8,0},{9,1},... | collective-permute-start | bytes 480008 | tf_op jit(solution)/shard_map/ppermute | solution.py:64
  84.4 1.9 %collective-permute-start.26 = (bf16[50,1600]{1,0:T(8,128)(2,1)S(1)}, bf16[50,1600]{1,0:T(8,128)(2,1)S(1)}, u32[]{:S(2)}, u32[]{:S(2)}) collective-permute-start(bf16[50,1600]{1,0:T(8,128)(2,1)S(1)} %get-tuple-element.61.second), channel_id=1, source_target_pairs={{4,24},{5,25},{6,26},{7,27},{12,16},{13,17},{14,18},{15,19},{16,4}... | collective-permute-start | bytes 480008 | tf_op jit(solution)/shard_map/ppermute | solution.py:64
  86.3 1.6 %collective-permute-start.27 = (bf16[400,200]{1,0:T(8,128)(2,1)S(1)}, bf16[400,200]{1,0:T(8,128)(2,1)S(1)}, u32[]{:S(2)}, u32[]{:S(2)}) collective-permute-start(bf16[400,200]{1,0:T(8,128)(2,1)S(1)} %get-tuple-element.63.near), channel_id=1, source_target_pairs={{0,2},{1,3},{2,0},{3,1},{4,6},{5,7},{6,4},{7,5},{8,10},{9,11},{10,... | collective-permute-start | bytes 480008 | tf_op jit(solution)/shard_map/ppermute | solution.py:47
  87.9 2.8 %collective-permute-done.25.got = bf16[50,1600]{1,0:T(8,128)(2,1)S(1)} collective-permute-done((bf16[50,1600]{1,0:T(8,128)(2,1)S(1)}, bf16[50,1600]{1,0:T(8,128)(2,1)S(1)}, u32[]{:S(2)}, u32[]{:S(2)}) %collective-permute-start.25) | collective-permute-done | bytes 160032 | tf_op jit(solution)/shard_map/ppermute | solution.py:64
  90.7 5.3 %collective-permute-done.26.more = bf16[50,1600]{1,0:T(8,128)(2,1)S(1)} collective-permute-done((bf16[50,1600]{1,0:T(8,128)(2,1)S(1)}, bf16[50,1600]{1,0:T(8,128)(2,1)S(1)}, u32[]{:S(2)}, u32[]{:S(2)}) %collective-permute-start.26) | collective-permute-done | bytes 160032 | tf_op jit(solution)/shard_map/ppermute | solution.py:64
  96.0 2.5 %collective-permute-start.28 = (bf16[100,1600]{1,0:T(8,128)(2,1)S(1)}, bf16[100,1600]{1,0:T(8,128)(2,1)S(1)}, u32[]{:S(2)}, u32[]{:S(2)}) collective-permute-start(bf16[100,1600]{1,0:T(8,128)(2,1)S(1)} %get-tuple-element.65), channel_id=1, source_target_pairs={{0,32},{16,48},{32,0},{48,16},{64,96},{80,112},{96,64},{112,80},{1... | collective-permute-start | bytes 960008 | tf_op jit(solution)/shard_map/ppermute | solution.py:35
  98.5 1.6 %collective-permute-start.34 = (bf16[50,1600]{1,0:T(8,128)(2,1)S(1)}, bf16[50,1600]{1,0:T(8,128)(2,1)S(1)}, u32[]{:S(2)}, u32[]{:S(2)}) collective-permute-start(bf16[50,1600]{1,0:T(8,128)(2,1)S(1)} %get-tuple-element.66.block), channel_id=1, source_target_pairs={{0,3},{1,0},{2,1},{3,2},{4,7},{5,4},{6,5},{7,6},{8,11},{9,8},{10,9... | collective-permute-start | bytes 480008 | tf_op jit(solution)/shard_map/ppermute | solution.py:43
  100.5 0.7 collective-permute-start.32
  101.2 5.0 %collective-permute-done.28.partners.low_blocks = bf16[100,1600]{1,0:T(8,128)(2,1)S(1)} collective-permute-done((bf16[100,1600]{1,0:T(8,128)(2,1)S(1)}, bf16[100,1600]{1,0:T(8,128)(2,1)S(1)}, u32[]{:S(2)}, u32[]{:S(2)}) %collective-permute-start.28) | collective-permute-done | bytes 320032 | tf_op jit(solution)/shard_map/ppermute | solution.py:35
  106.2 1.4 collective-permute-start.31
  107.9 0.7 collective-permute-start.29
  108.6 2.0 %collective-permute-done.32.b1 = bf16[50,1600]{1,0:T(8,128)(2,1)S(1)} collective-permute-done((bf16[50,1600]{1,0:T(8,128)(2,1)S(1)}, bf16[50,1600]{1,0:T(8,128)(2,1)S(1)}, u32[]{:S(2)}, u32[]{:S(2)}) %collective-permute-start.32) | collective-permute-done | bytes 160032 | tf_op jit(solution)/shard_map/ppermute | solution.py:43
  110.7 1.2 collective-permute-start.35
  111.9 4.5 %collective-permute-done.31.p3 = bf16[100,1600]{1,0:T(8,128)(2,1)S(1)} collective-permute-done((bf16[100,1600]{1,0:T(8,128)(2,1)S(1)}, bf16[100,1600]{1,0:T(8,128)(2,1)S(1)}, u32[]{:S(2)}, u32[]{:S(2)}) %collective-permute-start.31) | collective-permute-done | bytes 320032 | tf_op jit(solution)/shard_map/ppermute | solution.py:43
  116.4 2.5 %collective-permute-done.30.p2 = bf16[100,1600]{1,0:T(8,128)(2,1)S(1)} collective-permute-done((bf16[100,1600]{1,0:T(8,128)(2,1)S(1)}, bf16[100,1600]{1,0:T(8,128)(2,1)S(1)}, u32[]{:S(2)}, u32[]{:S(2)}) %collective-permute-start.30) | collective-permute-done | bytes 320032 | tf_op jit(solution)/shard_map/ppermute | solution.py:43
  118.9 7.4 %collective-permute-done.29.p1 = bf16[100,1600]{1,0:T(8,128)(2,1)S(1)} collective-permute-done((bf16[100,1600]{1,0:T(8,128)(2,1)S(1)}, bf16[100,1600]{1,0:T(8,128)(2,1)S(1)}, u32[]{:S(2)}, u32[]{:S(2)}) %collective-permute-start.29) | collective-permute-done | bytes 320032 | tf_op jit(solution)/shard_map/ppermute | solution.py:43
  127.3 1.3 collective-permute-done.36.swapped
  129.6 0.9 collective-permute-done.37.other0
  130.5 1.9 %collective-permute-done.38.other1 = bf16[400,1600]{1,0:T(8,128)(2,1)S(1)} collective-permute-done((bf16[400,1600]{1,0:T(8,128)(2,1)S(1)}, bf16[400,1600]{1,0:T(8,128)(2,1)S(1)}, u32[]{:S(2)}, u32[]{:S(2)}) %collective-permute-start.38) | collective-permute-done | bytes 1280032 | tf_op jit(solution)/shard_map/ppermute | solution.py:39
  132.4 9.6 %taylor.1 = bf16[200,100]{1,0:T(8,128)(2,1)S(1)} custom-call(bf16[400,1600]{1,0:T(8,128)(2,1)S(1)} %get-tuple-element.68.rows0, bf16[400,1600]{1,0:T(8,128)(2,1)S(1)} %get-tuple-element.71.rows1, bf16[400,1600]{1,0:T(8,128)(2,1)S(1)} %collective-permute-done.37.other0, bf16[400,1600]{1,0:T(8,128)(2,1)S(1)} %collective-permute-done.38.other1, ...), custom_call_target="tpu_custom_call" | custom-call | tf_op jit(solution)/shard_map/taylor/pallas_call | solution.py:394
  141.9 1.9 %collective-permute-start.39 = (bf16[200,100]{1,0:T(8,128)(2,1)S(1)}, bf16[200,100]{1,0:T(8,128)(2,1)S(1)}, u32[]{:S(2)}, u32[]{:S(2)}) collective-permute-start(bf16[200,100]{1,0:T(8,128)(2,1)S(1)} %taylor.1), channel_id=1, source_target_pairs={{0,0},{1,1},{2,2},{3,3},{4,16},{5,17},{6,18},{7,19},{8,32},{9,33},... | collective-permute-start | bytes 120008 | tf_op jit(solution)/shard_map/ppermute | solution.py:64
  143.9 6.8 %collective-permute-done.39 = bf16[200,100]{1,0:T(8,128)(2,1)S(1)} collective-permute-done((bf16[200,100]{1,0:T(8,128)(2,1)S(1)}, bf16[200,100]{1,0:T(8,128)(2,1)S(1)}, u32[]{:S(2)}, u32[]{:S(2)}) %collective-permute-start.39) | collective-permute-done | bytes 40032 | tf_op jit(solution)/shard_map/ppermute | solution.py:64
  150.7 0.6 copy.10
  (43 shorter events, 4.8 us)
Async XLA Ops:
  0.6 16.5 %collective-permute-start.4 = (bf16[100,16,1600]{2,1,0:T(8,128)(2,1)}, bf16[100,16,1600]{2,1,0:T(8,128)(2,1)S(1)}, u32[]{:S(2)}, u32[]{:S(2)}) collective-permute-start(bf16[100,16,1600]{2,1,0:T(8,128)(2,1)} %bitcast.14), channel_id=1, source_target_pairs={{0,16},{16,0},{32,48},{48,32},{64,80},{80,64},{96,112},{112,96},{1... | collective-permute-start | bytes 15360008 | tf_op jit(solution)/shard_map/ppermute | solution.py:39
  1.4 0.9 copy-start.1
  2.3 0.8 copy-start.2
  3.1 19.1 %copy-start.4 = (f32[16,16]{1,0:T(8,128)S(1)}, f32[16,16]{1,0:T(8,128)}, u32[]{:S(2)}) copy-start(f32[16,16]{1,0:T(8,128)} %aux.3) | copy-start | bytes 3076
  3.4 3.9 %collective-permute-start = (bf16[112,200]{1,0:T(8,128)(2,1)S(1)}, bf16[112,200]{1,0:T(8,128)(2,1)S(1)}, u32[]{:S(2)}, u32[]{:S(2)}) collective-permute-start(bf16[112,200]{1,0:T(8,128)(2,1)S(1)} %rotate.1.rotated), channel_id=1, source_target_pairs={{0,32},{16,48},{32,0},{48,16},{64,96},{80,112},{96,64},{112,80},{1... | collective-permute-start | bytes 134408 | tf_op jit(solution)/shard_map/ppermute | solution.py:35
  7.3 1.1 copy-start
  8.4 5.3 %collective-permute-start.3 = (bf16[2,112,200]{2,1,0:T(8,128)(2,1)S(1)}, bf16[2,112,200]{2,1,0:T(8,128)(2,1)S(1)}, u32[]{:S(2)}, u32[]{:S(2)}) collective-permute-start(bf16[2,112,200]{2,1,0:T(8,128)(2,1)S(1)} %get-tuple-element.39.r0), channel_id=1, source_target_pairs={{0,64},{16,80},{32,96},{48,112},{64,128},{80,144},{96,160},{112,17... | collective-permute-start | bytes 268808 | tf_op jit(solution)/shard_map/ppermute | solution.py:31
  9.5 7.0 %collective-permute-start.2 = (bf16[2,112,200]{2,1,0:T(8,128)(2,1)S(1)}, bf16[2,112,200]{2,1,0:T(8,128)(2,1)S(1)}, u32[]{:S(2)}, u32[]{:S(2)}) collective-permute-start(bf16[2,112,200]{2,1,0:T(8,128)(2,1)S(1)} %get-tuple-element.39.r0), channel_id=1, source_target_pairs={{0,128},{16,144},{32,160},{48,176},{64,192},{80,208},{96,224},{112... | collective-permute-start | bytes 268808 | tf_op jit(solution)/shard_map/ppermute | solution.py:31
  11.9 5.2 %collective-permute-start.1 = (bf16[2,112,200]{2,1,0:T(8,128)(2,1)S(1)}, bf16[2,112,200]{2,1,0:T(8,128)(2,1)S(1)}, u32[]{:S(2)}, u32[]{:S(2)}) collective-permute-start(bf16[2,112,200]{2,1,0:T(8,128)(2,1)S(1)} %get-tuple-element.39.r0), channel_id=1, source_target_pairs={{0,192},{16,208},{32,224},{48,240},{64,0},{80,16},{96,32},{112,48}... | collective-permute-start | bytes 268808 | tf_op jit(solution)/shard_map/ppermute | solution.py:31
  18.8 5.4 %copy-start.3 = (bf16[1,100,200]{1,2,0:T(8,128)(2,1)S(1)}, bf16[1,100,200]{1,2,0:T(8,128)(2,1)}, u32[]{:S(2)}) copy-start(bf16[1,100,200]{1,2,0:T(8,128)(2,1)} %param.6) | copy-start | bytes 120004
  18.8 3.4 %collective-permute-start.5 = (bf16[100,16,200]{2,1,0:T(8,128)(2,1)S(1)}, bf16[100,16,200]{2,1,0:T(8,128)(2,1)S(1)}, u32[]{:S(2)}, u32[]{:S(2)}) collective-permute-start(bf16[100,16,200]{2,1,0:T(8,128)(2,1)S(1)} %vector_factor.1.other), channel_id=1, source_target_pairs={{0,16},{16,0},{32,48},{48,32},{64,80},{80,64},{96,112},{112,96},{1... | collective-permute-start | bytes 1920008 | tf_op jit(solution)/shard_map/ppermute | solution.py:39
  23.8 23.7 %collective-permute-start.13 = (bf16[100,16,1600]{2,1,0:T(8,128)(2,1)S(1)}, bf16[100,16,1600]{2,1,0:T(8,128)(2,1)S(1)}, u32[]{:S(2)}, u32[]{:S(2)}) collective-permute-start(bf16[100,16,1600]{2,1,0:T(8,128)(2,1)S(1)} %get-tuple-element.43.other), channel_id=1, source_target_pairs={{0,16},{16,0},{32,48},{48,32},{64,80},{80,64},{96,112},{112,96},{1... | collective-permute-start | bytes 15360008 | tf_op jit(solution)/shard_map/ppermute | solution.py:39
  24.2 18.7 %collective-permute-start.12 = (bf16[200,100]{1,0:T(8,128)(2,1)S(1)}, bf16[200,100]{1,0:T(8,128)(2,1)S(1)}, u32[]{:S(2)}, u32[]{:S(2)}) collective-permute-start(bf16[200,100]{1,0:T(8,128)(2,1)S(1)} %bitcast.12), channel_id=1, source_target_pairs={{0,0},{1,1},{2,2},{3,3},{4,16},{5,17},{6,18},{7,19},{8,32},{9,33},... | collective-permute-start | bytes 120008 | tf_op jit(solution)/shard_map/ppermute | solution.py:64
  31.7 2.5 %collective-permute-start.6 = (f32[8,32]{1,0:T(8,128)S(1)}, f32[8,32]{1,0:T(8,128)S(1)}, u32[]{:S(2)}, u32[]{:S(2)}) collective-permute-start(f32[8,32]{1,0:T(8,128)S(1)} %get-tuple-element.41.mine), channel_id=1, source_target_pairs={{0,1},{1,0},{2,3},{3,2},{4,5},{5,4},{6,7},{7,6},{8,9},{9,8},{10,11... | collective-permute-start | bytes 3080 | tf_op jit(solution)/shard_map/ppermute | solution.py:47
  34.2 4.7 %collective-permute-start.7 = (f32[8,32]{1,0:T(8,128)S(1)}, f32[8,32]{1,0:T(8,128)S(1)}, u32[]{:S(2)}, u32[]{:S(2)}) collective-permute-start(f32[8,32]{1,0:T(8,128)S(1)} %sum_y.2.mine), channel_id=1, source_target_pairs={{0,2},{1,3},{2,0},{3,1},{4,6},{5,7},{6,4},{7,5},{8,10},{9,11},{10,... | collective-permute-start | bytes 3080 | tf_op jit(solution)/shard_map/ppermute | solution.py:47
  37.1 5.7 %collective-permute-start.11 = (f32[16,16]{1,0:T(8,128)S(1)}, f32[16,16]{1,0:T(8,128)S(1)}, u32[]{:S(2)}, u32[]{:S(2)}) collective-permute-start(f32[16,16]{1,0:T(8,128)S(1)} %get-tuple-element.42), channel_id=1, source_target_pairs={{0,16},{16,0},{32,48},{48,32},{64,80},{80,64},{96,112},{112,96},{1... | collective-permute-start | bytes 3080 | tf_op jit(solution)/shard_map/ppermute | solution.py:39
  39.0 3.9 %collective-permute-start.10 = (f32[8,32]{1,0:T(8,128)S(1)}, f32[8,32]{1,0:T(8,128)S(1)}, u32[]{:S(2)}, u32[]{:S(2)}) collective-permute-start(f32[8,32]{1,0:T(8,128)S(1)} %sum_y.3.b0), channel_id=1, source_target_pairs={{0,12},{1,13},{2,14},{3,15},{4,0},{5,1},{6,2},{7,3},{8,4},{9,5},{1... | collective-permute-start | bytes 3080 | tf_op jit(solution)/shard_map/ppermute | solution.py:51
  39.7 6.4 %collective-permute-start.9 = (f32[8,32]{1,0:T(8,128)S(1)}, f32[8,32]{1,0:T(8,128)S(1)}, u32[]{:S(2)}, u32[]{:S(2)}) collective-permute-start(f32[8,32]{1,0:T(8,128)S(1)} %sum_y.3.b0), channel_id=1, source_target_pairs={{0,8},{1,9},{2,10},{3,11},{4,12},{5,13},{6,14},{7,15},{8,0},{9,1},... | collective-permute-start | bytes 3080 | tf_op jit(solution)/shard_map/ppermute | solution.py:51
  42.9 4.6 %collective-permute-start.8 = (f32[8,32]{1,0:T(8,128)S(1)}, f32[8,32]{1,0:T(8,128)S(1)}, u32[]{:S(2)}, u32[]{:S(2)}) collective-permute-start(f32[8,32]{1,0:T(8,128)S(1)} %sum_y.3.b0), channel_id=1, source_target_pairs={{0,4},{1,5},{2,6},{3,7},{4,8},{5,9},{6,10},{7,11},{8,12},{9,13},{1... | collective-permute-start | bytes 3080 | tf_op jit(solution)/shard_map/ppermute | solution.py:51
  49.9 18.6 %collective-permute-start.18 = (bf16[224,1600]{1,0:T(8,128)(2,1)S(1)}, bf16[224,1600]{1,0:T(8,128)(2,1)S(1)}, u32[]{:S(2)}, u32[]{:S(2)}) collective-permute-start(bf16[224,1600]{1,0:T(8,128)(2,1)S(1)} %get-tuple-element.52), channel_id=1, source_target_pairs={{0,32},{16,48},{32,0},{48,16},{64,96},{80,112},{96,64},{112,80},{1... | collective-permute-start | bytes 2150408 | tf_op jit(solution)/shard_map/ppermute | solution.py:35
  50.0 7.4 %collective-permute-start.14 = (bf16[100,1600]{1,0:T(8,128)(2,1)S(1)}, bf16[100,1600]{1,0:T(8,128)(2,1)S(1)}, u32[]{:S(2)}, u32[]{:S(2)}) collective-permute-start(bf16[100,1600]{1,0:T(8,128)(2,1)S(1)} %get-tuple-element.45), channel_id=1, source_target_pairs={{0,64},{16,80},{32,96},{48,112},{64,128},{80,144},{96,160},{112,17... | collective-permute-start | bytes 960008 | tf_op jit(solution)/shard_map/ppermute | solution.py:31
  51.1 14.4 %collective-permute-start.15 = (bf16[100,1600]{1,0:T(8,128)(2,1)S(1)}, bf16[100,1600]{1,0:T(8,128)(2,1)S(1)}, u32[]{:S(2)}, u32[]{:S(2)}) collective-permute-start(bf16[100,1600]{1,0:T(8,128)(2,1)S(1)} %get-tuple-element.46), channel_id=1, source_target_pairs={{0,128},{16,144},{32,160},{48,176},{64,192},{80,208},{96,224},{112... | collective-permute-start | bytes 960008 | tf_op jit(solution)/shard_map/ppermute | solution.py:31
  53.6 13.6 %collective-permute-start.16 = (bf16[100,1600]{1,0:T(8,128)(2,1)S(1)}, bf16[100,1600]{1,0:T(8,128)(2,1)S(1)}, u32[]{:S(2)}, u32[]{:S(2)}) collective-permute-start(bf16[100,1600]{1,0:T(8,128)(2,1)S(1)} %get-tuple-element.47), channel_id=1, source_target_pairs={{0,192},{16,208},{32,224},{48,240},{64,0},{80,16},{96,32},{112,48}... | collective-permute-start | bytes 960008 | tf_op jit(solution)/shard_map/ppermute | solution.py:31
  54.5 13.9 %collective-permute-start.20 = (bf16[100,200]{1,0:T(8,128)(2,1)S(1)}, bf16[100,200]{1,0:T(8,128)(2,1)S(1)}, u32[]{:S(2)}, u32[]{:S(2)}) collective-permute-start(bf16[100,200]{1,0:T(8,128)(2,1)S(1)} %get-tuple-element.55.walkers), channel_id=1, source_target_pairs={{0,32},{16,48},{32,0},{48,16},{64,96},{80,112},{96,64},{112,80},{1... | collective-permute-start | bytes 120008 | tf_op jit(solution)/shard_map/ppermute | solution.py:35
  57.4 11.0 %collective-permute-start.19 = (f32[8,16]{1,0:T(8,128)S(1)}, f32[8,16]{1,0:T(8,128)S(1)}, u32[]{:S(2)}, u32[]{:S(2)}) collective-permute-start(f32[8,16]{1,0:T(8,128)S(1)} %get-tuple-element.54), channel_id=1, source_target_pairs={{0,16},{16,0},{32,48},{48,32},{64,80},{80,64},{96,112},{112,96},{1... | collective-permute-start | bytes 1544 | tf_op jit(solution)/shard_map/ppermute | solution.py:39
  67.3 8.7 %collective-permute-start.17 = (bf16[50,1600]{1,0:T(8,128)(2,1)S(1)}, bf16[50,1600]{1,0:T(8,128)(2,1)S(1)}, u32[]{:S(2)}, u32[]{:S(2)}) collective-permute-start(bf16[50,1600]{1,0:T(8,128)(2,1)S(1)} %x_sum.1), channel_id=1, source_target_pairs={{0,32},{16,48},{32,0},{48,16},{64,96},{80,112},{96,64},{112,80},{1... | collective-permute-start | bytes 480008 | tf_op jit(solution)/shard_map/ppermute | solution.py:35
  69.2 9.3 %collective-permute-start.21 = (bf16[50,1600]{1,0:T(8,128)(2,1)S(1)}, bf16[50,1600]{1,0:T(8,128)(2,1)S(1)}, u32[]{:S(2)}, u32[]{:S(2)}) collective-permute-start(bf16[50,1600]{1,0:T(8,128)(2,1)S(1)} %get-tuple-element.57), channel_id=1, source_target_pairs={{0,64},{16,80},{32,96},{48,112},{64,128},{80,144},{96,160},{112,17... | collective-permute-start | bytes 480008 | tf_op jit(solution)/shard_map/ppermute | solution.py:31
  72.3 7.7 %collective-permute-start.22 = (bf16[50,1600]{1,0:T(8,128)(2,1)S(1)}, bf16[50,1600]{1,0:T(8,128)(2,1)S(1)}, u32[]{:S(2)}, u32[]{:S(2)}) collective-permute-start(bf16[50,1600]{1,0:T(8,128)(2,1)S(1)} %get-tuple-element.58), channel_id=1, source_target_pairs={{0,128},{16,144},{32,160},{48,176},{64,192},{80,208},{96,224},{112... | collective-permute-start | bytes 480008 | tf_op jit(solution)/shard_map/ppermute | solution.py:31
  73.8 6.2 %collective-permute-start.23 = (bf16[50,1600]{1,0:T(8,128)(2,1)S(1)}, bf16[50,1600]{1,0:T(8,128)(2,1)S(1)}, u32[]{:S(2)}, u32[]{:S(2)}) collective-permute-start(bf16[50,1600]{1,0:T(8,128)(2,1)S(1)} %get-tuple-element.59), channel_id=1, source_target_pairs={{0,192},{16,208},{32,224},{48,240},{64,0},{80,16},{96,32},{112,48}... | collective-permute-start | bytes 480008 | tf_op jit(solution)/shard_map/ppermute | solution.py:31
  74.7 3.8 %collective-permute-start.24 = (bf16[200,200]{1,0:T(8,128)(2,1)S(1)}, bf16[200,200]{1,0:T(8,128)(2,1)S(1)}, u32[]{:S(2)}, u32[]{:S(2)}) collective-permute-start(bf16[200,200]{1,0:T(8,128)(2,1)S(1)} %get-tuple-element.60.walkers), channel_id=1, source_target_pairs={{0,1},{1,0},{2,3},{3,2},{4,5},{5,4},{6,7},{7,6},{8,9},{9,8},{10,11... | collective-permute-start | bytes 240008 | tf_op jit(solution)/shard_map/ppermute | solution.py:47
  80.3 10.4 %collective-permute-start.25 = (bf16[50,1600]{1,0:T(8,128)(2,1)S(1)}, bf16[50,1600]{1,0:T(8,128)(2,1)S(1)}, u32[]{:S(2)}, u32[]{:S(2)}) collective-permute-start(bf16[50,1600]{1,0:T(8,128)(2,1)S(1)} %get-tuple-element.62), channel_id=1, source_target_pairs={{0,8},{1,9},{2,10},{3,11},{4,16},{5,17},{6,18},{7,19},{8,0},{9,1},... | collective-permute-start | bytes 480008 | tf_op jit(solution)/shard_map/ppermute | solution.py:64
  84.4 11.6 %collective-permute-start.26 = (bf16[50,1600]{1,0:T(8,128)(2,1)S(1)}, bf16[50,1600]{1,0:T(8,128)(2,1)S(1)}, u32[]{:S(2)}, u32[]{:S(2)}) collective-permute-start(bf16[50,1600]{1,0:T(8,128)(2,1)S(1)} %get-tuple-element.61.second), channel_id=1, source_target_pairs={{4,24},{5,25},{6,26},{7,27},{12,16},{13,17},{14,18},{15,19},{16,4}... | collective-permute-start | bytes 480008 | tf_op jit(solution)/shard_map/ppermute | solution.py:64
  86.3 9.6 %collective-permute-start.27 = (bf16[400,200]{1,0:T(8,128)(2,1)S(1)}, bf16[400,200]{1,0:T(8,128)(2,1)S(1)}, u32[]{:S(2)}, u32[]{:S(2)}) collective-permute-start(bf16[400,200]{1,0:T(8,128)(2,1)S(1)} %get-tuple-element.63.near), channel_id=1, source_target_pairs={{0,2},{1,3},{2,0},{3,1},{4,6},{5,7},{6,4},{7,5},{8,10},{9,11},{10,... | collective-permute-start | bytes 480008 | tf_op jit(solution)/shard_map/ppermute | solution.py:47
  96.0 10.1 %collective-permute-start.28 = (bf16[100,1600]{1,0:T(8,128)(2,1)S(1)}, bf16[100,1600]{1,0:T(8,128)(2,1)S(1)}, u32[]{:S(2)}, u32[]{:S(2)}) collective-permute-start(bf16[100,1600]{1,0:T(8,128)(2,1)S(1)} %get-tuple-element.65), channel_id=1, source_target_pairs={{0,32},{16,48},{32,0},{48,16},{64,96},{80,112},{96,64},{112,80},{1... | collective-permute-start | bytes 960008 | tf_op jit(solution)/shard_map/ppermute | solution.py:35
  98.5 9.4 %collective-permute-start.34 = (bf16[50,1600]{1,0:T(8,128)(2,1)S(1)}, bf16[50,1600]{1,0:T(8,128)(2,1)S(1)}, u32[]{:S(2)}, u32[]{:S(2)}) collective-permute-start(bf16[50,1600]{1,0:T(8,128)(2,1)S(1)} %get-tuple-element.66.block), channel_id=1, source_target_pairs={{0,3},{1,0},{2,1},{3,2},{4,7},{5,4},{6,5},{7,6},{8,11},{9,8},{10,9... | collective-permute-start | bytes 480008 | tf_op jit(solution)/shard_map/ppermute | solution.py:43
  100.1 8.5 %collective-permute-start.33 = (bf16[50,1600]{1,0:T(8,128)(2,1)S(1)}, bf16[50,1600]{1,0:T(8,128)(2,1)S(1)}, u32[]{:S(2)}, u32[]{:S(2)}) collective-permute-start(bf16[50,1600]{1,0:T(8,128)(2,1)S(1)} %get-tuple-element.66.block), channel_id=1, source_target_pairs={{0,2},{1,3},{2,0},{3,1},{4,6},{5,7},{6,4},{7,5},{8,10},{9,11},{10,... | collective-permute-start | bytes 480008 | tf_op jit(solution)/shard_map/ppermute | solution.py:43
  100.5 10.1 %collective-permute-start.32 = (bf16[50,1600]{1,0:T(8,128)(2,1)S(1)}, bf16[50,1600]{1,0:T(8,128)(2,1)S(1)}, u32[]{:S(2)}, u32[]{:S(2)}) collective-permute-start(bf16[50,1600]{1,0:T(8,128)(2,1)S(1)} %get-tuple-element.66.block), channel_id=1, source_target_pairs={{0,1},{1,2},{2,3},{3,0},{4,5},{5,6},{6,7},{7,4},{8,9},{9,10},{10,1... | collective-permute-start | bytes 480008 | tf_op jit(solution)/shard_map/ppermute | solution.py:43
  106.2 10.2 %collective-permute-start.31 = (bf16[100,1600]{1,0:T(8,128)(2,1)S(1)}, bf16[100,1600]{1,0:T(8,128)(2,1)S(1)}, u32[]{:S(2)}, u32[]{:S(2)}) collective-permute-start(bf16[100,1600]{1,0:T(8,128)(2,1)S(1)} %stack_low.1.p0), channel_id=1, source_target_pairs={{0,3},{1,0},{2,1},{3,2},{4,7},{5,4},{6,5},{7,6},{8,11},{9,8},{10,9... | collective-permute-start | bytes 960008 | tf_op jit(solution)/shard_map/ppermute | solution.py:43
  107.6 11.4 %collective-permute-start.30 = (bf16[100,1600]{1,0:T(8,128)(2,1)S(1)}, bf16[100,1600]{1,0:T(8,128)(2,1)S(1)}, u32[]{:S(2)}, u32[]{:S(2)}) collective-permute-start(bf16[100,1600]{1,0:T(8,128)(2,1)S(1)} %stack_low.1.p0), channel_id=1, source_target_pairs={{0,2},{1,3},{2,0},{3,1},{4,6},{5,7},{6,4},{7,5},{8,10},{9,11},{10,... | collective-permute-start | bytes 960008 | tf_op jit(solution)/shard_map/ppermute | solution.py:43
  107.9 18.4 %collective-permute-start.29 = (bf16[100,1600]{1,0:T(8,128)(2,1)S(1)}, bf16[100,1600]{1,0:T(8,128)(2,1)S(1)}, u32[]{:S(2)}, u32[]{:S(2)}) collective-permute-start(bf16[100,1600]{1,0:T(8,128)(2,1)S(1)} %stack_low.1.p0), channel_id=1, source_target_pairs={{0,1},{1,2},{2,3},{3,0},{4,5},{5,6},{6,7},{7,4},{8,9},{9,10},{10,1... | collective-permute-start | bytes 960008 | tf_op jit(solution)/shard_map/ppermute | solution.py:43
  110.7 16.6 %collective-permute-start.35 = (bf16[150,1600]{1,0:T(8,128)(2,1)S(1)}, bf16[150,1600]{1,0:T(8,128)(2,1)S(1)}, u32[]{:S(2)}, u32[]{:S(2)}) collective-permute-start(bf16[150,1600]{1,0:T(8,128)(2,1)S(1)} %get-tuple-element.69.three), channel_id=1, source_target_pairs={{0,32},{16,48},{32,0},{48,16},{64,96},{80,112},{96,64},{112,80},{1... | collective-permute-start | bytes 1440008 | tf_op jit(solution)/shard_map/ppermute | solution.py:35
  126.7 1.9 %collective-permute-start.36 = (bf16[800,200]{1,0:T(8,128)(2,1)S(1)}, bf16[800,200]{1,0:T(8,128)(2,1)S(1)}, u32[]{:S(2)}, u32[]{:S(2)}) collective-permute-start(bf16[800,200]{1,0:T(8,128)(2,1)S(1)} %get-tuple-element.70.walkers), channel_id=1, source_target_pairs={{0,16},{16,0},{32,48},{48,32},{64,80},{80,64},{96,112},{112,96},{1... | collective-permute-start | bytes 960008 | tf_op jit(solution)/shard_map/ppermute | solution.py:39
  127.2 3.3 %collective-permute-start.37 = (bf16[400,1600]{1,0:T(8,128)(2,1)S(1)}, bf16[400,1600]{1,0:T(8,128)(2,1)S(1)}, u32[]{:S(2)}, u32[]{:S(2)}) collective-permute-start(bf16[400,1600]{1,0:T(8,128)(2,1)S(1)} %get-tuple-element.68.rows0), channel_id=1, source_target_pairs={{0,16},{16,0},{32,48},{48,32},{64,80},{80,64},{96,112},{112,96},{1... | collective-permute-start | bytes 3840008 | tf_op jit(solution)/shard_map/ppermute | solution.py:39
  129.1 3.3 %collective-permute-start.38 = (bf16[400,1600]{1,0:T(8,128)(2,1)S(1)}, bf16[400,1600]{1,0:T(8,128)(2,1)S(1)}, u32[]{:S(2)}, u32[]{:S(2)}) collective-permute-start(bf16[400,1600]{1,0:T(8,128)(2,1)S(1)} %get-tuple-element.71.rows1), channel_id=1, source_target_pairs={{0,16},{16,0},{32,48},{48,32},{64,80},{80,64},{96,112},{112,96},{1... | collective-permute-start | bytes 3840008 | tf_op jit(solution)/shard_map/ppermute | solution.py:39
  141.9 8.7 %collective-permute-start.39 = (bf16[200,100]{1,0:T(8,128)(2,1)S(1)}, bf16[200,100]{1,0:T(8,128)(2,1)S(1)}, u32[]{:S(2)}, u32[]{:S(2)}) collective-permute-start(bf16[200,100]{1,0:T(8,128)(2,1)S(1)} %taylor.1), channel_id=1, source_target_pairs={{0,0},{1,1},{2,2},{3,3},{4,16},{5,17},{6,18},{7,19},{8,32},{9,33},... | collective-permute-start | bytes 120008 | tf_op jit(solution)/shard_map/ppermute | solution.py:64
